TPU v7x, 32 devices: a whole 2x2x4 slice. The times are simulated.
32 devices in a mesh: ctx: 16 (over z, x, core), fsdp: 2 (over y).
Axes of the slice: x: 2, y: 2, z: 4, core: 2. Of those that a mesh axis runs over, the one named last changes fastest.
Arguments:
- inputs: bfloat16 [4, 1024, 1024], P('fsdp', 'ctx'), may hold values from -6 to 6
- gain_attn: bfloat16 [1024], P(('ctx', 'fsdp')), may hold values from 0.25 to 1.75
- gain_mlp: bfloat16 [1024], P(('ctx', 'fsdp')), may hold values from 0.25 to 1.75
- w_qkv: bfloat16 [1024, 3072], P(('ctx', 'fsdp')), may hold values from -0.1875 to 0.1875
- w_attn_out: bfloat16 [1024, 1024], P(('ctx', 'fsdp')), may hold values from -3.5 to 3.5
- w_in: bfloat16 [1024, 5248], P(('ctx', 'fsdp')), may hold values from -0.1875 to 0.1875
- w_out: bfloat16 [2624, 1024], P(None, ('ctx', 'fsdp')), may hold values from -0.125 to 0.125
- cotangent: bfloat16 [4, 1024, 1024], P('fsdp', 'ctx'), may hold values from -6 to 6
Outputs:
- output: bfloat16 [4, 1024, 1024], P('fsdp', 'ctx')
- input_grad: float32 [4, 1024, 1024], P('fsdp', 'ctx')
- grad_gain_attn: float32 [1024], P(('ctx', 'fsdp'))
- grad_gain_mlp: float32 [1024], P(('ctx', 'fsdp'))
- grad_qkv: float32 [1024, 3072], P(('ctx', 'fsdp'))
- grad_attn_out: float32 [1024, 1024], P(('ctx', 'fsdp'))
- grad_in: float32 [1024, 5248], P(('ctx', 'fsdp'))
- grad_out: float32 [2624, 1024], P(None, ('ctx', 'fsdp'))
All inputs are finite; a program needn't handle non-finite values.
Results may differ from a plain program's by a relative error of at most 0.035.
Values may be sent and summed in bfloat16 or wider, within the bound.
No kernel may reach another device: no remote copies, remote signals or barrier semaphores. Data moves between devices by JAX's collectives and lax.ppermute only.
A program may use at most 320 MiB of HBM per device.

v0:
```python
import math

import jax
import jax.numpy as jnp
from jax import lax
from jax.sharding import PartitionSpec as P

HEADS = 16


norm_eps = 1e-05
rope_base = 160000.0
key_block = 512
far_below = -1e30


def norm_forward(values, gain):
    centre = values - jnp.mean(values, axis=-1, keepdims=True)
    inverse = lax.rsqrt(jnp.mean(centre * centre, axis=-1, keepdims=True) + norm_eps)
    normed = centre * inverse
    return (normed, inverse, (normed * gain).astype(jnp.bfloat16))


def norm_backward(upstream, normed, inverse, gain):
    gain_grad = jnp.sum(upstream * normed, axis=(0, 1))
    scaled = upstream * gain
    inner_mean = jnp.mean(scaled * normed, axis=-1, keepdims=True)
    result = inverse * (scaled - jnp.mean(scaled, axis=-1, keepdims=True) - normed * inner_mean)
    return (result, gain_grad)


def rotate(heads_in, cosine, sine_table, direction):
    halfway = heads_in.shape[-1] // 2
    first_half = heads_in[..., :halfway]
    second_half = heads_in[..., halfway:]
    return jnp.concatenate(
        [
            first_half * cosine - direction * second_half * sine_table,
            second_half * cosine + direction * first_half * sine_table,
        ],
        axis=-1,
    )


def blocked(array_in, stride):
    seq_count, rows = (array_in.shape[0], array_in.shape[1])
    shaped = array_in.reshape((seq_count, rows // stride, stride) + array_in.shape[2:])
    return jnp.moveaxis(shaped, 1, 0)


def body(inputs, gain_attn, gain_mlp, w_qkv, w_attn_out, w_in, w_out, cotangent):
    gathered = (
        lax.all_gather(gain_attn, ("ctx", "fsdp"), axis=0, tiled=True),
        lax.all_gather(gain_mlp, ("ctx", "fsdp"), axis=0, tiled=True),
        lax.all_gather(w_qkv, ("ctx", "fsdp"), axis=0, tiled=True),
        lax.all_gather(w_attn_out, ("ctx", "fsdp"), axis=0, tiled=True),
        lax.all_gather(w_in, ("ctx", "fsdp"), axis=0, tiled=True),
        lax.all_gather(w_out, ("ctx", "fsdp"), axis=1, tiled=True),
    )
    gain_one, gain_two, full_qkv, full_attn, full_in, full_out = gathered
    in_shape = inputs.shape
    seq_count = in_shape[0]
    row_count = in_shape[1]
    width = in_shape[2]
    tokens_in = inputs.astype(jnp.float32)
    head_count = HEADS
    head_size = width // head_count
    halfway = head_size // 2
    score_scale = head_size ** (-0.5)
    head_shape = (seq_count, row_count, head_count, head_size)
    gain_first = gain_one.astype(jnp.float32)
    gain_second = gain_two.astype(jnp.float32)
    places = (lax.axis_index("ctx") * row_count + jnp.arange(row_count, dtype=jnp.int32)).astype(
        jnp.float32
    )
    inverse_freq = rope_base ** (
        -2.0 * jnp.arange(halfway, dtype=jnp.int32).astype(jnp.float32) / head_size
    )
    angles = places[:, None] * inverse_freq[None, :]
    cosine = jnp.cos(angles)[:, None, :]
    sine_table = jnp.sin(angles)[:, None, :]
    normed_one, inverse_one, lowered_one = norm_forward(tokens_in, gain_first)
    projected = jnp.einsum("srd,de->sre", lowered_one, full_qkv, preferred_element_type=jnp.float32)
    query_heads = rotate(
        projected[..., :width].reshape(head_shape), cosine, sine_table, 1.0
    ).astype(jnp.bfloat16)
    key_heads = rotate(
        projected[..., width : 2 * width].reshape(head_shape), cosine, sine_table, 1.0
    ).astype(jnp.bfloat16)
    value_heads = projected[..., 2 * width :].reshape(head_shape).astype(jnp.bfloat16)
    key_flat = key_heads.reshape(seq_count, row_count, width)
    value_flat = value_heads.reshape(seq_count, row_count, width)

    def forward_fold(carried, arriving):
        piece_keys, piece_values = arriving
        piece_rows = piece_keys.shape[1]
        stride = math.gcd(piece_rows, key_block)
        grouped_keys = blocked(
            piece_keys.reshape(seq_count, piece_rows, head_count, head_size), stride
        )
        grouped_values = blocked(
            piece_values.reshape(seq_count, piece_rows, head_count, head_size), stride
        )

        def forward_visit(running, member):
            running_top, running_sum, running_acc = running
            group_keys, group_values = member
            scores = (
                jnp.einsum(
                    "sqhd,skhd->sqhk", query_heads, group_keys, preferred_element_type=jnp.float32
                )
                * score_scale
            )
            new_top = jnp.maximum(running_top, jnp.max(scores, axis=-1))
            fading = jnp.exp(running_top - new_top)
            weights = jnp.exp(scores - new_top[..., None])
            new_sum = running_sum * fading + jnp.sum(weights, axis=-1)
            weighted = jnp.einsum(
                "sqhk,skhd->sqhd",
                weights.astype(jnp.bfloat16),
                group_values,
                preferred_element_type=jnp.float32,
            )
            return ((new_top, new_sum, running_acc * fading[..., None] + weighted), None)

        carried, unused = lax.scan(forward_visit, carried, (grouped_keys, grouped_values))
        return carried

    stat_shape = (seq_count, row_count, head_count)
    fold_begin = (
        jnp.full(stat_shape, far_below, jnp.float32),
        jnp.zeros(stat_shape, jnp.float32),
        jnp.zeros(head_shape, jnp.float32),
    )
    top_one, sum_one, acc_one = forward_fold(
        fold_begin,
        (
            lax.all_gather(key_flat, "ctx", axis=1, tiled=True),
            lax.all_gather(value_flat, "ctx", axis=1, tiled=True),
        ),
    )
    attended_low = (
        (acc_one / sum_one[..., None]).reshape(seq_count, row_count, width).astype(jnp.bfloat16)
    )
    middle = tokens_in + jnp.einsum(
        "srd,de->sre", attended_low, full_attn, preferred_element_type=jnp.float32
    )
    normed_two, inverse_two, lowered_two = norm_forward(middle, gain_second)
    gate_up = jnp.einsum("srd,df->srf", lowered_two, full_in, preferred_element_type=jnp.float32)
    ff_width = full_in.shape[1] // 2
    gate_part = gate_up[..., :ff_width]
    lift_part = gate_up[..., ff_width:]
    activated, gelu_pullback = jax.vjp(
        lambda values: jax.nn.gelu(values, approximate=False), gate_part
    )
    hidden = (activated * lift_part).astype(jnp.bfloat16)
    result = middle + jnp.einsum(
        "srf,fd->srd", hidden, full_out, preferred_element_type=jnp.float32
    )
    output = result.astype(jnp.bfloat16)
    grad_out_turned = jnp.einsum(
        "srd,srf->df", cotangent, hidden, preferred_element_type=jnp.float32
    )
    grad_hidden = jnp.einsum("srd,fd->srf", cotangent, full_out, preferred_element_type=jnp.float32)
    grad_gate = gelu_pullback(grad_hidden * lift_part)[0]
    grad_gate_up = jnp.concatenate([grad_gate, grad_hidden * activated], axis=-1).astype(
        jnp.bfloat16
    )
    grad_in = jnp.einsum(
        "srd,srf->df", lowered_two, grad_gate_up, preferred_element_type=jnp.float32
    )
    grad_normed_two = jnp.einsum(
        "srf,df->srd", grad_gate_up, full_in, preferred_element_type=jnp.float32
    )
    grad_middle_norm, gain_grad_two = norm_backward(
        grad_normed_two, normed_two, inverse_two, gain_second
    )
    grad_middle = cotangent.astype(jnp.float32) + grad_middle_norm
    grad_branch = grad_middle.astype(jnp.bfloat16)
    grad_attn = jnp.einsum(
        "srd,sre->de", attended_low, grad_branch, preferred_element_type=jnp.float32
    )
    grad_attended = jnp.einsum(
        "sre,de->srd", grad_branch, full_attn, preferred_element_type=jnp.float32
    ).astype(jnp.bfloat16)
    grad_att_heads = grad_attended.reshape(head_shape)
    top_two, sum_two, acc_two = forward_fold(
        fold_begin,
        (
            lax.all_gather(key_flat, "ctx", axis=1, tiled=True),
            lax.all_gather(value_flat, "ctx", axis=1, tiled=True),
        ),
    )
    attention_rows = acc_two / sum_two[..., None]
    log_total = top_two + jnp.log(sum_two)
    delta_rows = jnp.sum(grad_att_heads.astype(jnp.float32) * attention_rows, axis=-1)
    carried = jnp.zeros(head_shape, jnp.float32)
    piece_keys = lax.all_gather(key_flat, "ctx", axis=1, tiled=True)
    piece_values = lax.all_gather(value_flat, "ctx", axis=1, tiled=True)
    piece_rows = piece_keys.shape[1]
    stride = math.gcd(piece_rows, key_block)
    grouped_keys = blocked(piece_keys.reshape(seq_count, piece_rows, head_count, head_size), stride)
    grouped_values = blocked(
        piece_values.reshape(seq_count, piece_rows, head_count, head_size), stride
    )

    def query_visit(running, member):
        group_keys, group_values = member
        scores = (
            jnp.einsum(
                "sqhd,skhd->sqhk", query_heads, group_keys, preferred_element_type=jnp.float32
            )
            * score_scale
        )
        probability = jnp.exp(scores - log_total[..., None])
        grad_prob = jnp.einsum(
            "sqhd,skhd->sqhk", grad_att_heads, group_values, preferred_element_type=jnp.float32
        )
        grad_score = (probability * (grad_prob - delta_rows[..., None])).astype(jnp.bfloat16)
        return (
            running
            + jnp.einsum(
                "sqhk,skhd->sqhd", grad_score, group_keys, preferred_element_type=jnp.float32
            ),
            None,
        )

    carried, unused = lax.scan(query_visit, carried, (grouped_keys, grouped_values))
    grad_queries = carried * score_scale
    query_flat = query_heads.reshape(seq_count, row_count, width).astype(jnp.float32)
    grad_att_flat = grad_attended.astype(jnp.float32)
    empty_heads = jnp.zeros(head_shape, jnp.float32)
    carried = (empty_heads, empty_heads)
    piece_queries = lax.all_gather(
        query_flat.astype(jnp.bfloat16), "ctx", axis=1, tiled=True
    ).astype(jnp.float32)
    piece_grads = lax.all_gather(grad_att_flat.astype(jnp.bfloat16), "ctx", axis=1, tiled=True)
    piece_logs = lax.all_gather(log_total.astype(jnp.bfloat16), "ctx", axis=1, tiled=True).astype(
        jnp.float32
    )
    piece_deltas = lax.all_gather(
        delta_rows.astype(jnp.bfloat16), "ctx", axis=1, tiled=True
    ).astype(jnp.float32)
    piece_rows = piece_queries.shape[1]
    stride = math.gcd(piece_rows, key_block)
    grouped = (
        blocked(
            piece_queries.astype(jnp.bfloat16).reshape(
                seq_count, piece_rows, head_count, head_size
            ),
            stride,
        ),
        blocked(piece_grads.reshape(seq_count, piece_rows, head_count, head_size), stride),
        blocked(piece_logs, stride),
        blocked(piece_deltas, stride),
    )

    def key_visit(running, member):
        sum_keys, sum_values = running
        group_queries, group_grads, group_logs, group_deltas = member
        scores = (
            jnp.einsum(
                "sqhd,skhd->sqhk", group_queries, key_heads, preferred_element_type=jnp.float32
            )
            * score_scale
        )
        probability = jnp.exp(scores - group_logs[..., None])
        new_values = sum_values + jnp.einsum(
            "sqhk,sqhd->skhd",
            probability.astype(jnp.bfloat16),
            group_grads,
            preferred_element_type=jnp.float32,
        )
        grad_prob = jnp.einsum(
            "sqhd,skhd->sqhk", group_grads, value_heads, preferred_element_type=jnp.float32
        )
        grad_score = (probability * (grad_prob - group_deltas[..., None])).astype(jnp.bfloat16)
        new_keys = sum_keys + jnp.einsum(
            "sqhk,sqhd->skhd", grad_score, group_queries, preferred_element_type=jnp.float32
        )
        return ((new_keys, new_values), None)

    carried, unused = lax.scan(key_visit, carried, grouped)
    grad_keys, grad_values = carried
    grad_keys = grad_keys * score_scale
    flat_shape = (seq_count, row_count, width)
    grad_projected = jnp.concatenate(
        [
            rotate(grad_queries, cosine, sine_table, -1.0).reshape(flat_shape),
            rotate(grad_keys, cosine, sine_table, -1.0).reshape(flat_shape),
            grad_values.reshape(flat_shape),
        ],
        axis=-1,
    ).astype(jnp.bfloat16)
    grad_qkv = jnp.einsum(
        "srd,sre->de", lowered_one, grad_projected, preferred_element_type=jnp.float32
    )
    grad_normed_one = jnp.einsum(
        "sre,de->srd", grad_projected, full_qkv, preferred_element_type=jnp.float32
    )
    grad_tokens_norm, gain_grad_one = norm_backward(
        grad_normed_one, normed_one, inverse_one, gain_first
    )
    input_grad = grad_middle + grad_tokens_norm
    summed = (
        lax.psum_scatter(gain_grad_one, ("ctx", "fsdp"), scatter_dimension=0, tiled=True),
        lax.psum_scatter(gain_grad_two, ("ctx", "fsdp"), scatter_dimension=0, tiled=True),
        lax.psum_scatter(grad_qkv, ("ctx", "fsdp"), scatter_dimension=0, tiled=True),
        lax.psum_scatter(grad_attn, ("ctx", "fsdp"), scatter_dimension=0, tiled=True),
        lax.psum_scatter(grad_in, ("ctx", "fsdp"), scatter_dimension=0, tiled=True),
        lax.psum_scatter(grad_out_turned, ("ctx", "fsdp"), scatter_dimension=0, tiled=True),
    )
    return (
        output,
        input_grad,
        summed[0],
        summed[1],
        summed[2],
        summed[3],
        summed[4],
        jnp.transpose(summed[5]),
    )


def solution(mesh):
    placed = (
        P("fsdp", "ctx", None),
        P(("ctx", "fsdp")),
        P(("ctx", "fsdp")),
        P(("ctx", "fsdp"), None),
        P(("ctx", "fsdp"), None),
        P(("ctx", "fsdp"), None),
        P(None, ("ctx", "fsdp")),
        P("fsdp", "ctx", None),
    )
    return jax.shard_map(
        body,
        mesh=mesh,
        in_specs=placed,
        out_specs=(
            P("fsdp", "ctx", None),
            P("fsdp", "ctx", None),
            P(("ctx", "fsdp")),
            P(("ctx", "fsdp")),
            P(("ctx", "fsdp"), None),
            P(("ctx", "fsdp"), None),
            P(("ctx", "fsdp"), None),
            P(None, ("ctx", "fsdp")),
        ),
        check_vma=False,
    )
```

profile of v0, /device:TPU:0, one launch (start us, length us, event | category | flops | bytes accessed | tf_op | source)
XLA Modules:
  0.0 1434.0 jit_solution(8710287839346166591)
XLA Ops:
  9.6 43.0 %all-reduce.5 = (bf16[1024]{0:T(1024)(128)(2,1)S(1)}, bf16[1024]{0:T(1024)(128)(2,1)S(1)}) all-reduce(bf16[1024]{0:T(1024)(128)(2,1)S(1)} %dynamic-update-slice, bf16[1024]{0:T(1024)(128)(2,1)S(1)} %dynamic-update-slice.1), channel_id=1, replica_groups=mesh['ctx'=16,'fsdp'=2] {'ctx','fsdp'}, use_global_device_ids=true, to_apply=%add | all-reduce | flops 2048 | bytes 8192
  55.7 27.7 %all-gather.9.cloned.1.call-done = bf16[1024,3072]{1,0:T(8,128)(2,1)} async-done(((bf16[32,3072]{1,0:T(8,128)(2,1)}), bf16[1024,3072]{1,0:T(8,128)(2,1)}) %all-gather.9.cloned.1.call-update) | async-done | bytes 6291472 | tf_op jit(solution)/shard_map/all_gather | solution.py:55
  97.7 45.1 %all-gather.11.cloned.1.call-done = bf16[2,1024,1024]{2,0,1:T(2,128)(2,1)} async-done(((bf16[2,64,1024]{2,0,1:T(2,128)(2,1)}), bf16[2,1024,1024]{2,0,1:T(2,128)(2,1)}) %all-gather.11.cloned.1.call-update) | async-done | bytes 4194320 | tf_op jit(solution)/shard_map/all_gather | solution.py:138
  142.8 11.3 copy.96
  154.1 7.8 reshape_reshape.16
  161.9 5.2 copy.100
  167.1 27.6 %all-gather.13.cloned.1.call-done = bf16[2,1024,1024]{2,1,0:T(8,128)(2,1)} async-done(((bf16[2,64,1024]{2,1,0:T(8,128)(2,1)}), bf16[2,1024,1024]{2,1,0:T(8,128)(2,1)}) %all-gather.13.cloned.1.call-update) | async-done | bytes 4194320 | tf_op jit(solution)/shard_map/all_gather | solution.py:139
  194.7 6.2 copy.99
  200.9 7.8 reshape_reshape.17
  208.7 5.1 copy.102
  213.9 21.6 %while.45 = (s32[]{:T(128)}, f32[2,64,16]{1,2,0:T(8,128)S(1)}, f32[2,64,16]{1,2,0:T(8,128)S(1)}, f32[2,64,16,64]{1,3,2,0:T(8,128)S(1)}, bf16[2,2,512,16,64]{2,4,...) while((s32[]{:T(128)}, f32[2,64,16]{1,2,0:T(8,128)S(1)}, ...), condition=%wide.region_5.6_spmd.clone, body=%wide.region_2.5_spmd.clone.sunk | while | flops 277227520 | bytes 34996372 | solution.py:126
  213.9 4.4 bitcast_reduce_fusion.2
  224.6 4.3 bitcast_reduce_fusion.2
  235.7 17.0 %all-gather.15.cloned.1.call-done = bf16[1024,1024]{1,0:T(8,128)(2,1)} async-done(((bf16[32,1024]{1,0:T(8,128)(2,1)}), bf16[1024,1024]{1,0:T(8,128)(2,1)}) %all-gather.15.cloned.1.call-update) | async-done | bytes 2097168 | tf_op jit(solution)/shard_map/all_gather | solution.py:56
  255.1 87.2 %all-gather.17.cloned.1.call-done = bf16[1024,5248]{1,0:T(8,128)(2,1)} async-done(((bf16[32,5248]{1,0:T(8,128)(2,1)}), bf16[1024,5248]{1,0:T(8,128)(2,1)}) %all-gather.17.cloned.1.call-update) | async-done | bytes 10747920 | tf_op jit(solution)/shard_map/all_gather | solution.py:57
  342.2 7.3 fusion.93
  349.5 60.2 %all-gather.19.cloned.1.call-done = bf16[2624,1024]{0,1:T(8,128)(2,1)} async-done(((bf16[2624,32]{0,1:T(8,128)(2,1)}), bf16[2624,1024]{0,1:T(8,128)(2,1)}) %all-gather.19.cloned.1.call-update) | async-done | bytes 5373968 | tf_op jit(solution)/shard_map/all_gather | solution.py:58
  409.7 7.3 add_convert_fusion
  424.3 4.0 convolution_bitcast_fusion.3
  428.4 5.7 convolution_bitcast_fusion.1
  434.1 12.1 copy.139
  446.2 10.7 reduce-scatter.7.cloned.1.call-start
  463.1 11.2 copy.116
  474.3 7.8 reshape_reshape.18
  482.1 5.1 copy.122
  489.5 24.9 %all_gather.49 = bf16[2,1024,16]{2,0,1:T(2,128)(2,1)} all-gather(bf16[2,64,16]{2,0,1:T(2,128)(2,1)S(1)} %get-tuple-element.426), channel_id=1, replica_groups=mesh['ctx'=16,'fsdp'=2] {'ctx'}, dimensions={1}, use_global_device_ids=true | all-gather | bytes 69632 | tf_op jit(solution)/shard_map/all_gather | solution.py:238
  525.1 19.0 %all_gather.51 = bf16[2,1024,16]{2,0,1:T(2,128)(2,1)S(1)} all-gather(bf16[2,64,16]{2,0,1:T(2,128)(2,1)S(1)} %copy.120), channel_id=1, replica_groups=mesh['ctx'=16,'fsdp'=2] {'ctx'}, dimensions={1}, use_global_device_ids=true | all-gather | bytes 69632 | tf_op jit(solution)/shard_map/all_gather | solution.py:241
  545.2 22.2 %while.46 = (s32[]{:T(128)}, f32[2,64,16,64]{1,3,2,0:T(8,128)}, bf16[2,2,512,16,64]{2,4,3,1,0:T(8,128)(2,1)}, bf16[2,64,16,64]{3,1,2,0:T(8,128)(2,1)S(1)}, f32[2...) while((s32[]{:T(128)}, f32[2,64,16,64]{1,3,2,0:T(8,128)}, ...), condition=%wide.region_12.0_spmd.clone, body=%wide.region_11.12_spmd.clone.sunk | while | flops 408158208 | bytes 20727472 | solution.py:228
  545.2 4.4 fusion.197
  549.6 5.7 fusion.198
  556.3 4.4 fusion.197
  560.7 5.7 fusion.198
  569.7 6.2 copy.118
  575.9 7.8 reshape_reshape.19
  583.8 5.3 copy.125
  589.1 28.2 %while.47 = (s32[]{:T(128)}, f32[2,64,16,64]{1,3,2,0:T(8,128)S(1)}, f32[2,64,16,64]{1,3,2,0:T(8,128)S(1)}, bf16[2,2,512,16,64]{2,4,3,1,0:T(8,128)(2,1)}, bf16[2,...) while((s32[]{:T(128)}, f32[2,64,16,64]{1,3,2,0:T(8,128)S(1)}, ...), condition=%wide.region_14.15_spmd.clone, body=%wide.region_13.0_spmd.clone.sunk | while | flops 545783808 | bytes 25626304 | solution.py:283
  589.1 4.5 fusion.206
  593.7 5.5 fusion.207
  603.2 4.5 fusion.206
  607.9 5.5 fusion.207
  620.0 6.4 convolution_bitcast_fusion.2
  627.8 8.9 convolution_bitcast_fusion
  637.8 5.2 fusion.120
  643.0 5.2 fusion.137
  648.2 37.9 %all-reduce.4 = (f32[1024]{0:T(1024)S(1)}, f32[1024]{0:T(1024)S(1)}) all-reduce(f32[1024]{0:T(1024)S(1)} %get-tuple-element.368, f32[1024]{0:T(1024)S(1)} %get-tuple-element.366), channel_id=2, replica_groups=mesh['ctx'=16,'fsdp'=2] {'ctx','fsdp'}, use_global_device_ids=true, to_apply=%region_18.19.clone | all-reduce | flops 2048 | bytes 16384
  688.4 120.3 %reduce-scatter.13.cloned.1.call-done = f32[32,2624]{1,0:T(8,128)} async-done(((f32[1024,2624]{1,0:T(8,128)}), f32[32,2624]{1,0:T(8,128)}) %reduce-scatter.13.cloned.1.call-update) | async-done | bytes 335888
  808.7 160.9 %reduce-scatter.7.cloned.1.call-done = f32[32,3072]{1,0:T(8,128)} async-done(((f32[1024,3072]{1,0:T(8,128)}), f32[32,3072]{1,0:T(8,128)}) %reduce-scatter.7.cloned.1.call-update) | async-done | bytes 393232 | tf_op jit(solution)/shard_map/reduce_scatter | solution.py:308
  969.6 457.4 %reduce-scatter.11.cloned.1.call-done = f32[32,5248]{1,0:T(8,128)} async-done(((f32[1024,5248]{1,0:T(8,128)}), f32[32,5248]{1,0:T(8,128)}) %reduce-scatter.11.cloned.1.call-update) | async-done | bytes 671760 | tf_op jit(solution)/shard_map/reduce_scatter | solution.py:310
  (192 shorter events, 81.9 us)
Async XLA Ops:
  7.2 76.2 %all-gather.9.cloned.1.call-start = ((), (), s32[]{:S(2)}) async-start(), calls=%async_computation.4 | async-start | bytes 6488064 | tf_op jit(solution)/shard_map/all_gather | solution.py:55
  7.9 134.9 %all-gather.11.cloned.1.call-start = ((), (), s32[]{:S(2)}) async-start(), calls=%async_computation.5 | async-start | bytes 4456448 | tf_op jit(solution)/shard_map/all_gather | solution.py:138
  52.7 34.7 %copy-start.24 = (f32[1024]{0:T(1024)}, f32[1024]{0:T(1024)S(1)}, u32[]{:S(2)}) copy-start(f32[1024]{0:T(1024)S(1)} %convert_element_type.104) | copy-start | bytes 12292
  53.8 33.6 %copy-start.28 = (f32[2,64]{1,0:T(2,128)}, f32[2,64]{1,0:T(2,128)S(1)}, u32[]{:S(2)}) copy-start(f32[2,64]{1,0:T(2,128)S(1)} %broadcast_multiply_fusion.8) | copy-start | bytes 1540
  55.0 32.4 %copy-start.31 = (f32[2,64]{1,0:T(2,128)}, f32[2,64]{1,0:T(2,128)S(1)}, u32[]{:S(2)}) copy-start(f32[2,64]{1,0:T(2,128)S(1)} %add_rsqrt_fusion.1) | copy-start | bytes 1540
  55.7 35.3 %copy-start.26 = (f32[64,32]{0,1:T(8,128)}, f32[64,32]{0,1:T(8,128)S(1)}, u32[]{:S(2)}) copy-start(f32[64,32]{0,1:T(8,128)S(1)} %get-tuple-element.452) | copy-start | bytes 24580
  92.6 4.1 copy-start.14
  93.6 101.1 %all-gather.13.cloned.1.call-start = ((), (), s32[]{:S(2)}) async-start(), calls=%async_computation.6 | async-start | bytes 4456448 | tf_op jit(solution)/shard_map/all_gather | solution.py:139
  94.4 158.3 %all-gather.15.cloned.1.call-start = ((), (), s32[]{:S(2)}) async-start(), calls=%async_computation.7 | async-start | bytes 2162688 | tf_op jit(solution)/shard_map/all_gather | solution.py:56
  95.0 247.2 %all-gather.17.cloned.1.call-start = ((), (), s32[]{:S(2)}) async-start(), calls=%async_computation.8 | async-start | bytes 11083776 | tf_op jit(solution)/shard_map/all_gather | solution.py:57
  95.6 314.1 %all-gather.19.cloned.1.call-start = ((), (), s32[]{:S(2)}) async-start(), calls=%async_computation.9 | async-start | bytes 5677056 | tf_op jit(solution)/shard_map/all_gather | solution.py:58
  96.2 366.9 %all-gather.21.cloned.1.call-start = ((), (), s32[]{:S(2)}) async-start(), calls=%async_computation.10 | async-start | bytes 4456448 | tf_op jit(solution)/shard_map/all_gather | solution.py:234
  97.7 472.1 %all-gather.23.cloned.1.call-start = ((), (), s32[]{:S(2)}) async-start(), calls=%async_computation.11 | async-start | bytes 4456448 | tf_op jit(solution)/shard_map/all_gather | solution.py:237
  213.9 38.8 %copy-start.9 = (bf16[2,64,1024]{2,1,0:T(8,128)(2,1)S(1)}, bf16[2,64,1024]{2,1,0:T(8,128)(2,1)}, u32[]{:S(2)}) copy-start(bf16[2,64,1024]{2,1,0:T(8,128)(2,1)} %param.14) | copy-start | bytes 786436
  218.2 3.5 copy-start
  228.9 3.5 copy-start
  235.6 113.8 %copy-start.13 = (bf16[2,64,16,64]{1,3,2,0:T(8,128)(2,1)}, bf16[2,64,16,64]{1,3,2,0:T(8,128)(2,1)S(1)}, u32[]{:S(2)}) copy-start(bf16[2,64,16,64]{1,3,2,0:T(8,128)(2,1)S(1)} %fusion.139) | copy-start | bytes 786436
  255.1 154.6 %copy-start.20 = (bf16[2,64,1024]{2,1,0:T(8,128)(2,1)S(1)}, bf16[2,64,1024]{2,1,0:T(8,128)(2,1)}, u32[]{:S(2)}) copy-start(bf16[2,64,1024]{2,1,0:T(8,128)(2,1)} %param.21) | copy-start | bytes 786436
  409.7 7.4 copy-start.5
  409.7 8.2 copy-start.6
  417.6 4.0 copy-start.16
  417.7 10.7 copy-start.7
  417.9 4.8 copy-start.12
  424.3 264.1 %reduce-scatter.9.cloned.1.call-start = ((), (), s32[]{:S(2)}) async-start(), calls=%async_computation.13 | async-start | bytes 4325376 | tf_op jit(solution)/shard_map/reduce_scatter | solution.py:309
  428.3 380.3 %reduce-scatter.13.cloned.1.call-start = ((), (), s32[]{:S(2)}) async-start(), calls=%async_computation.15 | async-start | bytes 11354112
  446.2 523.4 %reduce-scatter.7.cloned.1.call-start = ((), (), s32[]{:S(2)}) async-start(), calls=%async_computation.12 | async-start | bytes 12976128 | tf_op jit(solution)/shard_map/reduce_scatter | solution.py:308
  545.2 4.4 copy-start.2
  555.3 1.0 copy-start.3
  556.3 4.4 copy-start.2
  566.4 1.0 copy-start.3
  583.8 5.3 copy-start.1
  583.8 5.3 copy-start.4
  589.1 4.5 copy-start.18
  589.1 4.5 copy-start.19
  603.2 4.5 copy-start.18
  603.2 4.5 copy-start.19
  617.3 1.1 copy-start.27
  617.3 1.1 copy-start.30
  617.4 1.3 copy-start.15
  619.0 1.0 copy-start.21
  619.1 0.9 copy-start.25
  619.1 0.9 copy-start.29
  619.1 0.9 copy-start.32
  626.4 1.1 copy-start.17
  626.4 1.3 copy-start.23
  626.5 800.5 %reduce-scatter.11.cloned.1.call-start = ((), (), s32[]{:S(2)}) async-start(), calls=%async_computation.14 | async-start | bytes 22167552 | tf_op jit(solution)/shard_map/reduce_scatter | solution.py:310
  636.7 1.1 copy-start.8
  643.0 44.3 %copy-start.11 = (f32[2,64,1024]{2,1,0:T(8,128)S(1)}, f32[2,64,1024]{2,1,0:T(8,128)}, u32[]{:S(2)}) copy-start(f32[2,64,1024]{2,1,0:T(8,128)} %copy-done.10) | copy-start | bytes 1572868
  (2 other events, 1.7 us)
Sparse Core Ops, SparseCore 0:
  10.9 72.4 all-gather.8
  93.7 49.0 all-gather.10
  145.6 49.0 all-gather.12
  197.7 54.9 all-gather.14
  255.4 86.7 all-gather.16
  345.0 64.6 all-gather.18
  411.9 49.5 all-gather.20
  464.2 53.6 all-gather.22
  520.7 140.7 reduce-scatter.8
  667.9 140.7 reduce-scatter.12
  815.3 154.2 reduce-scatter.6
  972.4 454.4 reduce-scatter.10
where the time goes:
time: 1440 us; the launch traced here: 1430 us
  waiting for transfers between devices  1010 us (70%)
  local copies, waits for them, and re-layouts  133 us (9%)
  blocking collectives  125 us (9%)
  matrix products  124 us (9%)
  other arithmetic  19.6 us (1%)
  between operations  14.9 us (1%)
    reduce_scatter x1, waiting for transfers between devices, body(): lax.psum_scatter(grad_in, ('ctx', 'fsdp'), scatter_dimension=0, tiled=True)  457 us
    reduce_scatter x1, waiting for transfers between devices, body(): lax.psum_scatter(grad_qkv, ('ctx', 'fsdp'), scatter_dimension=0, tiled=True)  161 us
    unnamed x13, waiting for transfers between devices  123 us
    all_gather x1, waiting for transfers between devices, body(): lax.all_gather(w_in, ('ctx', 'fsdp'), axis=0, tiled=True)  87.2 us
    unnamed x2, blocking collectives  81 us
    all_gather x1, waiting for transfers between devices, body(): lax.all_gather(w_out, ('ctx', 'fsdp'), axis=1, tiled=True)  60.2 us
    unnamed x72, local copies, waits for them, and re-layouts  46.7 us
    all_gather x1, waiting for transfers between devices, body(): lax.all_gather(key_flat, 'ctx', axis=1, tiled=True)  45.1 us
  transfers between devices with their start and end apart: 12, of which 9 were waited for; matrix products, arithmetic and copies ran while one was open for 18% of the time, Pallas kernels for 0%

commit v1 on v0

v1 whole, which is shorter than its diff:
```python
import functools
import math

import jax
import jax.numpy as jnp
from jax import lax
from jax.experimental import pallas as pl
from jax.experimental.pallas import tpu as pltpu
from jax.sharding import Mesh
from jax.sharding import PartitionSpec as P

HEADS = 16
norm_eps = 1e-05
rope_base = 160000.0
f32 = jnp.float32
bf16 = jnp.bfloat16
LANES = 128
MIB = 1024 * 1024


def partner(array, axis, step=1):
    size = lax.axis_size(axis)
    return lax.ppermute(array, axis, [(i, i ^ step) for i in range(size)])


def opposite(array):
    return lax.ppermute(array, ("x", "y"), [(i, 3 - i) for i in range(4)])


def paired(own, other, place, axis):
    first = jnp.where(place == 0, own, other)
    second = jnp.where(place == 0, other, own)
    return jnp.stack([first, second], axis=axis)


def core_swap(array):
    place = lax.axis_index("c")
    kept = lax.dynamic_index_in_dim(array, place, 0, False)
    sent = lax.dynamic_index_in_dim(array, 1 - place, 0, False)
    return paired(kept, partner(sent, "c"), place, 0)


def gather_chips(block):
    zi, xi = lax.axis_index("z"), lax.axis_index("x")
    pieces = [block] + [partner(block, "z", j) for j in range(1, 4)]
    whole = jnp.zeros((4, 2) + block.shape, block.dtype)
    rest = (0,) * block.ndim
    for j, piece in enumerate(pieces):
        across = partner(piece, "x")
        whole = lax.dynamic_update_slice(whole, piece[None, None], (zi ^ j, xi) + rest)
        whole = lax.dynamic_update_slice(whole, across[None, None], (zi ^ j, 1 - xi) + rest)
    return whole


def scatter_chips(terms):
    zi, xi = lax.axis_index("z"), lax.axis_index("x")

    def block(j, other):
        at = (zi ^ j, xi ^ other) + (0,) * (terms.ndim - 2)
        return lax.dynamic_slice(terms, at, (1, 1) + terms.shape[2:])[0, 0]

    total = None
    for j in (2, 3, 1, 0):
        part = block(j, 0).astype(f32) + partner(block(j, 1), "x").astype(f32)
        if j:
            part = partner(part.astype(terms.dtype), "z", j).astype(f32)
        total = part if total is None else total + part
    return total


def gather_plane(block):
    over_x = partner(block, "x")
    over_y = partner(block, "y")
    over_both = partner(over_y, "x")
    here = jnp.stack([block, over_x, over_y, over_both])
    return jnp.stack([here, partner(here, "c")])


def scatter_plane(terms):
    chip = (terms[0].astype(f32) + partner(terms[1], "c").astype(f32)).astype(terms.dtype)
    over_x = partner(chip[1], "x")
    over_y = partner(chip[2], "y")
    over_both = opposite(chip[3])
    return (
        chip[0].astype(f32)
        + over_x.astype(f32)
        + over_y.astype(f32)
        + over_both.astype(f32)
    )


def nt(left, right):
    return lax.dot_general(left, right, (((1,), (1,)), ((), ())), preferred_element_type=f32)


def tn(left, right):
    return lax.dot_general(left, right, (((0,), (0,)), ((), ())), preferred_element_type=f32)


def nn(left, right):
    return lax.dot_general(left, right, (((1,), (0,)), ((), ())), preferred_element_type=f32)


def halves_swapped(values, half):
    lane = lax.broadcasted_iota(jnp.int32, values.shape, 1)
    up = pltpu.roll(values, half, 1)
    down = pltpu.roll(values, values.shape[1] - half, 1)
    return jnp.where(lane % (2 * half) < half, down, up)


def project_kernel(half, tokens_ref, weight_ref, cos_ref, sin_ref, q_ref, k_ref, v_ref):
    width = q_ref.shape[1]
    made = nn(tokens_ref[...], weight_ref[...])
    cosine, sine = cos_ref[...], sin_ref[...]
    for place, ref in ((0, q_ref), (1, k_ref)):
        part = made[:, place * width : (place + 1) * width]
        ref[...] = (part * cosine + halves_swapped(part, half) * sine).astype(bf16)
    v_ref[...] = made[:, 2 * width :].astype(bf16)


def project(tokens, weight, cosine, sine, half):
    rows, depth = tokens.shape
    width = weight.shape[1] // 3
    step = math.gcd(rows, 256)
    by_row = lambda w: pl.BlockSpec((step, w), lambda i: (i, 0))
    return pl.pallas_call(
        functools.partial(project_kernel, half),
        grid=(rows // step,),
        in_specs=[
            by_row(depth),
            pl.BlockSpec((depth, 3 * width), lambda i: (0, 0)),
            by_row(width),
            by_row(width),
        ],
        out_specs=[by_row(width)] * 3,
        out_shape=[jax.ShapeDtypeStruct((rows, width), bf16)] * 3,
        compiler_params=pltpu.CompilerParams(vmem_limit_bytes=24 * MIB),
        name="project",
    )(tokens, weight, cosine, sine)


def of_head(values, head, size):
    lane = lax.broadcasted_iota(jnp.int32, values.shape, 1)
    return jnp.where(lane // size == head, values, jnp.zeros_like(values))


def attend_kernel(size, scale, q_ref, k_ref, v_ref, o_ref, log_ref):
    keys, values, queries = k_ref[...], v_ref[...], q_ref[...]
    outs = []
    for head in range(q_ref.shape[1] // size):
        scores = nt(keys, of_head(queries, head, size))
        top = jnp.max(scores, axis=0, keepdims=True)
        weights = jnp.exp2((scores - top) * scale)
        total = jnp.sum(weights, axis=0, keepdims=True)
        probs = (weights * (1.0 / total)).astype(bf16)
        outs.append(tn(values, probs)[head * size : (head + 1) * size])
        log_ref[head : head + 1, :] = top * scale + jnp.log2(total)
    o_ref[...] = jnp.transpose(jnp.concatenate(outs, axis=0)).astype(bf16)


def attend(queries, keys, values, size):
    rows, width = queries.shape
    count = keys.shape[0]
    step = math.gcd(rows, 256 if count <= 2048 else 128)
    scale = math.log2(math.e) / math.sqrt(size)
    by_row = pl.BlockSpec((step, width), lambda i: (i, 0))
    whole = pl.BlockSpec((count, width), lambda i: (0, 0))
    return pl.pallas_call(
        functools.partial(attend_kernel, size, scale),
        grid=(rows // step,),
        in_specs=[by_row, whole, whole],
        out_specs=[by_row, pl.BlockSpec((8, step), lambda i: (0, i))],
        out_shape=[
            jax.ShapeDtypeStruct((rows, width), bf16),
            jax.ShapeDtypeStruct((8, rows), f32),
        ],
        compiler_params=pltpu.CompilerParams(vmem_limit_bytes=40 * MIB),
        name="attend",
    )(queries, keys, values)


def attend_back_kernel(
    size, scale, q_ref, k_ref, v_ref, grad_ref, log_ref, dq_ref, dk_ref, dv_ref
):
    @pl.when(pl.program_id(0) == 0)
    def _():
        dk_ref[...] = jnp.zeros_like(dk_ref)
        dv_ref[...] = jnp.zeros_like(dv_ref)

    keys, values, queries, grads = k_ref[...], v_ref[...], q_ref[...], grad_ref[...]
    exponent = scale * math.log2(math.e)
    outs = []
    for head in range(q_ref.shape[1] // size):
        query, grad = of_head(queries, head, size), of_head(grads, head, size)
        probs = jnp.exp2(nt(keys, query) * exponent - log_ref[head : head + 1, :])
        grad_probs = nt(values, grad)
        delta = jnp.sum(probs * grad_probs, axis=0, keepdims=True)
        grad_scores = (probs * (grad_probs - delta)).astype(bf16)
        outs.append(tn(keys, grad_scores)[head * size : (head + 1) * size])
        dk_ref[...] += nn(grad_scores, query) * scale
        dv_ref[...] += nn(probs.astype(bf16), grad)
    dq_ref[...] = jnp.transpose(jnp.concatenate(outs, axis=0)) * scale


def attend_back(queries, keys, values, grads, logs, size):
    rows, width = queries.shape
    count = keys.shape[0]
    step = math.gcd(rows, 256 if count <= 2048 else 128)
    by_row = pl.BlockSpec((step, width), lambda i: (i, 0))
    whole = pl.BlockSpec((count, width), lambda i: (0, 0))
    return pl.pallas_call(
        functools.partial(attend_back_kernel, size, 1.0 / math.sqrt(size)),
        grid=(rows // step,),
        in_specs=[by_row, whole, whole, by_row, pl.BlockSpec((8, step), lambda i: (0, i))],
        out_specs=[by_row, whole, whole],
        out_shape=[
            jax.ShapeDtypeStruct((rows, width), f32),
            jax.ShapeDtypeStruct((count, width), f32),
            jax.ShapeDtypeStruct((count, width), f32),
        ],
        compiler_params=pltpu.CompilerParams(vmem_limit_bytes=52 * MIB),
        name="attend_back",
    )(queries, keys, values, grads, logs)


def turn_back_kernel(half, dq_ref, dk_ref, dv_ref, cos_ref, sin_ref, out_ref):
    width = dq_ref.shape[1]
    cosine, sine = cos_ref[...], sin_ref[...]
    for place, ref in ((0, dq_ref), (1, dk_ref)):
        part = ref[...]
        turned = part * cosine - halves_swapped(part, half) * sine
        out_ref[:, place * width : (place + 1) * width] = turned.astype(bf16)
    out_ref[:, 2 * width :] = dv_ref[...].astype(bf16)


def turn_back(dq, dk, dv, cosine, sine, half):
    rows, width = dq.shape
    return pl.pallas_call(
        functools.partial(turn_back_kernel, half),
        out_shape=jax.ShapeDtypeStruct((rows, 3 * width), bf16),
        compiler_params=pltpu.CompilerParams(vmem_limit_bytes=24 * MIB),
        name="turn_back",
    )(dq, dk, dv, cosine, sine)


def normalize(values):
    centre = values - jnp.mean(values, axis=-1, keepdims=True)
    inverse = lax.rsqrt(jnp.mean(centre * centre, axis=-1, keepdims=True) + norm_eps)
    return centre * inverse, inverse


def normalize_back(scaled, normed, inverse):
    inner = jnp.mean(scaled * normed, axis=-1, keepdims=True)
    return inverse * (scaled - jnp.mean(scaled, axis=-1, keepdims=True) - normed * inner)


def columns_by(array, pieces, piece):
    rows, count = array.shape
    padded = jnp.pad(array, ((0, 0), (0, pieces * piece - count)))
    return jnp.swapaxes(padded.reshape(rows, pieces, piece), 0, 1)


def columns_back(array, count):
    pieces, rows, piece = array.shape
    return jnp.swapaxes(array, 0, 1).reshape(rows, pieces * piece)[:, :count]


def body(inputs, gain_attn, gain_mlp, w_qkv, w_attn_out, w_in, w_out, cotangent):
    pairs, planes = 8, 8
    rings = lax.axis_size("r")
    ci, yi, ri = (lax.axis_index(name) for name in "cyr")
    seqs, half_block, width = inputs.shape
    owned = w_qkv.shape[0]
    size = width // HEADS
    half = size // 2
    wide = width // pairs
    block = seqs * half_block
    span = pairs * block
    ff = w_out.shape[0]
    piece = -(-ff // (planes * LANES)) * LANES

    gain_one = gain_attn.astype(f32)[:, None]
    gain_two = gain_mlp.astype(f32)[:, None]

    tokens = core_swap(inputs).reshape(block, width).astype(f32)
    cotangent_here = core_swap(cotangent).reshape(block, width)
    normed_one, inverse_one = normalize(tokens)
    all_one = gather_chips(normed_one.astype(bf16)).reshape(span, width)

    scaled_qkv = (w_qkv.astype(f32) * gain_one).astype(bf16)
    part = scaled_qkv.reshape(owned, 3, pairs, wide).transpose(2, 0, 1, 3)
    part = part.reshape(pairs, owned, 3 * wide)
    part = lax.all_to_all(part, ("z", "x"), 0, 0, tiled=True)
    part = paired(part, partner(part, "c"), ci, 1)
    part = paired(part, partner(part, "y"), yi, 2)
    pair_qkv = lax.all_gather(part, "r", axis=0) if rings > 1 else part
    pair_qkv = pair_qkv.reshape(width, 3 * wide)

    full_attn = lax.all_gather(w_attn_out, ("r", "z", "x", "c", "y"), axis=0, tiled=True)

    scaled_in = (w_in.astype(f32) * gain_two).astype(bf16)
    turned_out = jnp.transpose(w_out)
    packed = jnp.concatenate(
        [
            columns_by(scaled_in[:, :ff], planes, piece),
            columns_by(scaled_in[:, ff:], planes, piece),
            columns_by(turned_out, planes, piece),
        ],
        axis=2,
    )
    packed = lax.all_to_all(packed, ("x", "c", "y"), 0, 0, tiled=True)
    packed = packed.reshape(planes * owned, 3 * piece)
    packed = lax.all_gather(packed, ("r", "z"), axis=0, tiled=True)
    part_in, part_out = packed[:, : 2 * piece], packed[:, 2 * piece :]

    all_cotangent = gather_plane(cotangent_here).reshape(planes * block, width)

    places = (ri * span + jnp.arange(span, dtype=jnp.int32)).astype(f32)
    frequency = rope_base ** (-2.0 * jnp.arange(half, dtype=jnp.int32).astype(f32) / size)
    angles = places[:, None] * frequency[None, :]
    cosine = jnp.tile(jnp.cos(angles), (1, wide // half))
    sine = jnp.sin(angles)
    sine = jnp.tile(jnp.concatenate([-sine, sine], axis=1), (1, wide // size))
    queries, keys, values = project(all_one, pair_qkv, cosine, sine, half)
    if rings > 1:
        keys = lax.all_gather(keys, "r", axis=0, tiled=True)
        values = lax.all_gather(values, "r", axis=0, tiled=True)
    heads_out, logs = attend(queries, keys, values, size)
    arrived = lax.all_to_all(heads_out.reshape(pairs, block, wide), ("z", "x"), 0, 0, tiled=True)
    attended = jnp.swapaxes(arrived, 0, 1).reshape(block, width)

    middle = tokens + nn(attended, full_attn)
    normed_two, inverse_two = normalize(middle)
    all_two = gather_plane(normed_two.astype(bf16)).reshape(planes * block, width)

    gate_up = nn(all_two, part_in)
    grad_hidden = nt(all_cotangent, part_out.T)
    gate, lift = gate_up[:, :piece], gate_up[:, piece:]
    cdf = 0.5 * (1.0 + lax.erf(gate * math.sqrt(0.5)))
    density = jnp.exp(-0.5 * gate * gate) * (1.0 / math.sqrt(2.0 * math.pi))
    activated = gate * cdf
    hidden = (activated * lift).astype(bf16)
    grad_gate_up = jnp.concatenate(
        [grad_hidden * lift * (cdf + gate * density), grad_hidden * activated], axis=1
    ).astype(bf16)
    plane_shape = (2, 4, block, width)
    grad_two = scatter_plane(nt(grad_gate_up, part_in).astype(bf16).reshape(plane_shape))
    result = scatter_plane(nt(hidden, part_out).astype(bf16).reshape(plane_shape))
    output = core_swap((middle + result).astype(bf16).reshape(seqs, half_block, width))

    grad_packed = jnp.concatenate([tn(all_two, grad_gate_up), tn(all_cotangent, hidden)], axis=1)
    grad_packed = lax.psum_scatter(
        grad_packed.astype(bf16), ("r", "z"), scatter_dimension=0, tiled=True
    )
    grad_packed = lax.all_to_all(
        grad_packed.reshape(planes, owned, 3 * piece), ("x", "c", "y"), 0, 0, tiled=True
    ).astype(f32)
    grad_in = jnp.concatenate(
        [
            columns_back(grad_packed[:, :, :piece], ff),
            columns_back(grad_packed[:, :, piece : 2 * piece], ff),
        ],
        axis=1,
    )
    grad_out = jnp.transpose(columns_back(grad_packed[:, :, 2 * piece :], ff))
    grad_gain_mlp = jnp.sum(grad_in * w_in.astype(f32), axis=1)
    grad_in = grad_in * gain_two

    grad_middle = cotangent_here.astype(f32) + normalize_back(grad_two, normed_two, inverse_two)
    grad_branch = grad_middle.astype(bf16)

    grad_attended = nt(grad_branch, full_attn).astype(bf16)
    leaving = jnp.swapaxes(grad_attended.reshape(block, pairs, wide), 0, 1)
    grad_heads = lax.all_to_all(leaving, ("z", "x"), 0, 0, tiled=True).reshape(span, wide)

    terms = tn(attended, grad_branch).astype(bf16)
    if rings > 1:
        terms = lax.psum_scatter(terms, "r", scatter_dimension=0, tiled=True)
    terms = terms.reshape(pairs, 2, 2, owned, width)
    grad_attn = sum_square(terms)
    grad_attn = scatter_chips(grad_attn.reshape(4, 2, owned, width))

    grad_q, grad_k, grad_v = attend_back(queries, keys, values, grad_heads, logs, size)
    if rings > 1:
        grad_k = lax.psum_scatter(grad_k, "r", scatter_dimension=0, tiled=True)
        grad_v = lax.psum_scatter(grad_v, "r", scatter_dimension=0, tiled=True)
    grad_projected = turn_back(grad_q, grad_k, grad_v, cosine, sine, half)

    grad_one = nt(grad_projected, pair_qkv).astype(bf16)
    grad_one = scatter_chips(grad_one.reshape(4, 2, block, width))
    input_grad = grad_middle + normalize_back(grad_one, normed_one, inverse_one)
    input_grad = core_swap(input_grad.reshape(seqs, half_block, width))

    terms = tn(all_one, grad_projected).astype(bf16)
    if rings > 1:
        terms = lax.psum_scatter(terms, "r", scatter_dimension=0, tiled=True)
    terms = sum_square(terms.reshape(pairs, 2, 2, owned, 3 * wide))
    terms = lax.all_to_all(terms, ("z", "x"), 0, 0, tiled=True).astype(f32)
    grad_qkv = terms.reshape(pairs, owned, 3, wide).transpose(1, 2, 0, 3).reshape(owned, 3 * width)
    grad_gain_attn = jnp.sum(grad_qkv * w_qkv.astype(f32), axis=1)
    grad_qkv = grad_qkv * gain_one
    return (
        output,
        input_grad,
        grad_gain_attn,
        grad_gain_mlp,
        grad_qkv,
        grad_attn,
        grad_in,
        grad_out,
    )


def sum_square(terms):
    ci, yi = lax.axis_index("c"), lax.axis_index("y")

    def member(array, place):
        return lax.dynamic_index_in_dim(array, place, 1, False)

    own = member(terms, ci).astype(f32)
    terms = (own + partner(member(terms, 1 - ci), "c").astype(f32)).astype(terms.dtype)
    own = member(terms, yi).astype(f32)
    return (own + partner(member(terms, 1 - yi), "y").astype(f32)).astype(terms.dtype)


def solution(mesh):
    ctx, fsdp = mesh.shape["ctx"], mesh.shape["fsdp"]
    grid = Mesh(mesh.devices.reshape(ctx // 16, 4, 2, 2, fsdp), ("r", "z", "x", "c", "y"))
    tokens = P("y", ("r", "z", "x", "c"), None)
    everyone = ("r", "z", "x", "c", "y")
    gain, rows, columns = P(everyone), P(everyone, None), P(None, everyone)
    return jax.shard_map(
        body,
        mesh=grid,
        in_specs=(tokens, gain, gain, rows, rows, rows, columns, tokens),
        out_specs=(tokens, tokens, gain, gain, rows, rows, rows, columns),
        check_vma=False,
    )
```

time: 1440 us -> 332 us (0.23)
  waiting for transfers between devices: 1010 us -> 120 us
  blocking collectives: 125 us -> 0 us
  matrix products: 124 us -> 19.5 us
  local copies, waits for them, and re-layouts: 133 us -> 33.2 us
  starting transfers between devices: 11.3 us -> 84.6 us
  Pallas kernels: 0 us -> 21.7 us
  other arithmetic: 19.6 us -> 35.9 us
    reduce_scatter x3 -> x1, waiting for transfers between devices: 618 us -> 0.01 us  [body(): lax.psum_scatter(grad_packed.astype(bf16), ('r', 'z'), scatter_dimension=...]
    all_gather x8 -> x2, waiting for transfers between devices: 265 us -> 11.5 us  [the longest x1 11.5 us: body(): packed = lax.all_gather(packed, ('r', 'z'), axis=0, tiled=True)]
    unnamed x13 -> x3, waiting for transfers between devices: 123 us -> 1.39 us
    dot_general x26 -> x11, matrix products: 124 us -> 19.5 us  [the longest x5 7.28 us: nt(): lax.dot_general(left, right, (((1,), (1,)), ((), ())), preferred_element_...]
    ppermute x0 -> x47, waiting for transfers between devices: none -> 95.3 us  [the longest x45 84.7 us: partner(): return lax.ppermute(array, axis, [(i, i ^ step) for i in range(size)])]
    unnamed x2 -> x0, blocking collectives: 81 us -> none
    ppermute x0 -> x47, starting transfers between devices: none -> 54 us  [the longest x45 51 us: partner(): return lax.ppermute(array, axis, [(i, i ^ step) for i in range(size)])]
    all_gather x2 -> x0, blocking collectives: 43.9 us -> none  [the longest x1 24.9 us: body(): lax.all_gather(log_total.astype(jnp.bfloat16), 'ctx', axis=1, tiled=True)]
  transfers between devices with their start and end apart: 12 -> 56, of which waited for: 9 -> 24; matrix products, arithmetic and copies ran while one was open for 18% -> 19% of each run, Pallas kernels for 0% -> 7%
where the time goes in v1:
time: 332 us; the launch traced here: 330 us
  waiting for transfers between devices  120 us (36%)
  starting transfers between devices  84.6 us (25%)
  other arithmetic  35.9 us (11%)
  local copies, waits for them, and re-layouts  33.2 us (10%)
  Pallas kernels  21.7 us (7%)
  matrix products  19.5 us (6%)
  between operations  14.9 us (4%)
    ppermute x45, waiting for transfers between devices, partner(): return lax.ppermute(array, axis, [(i, i ^ step) for i in range(size)])  84.7 us
    ppermute x45, starting transfers between devices, partner(): return lax.ppermute(array, axis, [(i, i ^ step) for i in range(size)])  51 us
    pallas_call x1, Pallas kernels, attend_back(): pl.pallas_call(functools.partial(attend_back_kernel, size, 1.0 / math.sqr...  11.6 us
    all_gather x1, waiting for transfers between devices, body(): packed = lax.all_gather(packed, ('r', 'z'), axis=0, tiled=True)  11.5 us
    unnamed x79, local copies, waits for them, and re-layouts  10.9 us
    ppermute x2, waiting for transfers between devices, opposite(): return lax.ppermute(array, ('x', 'y'), [(i, 3 - i) for i in range(4)])  10.5 us
    another operation x4, other arithmetic, gather_plane(): return jnp.stack([here, partner(here, 'c')])  10 us
    all_to_all x1, waiting for transfers between devices, body(): lax.all_to_all(leaving, ('z', 'x'), 0, 0, tiled=True).reshape(span, wide)  7.95 us
  transfers between devices with their start and end apart: 56, of which 24 were waited for; matrix products, arithmetic and copies ran while one was open for 19% of the time, Pallas kernels for 7%

profile of v1, /device:TPU:0, one launch (start us, length us, event | category | flops | bytes accessed | tf_op | source)
XLA Modules:
  0.0 330.0 jit_solution(16850843645437952079)
XLA Ops:
  13.7 7.3 %all-to-all-start = ((bf16[8,32,384]{2,1,0:T(8,128)(2,1)}), bf16[8,32,384]{2,1,0:T(8,128)(2,1)S(1)}, u32[]{:S(2)}, u32[]{:S(2)}) async-start(bf16[8,32,384]{2,1,0:T(8,128)(2,1)} %reshape.313), calls=%async_computation | async-start | bytes 393216 | tf_op jit(solution)/shard_map/all_to_all | solution.py:293
  25.4 3.8 %collective-permute-start.6 = (bf16[128,1024]{1,0:T(8,128)(2,1)}, bf16[128,1024]{1,0:T(8,128)(2,1)}, u32[]{:S(2)}, u32[]{:S(2)}) collective-permute-start(bf16[128,1024]{1,0:T(8,128)(2,1)} %fusion.33), channel_id=1, source_target_pairs={{0,24},{8,16},{16,8},{24,0},{1,25},{9,17},{17,9},{25,1},{2,26},{10... | collective-permute-start | bytes 786440 | tf_op jit(solution)/shard_map/ppermute | solution.py:23
  29.8 2.0 collective-permute-start.1
  32.8 4.2 %all-to-all-start.2 = ((bf16[8,32,1152]{2,1,0:T(8,128)(2,1)}), bf16[8,32,1152]{2,1,0:T(8,128)(2,1)}, u32[]{:S(2)}, u32[]{:S(2)}) async-start(bf16[8,32,1152]{2,1,0:T(8,128)(2,1)} %copy.56), calls=%async_computation.2 | async-start | bytes 1179648 | tf_op jit(solution)/shard_map/all_to_all | solution.py:311
  37.4 16.2 %collective-permute-done.4 = bf16[128,1024]{1,0:T(8,128)(2,1)} collective-permute-done((bf16[128,1024]{1,0:T(8,128)(2,1)}, bf16[128,1024]{1,0:T(8,128)(2,1)}, u32[]{:S(2)}, u32[]{:S(2)}) %collective-permute-start.4) | collective-permute-done | bytes 262176 | tf_op jit(solution)/shard_map/ppermute | solution.py:23
  61.6 14.9 %collective-permute-done.3 = bf16[128,1024]{1,0:T(8,128)(2,1)S(1)} collective-permute-done((bf16[128,1024]{1,0:T(8,128)(2,1)}, bf16[128,1024]{1,0:T(8,128)(2,1)S(1)}, u32[]{:S(2)}, u32[]{:S(2)}) %collective-permute-start.3) | collective-permute-done | bytes 262176 | tf_op jit(solution)/shard_map/ppermute | solution.py:23
  79.0 2.3 project.1
  82.2 7.2 %attend.1 = (bf16[1024,128]{1,0:T(8,128)(2,1)S(1)}, f32[8,1024]{1,0:T(8,128)S(1)}) custom-call(bf16[1024,128]{1,0:T(8,128)(2,1)S(1)} %get-tuple-element.16.q_ref, bf16[1024,128]{1,0:T(8,128)(2,1)S(1)} %get-tuple-element.17.k_ref, bf16[1024,128]{1,0:T(8,128)(2,1)S(1)} %get-tuple-element.18.v_ref), custom_call_target="tpu_custom_call" | custom-call | tf_op jit(solution)/shard_map/attend/pallas_call | solution.py:168
  90.8 1.8 copy.55
  92.6 4.0 %all-to-all-start.1 = ((bf16[8,128,128]{1,2,0:T(8,128)(2,1)}), bf16[8,128,128]{1,2,0:T(8,128)(2,1)}, u32[]{:S(2)}, u32[]{:S(2)}) async-start(bf16[8,128,128]{1,2,0:T(8,128)(2,1)} %copy.55), calls=%async_computation.1 | async-start | bytes 524288 | tf_op jit(solution)/shard_map/all_to_all | solution.py:329
  100.8 4.1 %all-to-all-done.1 = bf16[8,128,128]{1,2,0:T(8,128)(2,1)} async-done(((bf16[8,128,128]{1,2,0:T(8,128)(2,1)}), bf16[8,128,128]{1,2,0:T(8,128)(2,1)}, u32[]{:S(2)}, u32[]{:S(2)}) %all-to-all-start.1) | async-done | bytes 262176 | tf_op jit(solution)/shard_map/all_to_all | solution.py:329
  104.9 2.3 fusion.64
  107.6 1.8 collective-permute-start.11
  115.4 3.4 %collective-permute-done.20 = bf16[128,1024]{1,0:T(8,128)(2,1)S(1)} collective-permute-done((bf16[128,1024]{1,0:T(8,128)(2,1)}, bf16[128,1024]{1,0:T(8,128)(2,1)S(1)}, u32[]{:S(2)}, u32[]{:S(2)}) %collective-permute-start.20) | collective-permute-done | bytes 262176 | tf_op jit(solution)/shard_map/ppermute | solution.py:23
  118.8 5.6 %collective-permute-done.22 = bf16[128,1024]{1,0:T(8,128)(2,1)S(1)} collective-permute-done((bf16[128,1024]{1,0:T(8,128)(2,1)}, bf16[128,1024]{1,0:T(8,128)(2,1)S(1)}, u32[]{:S(2)}, u32[]{:S(2)}) %collective-permute-start.22) | collective-permute-done | bytes 262176 | tf_op jit(solution)/shard_map/ppermute | solution.py:23
  124.4 2.5 fusion.58
  127.1 2.1 collective-permute-done.10
  129.2 2.8 collective-permute-done.12
  133.5 3.2 pad_maximum_fusion.2
  136.7 2.8 pad_maximum_fusion.1
  139.5 11.5 %all-gather.5.cloned.1.call-done = bf16[1024,1152]{1,0:T(8,128)(2,1)} async-done(((bf16[256,1152]{1,0:T(8,128)(2,1)}), bf16[1024,1152]{1,0:T(8,128)(2,1)}) %all-gather.5.cloned.1.call-update) | async-done | bytes 2359312 | tf_op jit(solution)/shard_map/all_gather | solution.py:313
  151.0 4.1 %fusion.10 = f32[1024,768]{0,1:T(8,128)S(1)} fusion(bf16[1024,1024]{1,0:T(8,128)(2,1)} %bitcast.299, bf16[1024,1152]{1,0:T(8,128)(2,1)} %all-gather.5.cloned.1.call-done), kind=kOutput, calls=%fused_computation.29 | convolution fusion | flops 1610612736 | bytes 6815744 | tf_op jit(solution)/shard_map/dot_general | solution.py:101
  155.1 2.0 fusion.8
  160.0 1.8 convolution_convert_fusion.3
  164.2 1.8 convolution_convert_fusion.4
  168.7 2.0 fusion.1
  181.5 5.1 %collective-permute-done.27 = bf16[128,1024]{1,0:T(8,128)(2,1)S(1)} collective-permute-done((bf16[128,1024]{1,0:T(8,128)(2,1)S(1)}, bf16[128,1024]{1,0:T(8,128)(2,1)S(1)}, u32[]{:S(2)}, u32[]{:S(2)}) %collective-permute-start.27) | collective-permute-done | bytes 262176 | tf_op jit(solution)/shard_map/ppermute | solution.py:27
  186.6 1.9 collective-permute-done.26
  188.8 2.5 collective-permute-done.15
  191.3 5.4 %collective-permute-done.17 = bf16[128,1024]{1,0:T(8,128)(2,1)S(1)} collective-permute-done((bf16[128,1024]{1,0:T(8,128)(2,1)S(1)}, bf16[128,1024]{1,0:T(8,128)(2,1)S(1)}, u32[]{:S(2)}, u32[]{:S(2)}) %collective-permute-start.17) | collective-permute-done | bytes 262176 | tf_op jit(solution)/shard_map/ppermute | solution.py:27
  198.1 1.9 multiply_add_fusion.1
  201.6 4.3 %all-to-all-start.3 = ((bf16[8,128,128]{2,1,0:T(8,128)(2,1)}), bf16[8,128,128]{2,1,0:T(8,128)(2,1)}, u32[]{:S(2)}, u32[]{:S(2)}) async-start(bf16[8,128,128]{2,1,0:T(8,128)(2,1)} %bitcast.314), calls=%async_computation.3 | async-start | bytes 524288 | tf_op jit(solution)/shard_map/all_to_all | solution.py:374
  207.4 1.8 convolution_convert_fusion.2
  212.2 7.9 %all-to-all-done.3 = bf16[8,128,128]{2,1,0:T(8,128)(2,1)} async-done(((bf16[8,128,128]{2,1,0:T(8,128)(2,1)}), bf16[8,128,128]{2,1,0:T(8,128)(2,1)}, u32[]{:S(2)}, u32[]{:S(2)}) %all-to-all-start.3) | async-done | bytes 262176 | tf_op jit(solution)/shard_map/all_to_all | solution.py:374
  222.0 11.6 %attend_back.1 = (f32[1024,128]{1,0:T(8,128)S(1)}, f32[1024,128]{1,0:T(8,128)}, f32[1024,128]{1,0:T(8,128)}) custom-call(bf16[1024,128]{1,0:T(8,128)(2,1)S(1)} %get-tuple-element.16.q_ref, bf16[1024,128]{1,0:T(8,128)(2,1)S(1)} %copy-done.3, bf16[1024,128]{1,0:T(8,128)(2,1)S(1)} %copy-done.5, bf16[1024,128]{1,0:T(8,128)(2,1)} %bitcast.67.grad_ref, ...), custom_call_target="tpu_custom_call" | custom-call | tf_op jit(solution)/shard_map/attend_back/pallas_call | solution.py:211
  244.5 2.6 collective-permute-done.28
  248.5 4.2 %collective-permute-done.32 = bf16[128,1024]{1,0:T(8,128)(2,1)S(1)} collective-permute-done((bf16[128,1024]{1,0:T(8,128)(2,1)S(1)}, bf16[128,1024]{1,0:T(8,128)(2,1)S(1)}, u32[]{:S(2)}, u32[]{:S(2)}) %collective-permute-start.32) | collective-permute-done | bytes 262176 | tf_op jit(solution)/shard_map/ppermute | solution.py:23
  252.6 5.6 %collective-permute-done.30 = bf16[128,1024]{1,0:T(8,128)(2,1)S(1)} collective-permute-done((bf16[128,1024]{1,0:T(8,128)(2,1)S(1)}, bf16[128,1024]{1,0:T(8,128)(2,1)S(1)}, u32[]{:S(2)}, u32[]{:S(2)}) %collective-permute-start.30) | collective-permute-done | bytes 262176 | tf_op jit(solution)/shard_map/ppermute | solution.py:23
  258.7 1.9 collective-permute-start.33
  260.6 2.4 collective-permute-start.31
  264.7 12.2 %collective-permute-done.29 = bf16[128,1024]{1,0:T(8,128)(2,1)S(1)} collective-permute-done((bf16[128,1024]{1,0:T(8,128)(2,1)S(1)}, bf16[128,1024]{1,0:T(8,128)(2,1)S(1)}, u32[]{:S(2)}, u32[]{:S(2)}) %collective-permute-start.29) | collective-permute-done | bytes 262176 | tf_op jit(solution)/shard_map/ppermute | solution.py:23
  284.2 7.2 %all-to-all-start.4 = ((bf16[8,32,384]{2,1,0:T(8,128)(2,1)}), bf16[8,32,384]{2,1,0:T(8,128)(2,1)S(1)}, u32[]{:S(2)}, u32[]{:S(2)}) async-start(bf16[8,32,384]{2,1,0:T(8,128)(2,1)} %fusion.36), calls=%async_computation.4 | async-start | bytes 393216 | tf_op jit(solution)/shard_map/all_to_all | solution.py:398
  292.4 3.0 collective-permute-done.39
  301.2 2.1 copy.63
  303.3 3.5 %all-to-all-start.5 = ((bf16[8,32,1152]{2,1,0:T(8,128)(2,1)}), bf16[8,32,1152]{2,1,0:T(8,128)(2,1)S(1)}, u32[]{:S(2)}, u32[]{:S(2)}) async-start(bf16[8,32,1152]{2,1,0:T(8,128)(2,1)} %bitcast.88), calls=%async_computation.6 | async-start | bytes 1179648 | tf_op jit(solution)/shard_map/all_to_all | solution.py:355
  307.0 5.0 %collective-permute-start.41 = (bf16[32,1024]{1,0:T(8,128)(2,1)S(1)}, bf16[32,1024]{1,0:T(8,128)(2,1)S(1)}, u32[]{:S(2)}, u32[]{:S(2)}) collective-permute-start(bf16[32,1024]{1,0:T(8,128)(2,1)S(1)} %get-tuple-element.64), channel_id=1, source_target_pairs={{0,16},{8,24},{16,0},{24,8},{1,17},{9,25},{17,1},{25,9},{2,18},{10... | collective-permute-start | bytes 196616 | tf_op jit(solution)/shard_map/ppermute | solution.py:23
  312.4 2.3 collective-permute-start.43
  316.2 3.7 %collective-permute-done.43 = bf16[32,1024]{1,0:T(8,128)(2,1)S(1)} collective-permute-done((bf16[32,1024]{1,0:T(8,128)(2,1)S(1)}, bf16[32,1024]{1,0:T(8,128)(2,1)S(1)}, u32[]{:S(2)}, u32[]{:S(2)}) %collective-permute-start.43) | collective-permute-done | bytes 65568 | tf_op jit(solution)/shard_map/ppermute | solution.py:23
  (265 shorter events, 99.3 us)
Async XLA Ops:
  7.2 97.7 %all-gather.3.cloned.1.call-start = ((), (), s32[]{:S(2)}) async-start(), calls=%async_computation.7 | async-start | bytes 2162688 | tf_op jit(solution)/shard_map/all_gather | solution.py:299
  9.5 87.9 %collective-permute-start.19 = (bf16[64,1024]{1,0:T(8,128)(2,1)}, bf16[64,1024]{1,0:T(8,128)(2,1)}, u32[]{:S(2)}, u32[]{:S(2)}) collective-permute-start(bf16[64,1024]{1,0:T(8,128)(2,1)} %dynamic-slice_bitcast_fusion.8), channel_id=1, source_target_pairs={{0,2},{2,0},{1,3},{3,1},{4,6},{6,4},{5,7},{7,5},{8,10},{10,8},{9,1... | collective-permute-start | bytes 393224 | tf_op jit(solution)/shard_map/ppermute | solution.py:23
  10.9 12.6 %collective-permute-start = (bf16[64,1024]{1,0:T(8,128)(2,1)S(1)}, bf16[64,1024]{1,0:T(8,128)(2,1)S(1)}, u32[]{:S(2)}, u32[]{:S(2)}) collective-permute-start(bf16[64,1024]{1,0:T(8,128)(2,1)S(1)} %dynamic-slice_bitcast_fusion.10), channel_id=1, source_target_pairs={{0,2},{2,0},{1,3},{3,1},{4,6},{6,4},{5,7},{7,5},{8,10},{10,8},{9,1... | collective-permute-start | bytes 393224 | tf_op jit(solution)/shard_map/ppermute | solution.py:23
  13.7 19.1 %all-to-all-start = ((bf16[8,32,384]{2,1,0:T(8,128)(2,1)}), bf16[8,32,384]{2,1,0:T(8,128)(2,1)S(1)}, u32[]{:S(2)}, u32[]{:S(2)}) async-start(bf16[8,32,384]{2,1,0:T(8,128)(2,1)} %reshape.313), calls=%async_computation | async-start | bytes 393216 | tf_op jit(solution)/shard_map/all_to_all | solution.py:293
  25.4 12.0 %collective-permute-start.6 = (bf16[128,1024]{1,0:T(8,128)(2,1)}, bf16[128,1024]{1,0:T(8,128)(2,1)}, u32[]{:S(2)}, u32[]{:S(2)}) collective-permute-start(bf16[128,1024]{1,0:T(8,128)(2,1)} %fusion.33), channel_id=1, source_target_pairs={{0,24},{8,16},{16,8},{24,0},{1,25},{9,17},{17,9},{25,1},{2,26},{10... | collective-permute-start | bytes 786440 | tf_op jit(solution)/shard_map/ppermute | solution.py:23
  29.2 24.4 %collective-permute-start.4 = (bf16[128,1024]{1,0:T(8,128)(2,1)}, bf16[128,1024]{1,0:T(8,128)(2,1)}, u32[]{:S(2)}, u32[]{:S(2)}) collective-permute-start(bf16[128,1024]{1,0:T(8,128)(2,1)} %fusion.33), channel_id=1, source_target_pairs={{0,16},{8,24},{16,0},{24,8},{1,17},{9,25},{17,1},{25,9},{2,18},{10... | collective-permute-start | bytes 786440 | tf_op jit(solution)/shard_map/ppermute | solution.py:23
  29.2 25.8 %collective-permute-start.2 = (bf16[128,1024]{1,0:T(8,128)(2,1)}, bf16[128,1024]{1,0:T(8,128)(2,1)}, u32[]{:S(2)}, u32[]{:S(2)}) collective-permute-start(bf16[128,1024]{1,0:T(8,128)(2,1)} %fusion.33), channel_id=1, source_target_pairs={{0,8},{8,0},{16,24},{24,16},{1,9},{9,1},{17,25},{25,17},{2,10},{10... | collective-permute-start | bytes 786440 | tf_op jit(solution)/shard_map/ppermute | solution.py:23
  29.8 25.9 %collective-permute-start.1 = (bf16[128,1024]{1,0:T(8,128)(2,1)}, bf16[128,1024]{1,0:T(8,128)(2,1)}, u32[]{:S(2)}, u32[]{:S(2)}) collective-permute-start(bf16[128,1024]{1,0:T(8,128)(2,1)} %fusion.33), channel_id=1, source_target_pairs={{0,4},{4,0},{1,5},{5,1},{2,6},{6,2},{3,7},{7,3},{8,12},{12,8},{9,1... | collective-permute-start | bytes 786440 | tf_op jit(solution)/shard_map/ppermute | solution.py:23
  32.8 59.8 %all-to-all-start.2 = ((bf16[8,32,1152]{2,1,0:T(8,128)(2,1)}), bf16[8,32,1152]{2,1,0:T(8,128)(2,1)}, u32[]{:S(2)}, u32[]{:S(2)}) async-start(bf16[8,32,1152]{2,1,0:T(8,128)(2,1)} %copy.56), calls=%async_computation.2 | async-start | bytes 1179648 | tf_op jit(solution)/shard_map/all_to_all | solution.py:311
  37.4 21.7 %collective-permute-start.8 = (bf16[8,32,384]{2,1,0:T(8,128)(2,1)S(1)}, bf16[8,32,384]{2,1,0:T(8,128)(2,1)S(1)}, u32[]{:S(2)}, u32[]{:S(2)}) collective-permute-start(bf16[8,32,384]{2,1,0:T(8,128)(2,1)S(1)} %all-to-all-done), channel_id=1, source_target_pairs={{0,2},{2,0},{1,3},{3,1},{4,6},{6,4},{5,7},{7,5},{8,10},{10,8},{9,1... | collective-permute-start | bytes 589832 | tf_op jit(solution)/shard_map/ppermute | solution.py:23
  53.6 25.0 %collective-permute-start.7 = (bf16[128,1024]{1,0:T(8,128)(2,1)}, bf16[128,1024]{1,0:T(8,128)(2,1)S(1)}, u32[]{:S(2)}, u32[]{:S(2)}) collective-permute-start(bf16[128,1024]{1,0:T(8,128)(2,1)} %collective-permute-done.6), channel_id=1, source_target_pairs={{0,4},{4,0},{1,5},{5,1},{2,6},{6,2},{3,7},{7,3},{8,12},{12,8},{9,1... | collective-permute-start | bytes 786440 | tf_op jit(solution)/shard_map/ppermute | solution.py:23
  55.0 22.5 %collective-permute-start.5 = (bf16[128,1024]{1,0:T(8,128)(2,1)}, bf16[128,1024]{1,0:T(8,128)(2,1)S(1)}, u32[]{:S(2)}, u32[]{:S(2)}) collective-permute-start(bf16[128,1024]{1,0:T(8,128)(2,1)} %collective-permute-done.4), channel_id=1, source_target_pairs={{0,4},{4,0},{1,5},{5,1},{2,6},{6,2},{3,7},{7,3},{8,12},{12,8},{9,1... | collective-permute-start | bytes 786440 | tf_op jit(solution)/shard_map/ppermute | solution.py:23
  55.7 20.9 %collective-permute-start.3 = (bf16[128,1024]{1,0:T(8,128)(2,1)}, bf16[128,1024]{1,0:T(8,128)(2,1)S(1)}, u32[]{:S(2)}, u32[]{:S(2)}) collective-permute-start(bf16[128,1024]{1,0:T(8,128)(2,1)} %collective-permute-done.2), channel_id=1, source_target_pairs={{0,4},{4,0},{1,5},{5,1},{2,6},{6,2},{3,7},{7,3},{8,12},{12,8},{9,1... | collective-permute-start | bytes 786440 | tf_op jit(solution)/shard_map/ppermute | solution.py:23
  60.1 18.6 %collective-permute-start.9 = (bf16[8,2,32,384]{3,2,0,1:T(8,128)(2,1)S(1)}, bf16[8,2,32,384]{3,2,0,1:T(8,128)(2,1)S(1)}, u32[]{:S(2)}, u32[]{:S(2)}) collective-permute-start(bf16[8,2,32,384]{3,2,0,1:T(8,128)(2,1)S(1)} %pad_maximum_fusion.12), channel_id=1, source_target_pairs={{0,1},{1,0},{2,3},{3,2},{4,5},{5,4},{6,7},{7,6},{8,9},{9,8},{10,11... | collective-permute-start | bytes 1179656 | tf_op jit(solution)/shard_map/ppermute | solution.py:23
  92.6 12.3 %all-to-all-start.1 = ((bf16[8,128,128]{1,2,0:T(8,128)(2,1)}), bf16[8,128,128]{1,2,0:T(8,128)(2,1)}, u32[]{:S(2)}, u32[]{:S(2)}) async-start(bf16[8,128,128]{1,2,0:T(8,128)(2,1)} %copy.55), calls=%async_computation.1 | async-start | bytes 524288 | tf_op jit(solution)/shard_map/all_to_all | solution.py:329
  96.7 54.3 %all-gather.5.cloned.1.call-start = ((), (), s32[]{:S(2)}) async-start(), calls=%async_computation.8 | async-start | bytes 2949120 | tf_op jit(solution)/shard_map/all_gather | solution.py:313
  97.4 203.8 %reduce-scatter.2.cloned.1.call-start = ((), (), s32[]{:S(2)}) async-start(), calls=%async_computation.9 | async-start | bytes 2949120 | tf_op jit(solution)/shard_map/reduce_scatter | solution.py:352
  99.2 11.5 %collective-permute-start.21 = (bf16[128,1024]{1,0:T(8,128)(2,1)}, bf16[128,1024]{1,0:T(8,128)(2,1)}, u32[]{:S(2)}, u32[]{:S(2)}) collective-permute-start(bf16[128,1024]{1,0:T(8,128)(2,1)} %bitcast.52), channel_id=1, source_target_pairs={{0,1},{1,0},{2,3},{3,2},{4,5},{5,4},{6,7},{7,6},{8,9},{9,8},{10,11... | collective-permute-start | bytes 786440 | tf_op jit(solution)/shard_map/ppermute | solution.py:23
  109.3 9.5 %collective-permute-start.20 = (bf16[128,1024]{1,0:T(8,128)(2,1)}, bf16[128,1024]{1,0:T(8,128)(2,1)S(1)}, u32[]{:S(2)}, u32[]{:S(2)}) collective-permute-start(bf16[128,1024]{1,0:T(8,128)(2,1)} %bitcast.52), channel_id=1, source_target_pairs={{0,4},{4,0},{1,5},{5,1},{2,6},{6,2},{3,7},{7,3},{8,12},{12,8},{9,1... | collective-permute-start | bytes 786440 | tf_op jit(solution)/shard_map/ppermute | solution.py:23
  110.7 13.8 %collective-permute-start.22 = (bf16[128,1024]{1,0:T(8,128)(2,1)}, bf16[128,1024]{1,0:T(8,128)(2,1)S(1)}, u32[]{:S(2)}, u32[]{:S(2)}) collective-permute-start(bf16[128,1024]{1,0:T(8,128)(2,1)} %collective-permute-done.21), channel_id=1, source_target_pairs={{0,4},{4,0},{1,5},{5,1},{2,6},{6,2},{3,7},{7,3},{8,12},{12,8},{9,1... | collective-permute-start | bytes 786440 | tf_op jit(solution)/shard_map/ppermute | solution.py:23
  111.4 17.8 %collective-permute-start.10 = (bf16[128,1024]{1,0:T(8,128)(2,1)S(1)}, bf16[128,1024]{1,0:T(8,128)(2,1)S(1)}, u32[]{:S(2)}, u32[]{:S(2)}) collective-permute-start(bf16[128,1024]{1,0:T(8,128)(2,1)S(1)} %fusion.32), channel_id=1, source_target_pairs={{0,4},{4,0},{1,5},{5,1},{2,6},{6,2},{3,7},{7,3},{8,12},{12,8},{9,1... | collective-permute-start | bytes 786440 | tf_op jit(solution)/shard_map/ppermute | solution.py:23
  114.0 18.0 %collective-permute-start.12 = (bf16[128,1024]{1,0:T(8,128)(2,1)S(1)}, bf16[128,1024]{1,0:T(8,128)(2,1)S(1)}, u32[]{:S(2)}, u32[]{:S(2)}) collective-permute-start(bf16[128,1024]{1,0:T(8,128)(2,1)S(1)} %collective-permute-done.11), channel_id=1, source_target_pairs={{0,4},{4,0},{1,5},{5,1},{2,6},{6,2},{3,7},{7,3},{8,12},{12,8},{9,1... | collective-permute-start | bytes 786440 | tf_op jit(solution)/shard_map/ppermute | solution.py:23
  163.4 10.9 %collective-permute-start.14 = (bf16[4,128,1024]{2,1,0:T(8,128)(2,1)}, bf16[4,128,1024]{2,1,0:T(8,128)(2,1)}, u32[]{:S(2)}, u32[]{:S(2)}) collective-permute-start(bf16[4,128,1024]{2,1,0:T(8,128)(2,1)} %bitcast.38), channel_id=1, source_target_pairs={{0,2},{2,0},{1,3},{3,1},{4,6},{6,4},{5,7},{7,5},{8,10},{10,8},{9,1... | collective-permute-start | bytes 3145736 | tf_op jit(solution)/shard_map/ppermute | solution.py:23
  170.7 9.3 %collective-permute-start.25 = (bf16[128,1024]{1,0:T(8,128)(2,1)S(1)}, bf16[128,1024]{1,0:T(8,128)(2,1)S(1)}, u32[]{:S(2)}, u32[]{:S(2)}) collective-permute-start(bf16[128,1024]{1,0:T(8,128)(2,1)S(1)} %get-tuple-element.46), channel_id=1, source_target_pairs={{0,4},{4,0},{1,5},{5,1},{2,6},{6,2},{3,7},{7,3},{8,12},{12,8},{9,1... | collective-permute-start | bytes 786440 | tf_op jit(solution)/shard_map/ppermute | solution.py:23
  172.3 14.3 %collective-permute-start.27 = (bf16[128,1024]{1,0:T(8,128)(2,1)S(1)}, bf16[128,1024]{1,0:T(8,128)(2,1)S(1)}, u32[]{:S(2)}, u32[]{:S(2)}) collective-permute-start(bf16[128,1024]{1,0:T(8,128)(2,1)S(1)} %get-tuple-element.47), channel_id=1, source_target_pairs={{0,5},{1,4},{4,1},{5,0},{2,7},{3,6},{6,3},{7,2},{8,13},{9,12},{12,... | collective-permute-start | bytes 786440 | tf_op jit(solution)/shard_map/ppermute | solution.py:27
  173.7 14.7 %collective-permute-start.26 = (bf16[128,1024]{1,0:T(8,128)(2,1)S(1)}, bf16[128,1024]{1,0:T(8,128)(2,1)S(1)}, u32[]{:S(2)}, u32[]{:S(2)}) collective-permute-start(bf16[128,1024]{1,0:T(8,128)(2,1)S(1)} %get-tuple-element.48), channel_id=1, source_target_pairs={{0,1},{1,0},{2,3},{3,2},{4,5},{5,4},{6,7},{7,6},{8,9},{9,8},{10,11... | collective-permute-start | bytes 786440 | tf_op jit(solution)/shard_map/ppermute | solution.py:23
  176.1 15.2 %collective-permute-start.15 = (bf16[128,1024]{1,0:T(8,128)(2,1)S(1)}, bf16[128,1024]{1,0:T(8,128)(2,1)S(1)}, u32[]{:S(2)}, u32[]{:S(2)}) collective-permute-start(bf16[128,1024]{1,0:T(8,128)(2,1)S(1)} %get-tuple-element.51), channel_id=1, source_target_pairs={{0,4},{4,0},{1,5},{5,1},{2,6},{6,2},{3,7},{7,3},{8,12},{12,8},{9,1... | collective-permute-start | bytes 786440 | tf_op jit(solution)/shard_map/ppermute | solution.py:23
  177.6 19.1 %collective-permute-start.17 = (bf16[128,1024]{1,0:T(8,128)(2,1)S(1)}, bf16[128,1024]{1,0:T(8,128)(2,1)S(1)}, u32[]{:S(2)}, u32[]{:S(2)}) collective-permute-start(bf16[128,1024]{1,0:T(8,128)(2,1)S(1)} %get-tuple-element.52), channel_id=1, source_target_pairs={{0,5},{1,4},{4,1},{5,0},{2,7},{3,6},{6,3},{7,2},{8,13},{9,12},{12,... | collective-permute-start | bytes 786440 | tf_op jit(solution)/shard_map/ppermute | solution.py:27
  180.0 18.0 %collective-permute-start.16 = (bf16[128,1024]{1,0:T(8,128)(2,1)S(1)}, bf16[128,1024]{1,0:T(8,128)(2,1)S(1)}, u32[]{:S(2)}, u32[]{:S(2)}) collective-permute-start(bf16[128,1024]{1,0:T(8,128)(2,1)S(1)} %get-tuple-element.53), channel_id=1, source_target_pairs={{0,1},{1,0},{2,3},{3,2},{4,5},{5,4},{6,7},{7,6},{8,9},{9,8},{10,11... | collective-permute-start | bytes 786440 | tf_op jit(solution)/shard_map/ppermute | solution.py:23
  201.6 18.6 %all-to-all-start.3 = ((bf16[8,128,128]{2,1,0:T(8,128)(2,1)}), bf16[8,128,128]{2,1,0:T(8,128)(2,1)}, u32[]{:S(2)}, u32[]{:S(2)}) async-start(bf16[8,128,128]{2,1,0:T(8,128)(2,1)} %bitcast.314), calls=%async_computation.3 | async-start | bytes 524288 | tf_op jit(solution)/shard_map/all_to_all | solution.py:374
  207.4 35.3 %collective-permute-start.18 = (bf16[64,1024]{1,0:T(8,128)(2,1)}, bf16[64,1024]{1,0:T(8,128)(2,1)}, u32[]{:S(2)}, u32[]{:S(2)}) collective-permute-start(bf16[64,1024]{1,0:T(8,128)(2,1)} %dynamic-slice_bitcast_fusion.9), channel_id=1, source_target_pairs={{0,2},{2,0},{1,3},{3,1},{4,6},{6,4},{5,7},{7,5},{8,10},{10,8},{9,1... | collective-permute-start | bytes 393224 | tf_op jit(solution)/shard_map/ppermute | solution.py:23
  211.7 66.7 %collective-permute-start.38 = (bf16[8,2,32,1024]{3,2,1,0:T(8,128)(2,1)}, bf16[8,2,32,1024]{3,2,1,0:T(8,128)(2,1)}, u32[]{:S(2)}, u32[]{:S(2)}) collective-permute-start(bf16[8,2,32,1024]{3,2,1,0:T(8,128)(2,1)} %dynamic-slice_bitcast_fusion), channel_id=1, source_target_pairs={{0,2},{2,0},{1,3},{3,1},{4,6},{6,4},{5,7},{7,5},{8,10},{10,8},{9,1... | collective-permute-start | bytes 3145736 | tf_op jit(solution)/shard_map/ppermute | solution.py:23
  237.7 9.3 %collective-permute-start.28 = (bf16[128,1024]{1,0:T(8,128)(2,1)S(1)}, bf16[128,1024]{1,0:T(8,128)(2,1)S(1)}, u32[]{:S(2)}, u32[]{:S(2)}) collective-permute-start(bf16[128,1024]{1,0:T(8,128)(2,1)S(1)} %get-tuple-element.35), channel_id=1, source_target_pairs={{0,4},{4,0},{1,5},{5,1},{2,6},{6,2},{3,7},{7,3},{8,12},{12,8},{9,1... | collective-permute-start | bytes 786440 | tf_op jit(solution)/shard_map/ppermute | solution.py:23
  239.2 13.4 %collective-permute-start.32 = (bf16[128,1024]{1,0:T(8,128)(2,1)S(1)}, bf16[128,1024]{1,0:T(8,128)(2,1)S(1)}, u32[]{:S(2)}, u32[]{:S(2)}) collective-permute-start(bf16[128,1024]{1,0:T(8,128)(2,1)S(1)} %get-tuple-element.37), channel_id=1, source_target_pairs={{0,4},{4,0},{1,5},{5,1},{2,6},{6,2},{3,7},{7,3},{8,12},{12,8},{9,1... | collective-permute-start | bytes 786440 | tf_op jit(solution)/shard_map/ppermute | solution.py:23
  239.8 18.5 %collective-permute-start.30 = (bf16[128,1024]{1,0:T(8,128)(2,1)S(1)}, bf16[128,1024]{1,0:T(8,128)(2,1)S(1)}, u32[]{:S(2)}, u32[]{:S(2)}) collective-permute-start(bf16[128,1024]{1,0:T(8,128)(2,1)S(1)} %get-tuple-element.38), channel_id=1, source_target_pairs={{0,4},{4,0},{1,5},{5,1},{2,6},{6,2},{3,7},{7,3},{8,12},{12,8},{9,1... | collective-permute-start | bytes 786440 | tf_op jit(solution)/shard_map/ppermute | solution.py:23
  242.7 17.9 %collective-permute-start.36 = (bf16[8,2,32,384]{3,2,0,1:T(8,128)(2,1)S(1)}, bf16[8,2,32,384]{3,2,0,1:T(8,128)(2,1)S(1)}, u32[]{:S(2)}, u32[]{:S(2)}) collective-permute-start(bf16[8,2,32,384]{3,2,0,1:T(8,128)(2,1)S(1)} %bitcast.323), channel_id=1, source_target_pairs={{0,2},{2,0},{1,3},{3,1},{4,6},{6,4},{5,7},{7,5},{8,10},{10,8},{9,1... | collective-permute-start | bytes 1179656 | tf_op jit(solution)/shard_map/ppermute | solution.py:23
  247.0 16.2 %collective-permute-start.34 = (bf16[128,1024]{1,0:T(8,128)(2,1)S(1)}, bf16[128,1024]{1,0:T(8,128)(2,1)S(1)}, u32[]{:S(2)}, u32[]{:S(2)}) collective-permute-start(bf16[128,1024]{1,0:T(8,128)(2,1)S(1)} %get-tuple-element.36), channel_id=1, source_target_pairs={{0,4},{4,0},{1,5},{5,1},{2,6},{6,2},{3,7},{7,3},{8,12},{12,8},{9,1... | collective-permute-start | bytes 786440 | tf_op jit(solution)/shard_map/ppermute | solution.py:23
  258.6 18.4 %collective-permute-start.29 = (bf16[128,1024]{1,0:T(8,128)(2,1)S(1)}, bf16[128,1024]{1,0:T(8,128)(2,1)S(1)}, u32[]{:S(2)}, u32[]{:S(2)}) collective-permute-start(bf16[128,1024]{1,0:T(8,128)(2,1)S(1)} %get-tuple-element.32), channel_id=1, source_target_pairs={{0,16},{8,24},{16,0},{24,8},{1,17},{9,25},{17,1},{25,9},{2,18},{10... | collective-permute-start | bytes 786440 | tf_op jit(solution)/shard_map/ppermute | solution.py:23
  258.7 18.3 %collective-permute-start.33 = (bf16[128,1024]{1,0:T(8,128)(2,1)S(1)}, bf16[128,1024]{1,0:T(8,128)(2,1)S(1)}, u32[]{:S(2)}, u32[]{:S(2)}) collective-permute-start(bf16[128,1024]{1,0:T(8,128)(2,1)S(1)} %get-tuple-element.33), channel_id=1, source_target_pairs={{0,8},{8,0},{16,24},{24,16},{1,9},{9,1},{17,25},{25,17},{2,10},{10... | collective-permute-start | bytes 786440 | tf_op jit(solution)/shard_map/ppermute | solution.py:23
  260.6 16.4 %collective-permute-start.31 = (bf16[128,1024]{1,0:T(8,128)(2,1)S(1)}, bf16[128,1024]{1,0:T(8,128)(2,1)S(1)}, u32[]{:S(2)}, u32[]{:S(2)}) collective-permute-start(bf16[128,1024]{1,0:T(8,128)(2,1)S(1)} %get-tuple-element.34), channel_id=1, source_target_pairs={{0,24},{8,16},{16,8},{24,0},{1,25},{9,17},{17,9},{25,1},{2,26},{10... | collective-permute-start | bytes 786440 | tf_op jit(solution)/shard_map/ppermute | solution.py:23
  263.2 20.3 %collective-permute-start.37 = (bf16[8,32,384]{2,1,0:T(8,128)(2,1)S(1)}, bf16[8,32,384]{2,1,0:T(8,128)(2,1)S(1)}, u32[]{:S(2)}, u32[]{:S(2)}) collective-permute-start(bf16[8,32,384]{2,1,0:T(8,128)(2,1)S(1)} %dynamic-slice_bitcast_fusion.7), channel_id=1, source_target_pairs={{0,1},{1,0},{2,3},{3,2},{4,5},{5,4},{6,7},{7,6},{8,9},{9,8},{10,11... | collective-permute-start | bytes 589832 | tf_op jit(solution)/shard_map/ppermute | solution.py:23
  278.3 13.1 %collective-permute-start.35 = (f32[64,1024]{1,0:T(8,128)}, f32[64,1024]{1,0:T(8,128)}, u32[]{:S(2)}, u32[]{:S(2)}) collective-permute-start(f32[64,1024]{1,0:T(8,128)} %dynamic-slice_bitcast_fusion.2), channel_id=1, source_target_pairs={{0,2},{2,0},{1,3},{3,1},{4,6},{6,4},{5,7},{7,5},{8,10},{10,8},{9,1... | collective-permute-start | bytes 786440 | tf_op jit(solution)/shard_map/ppermute | solution.py:23
  281.0 14.4 %collective-permute-start.39 = (bf16[8,32,1024]{2,1,0:T(8,128)(2,1)S(1)}, bf16[8,32,1024]{2,1,0:T(8,128)(2,1)S(1)}, u32[]{:S(2)}, u32[]{:S(2)}) collective-permute-start(bf16[8,32,1024]{2,1,0:T(8,128)(2,1)S(1)} %dynamic-slice_bitcast_fusion.1), channel_id=1, source_target_pairs={{0,1},{1,0},{2,3},{3,2},{4,5},{5,4},{6,7},{7,6},{8,9},{9,8},{10,11... | collective-permute-start | bytes 1572872 | tf_op jit(solution)/shard_map/ppermute | solution.py:23
  284.2 15.6 %all-to-all-start.4 = ((bf16[8,32,384]{2,1,0:T(8,128)(2,1)}), bf16[8,32,384]{2,1,0:T(8,128)(2,1)S(1)}, u32[]{:S(2)}, u32[]{:S(2)}) async-start(bf16[8,32,384]{2,1,0:T(8,128)(2,1)} %fusion.36), calls=%async_computation.4 | async-start | bytes 393216 | tf_op jit(solution)/shard_map/all_to_all | solution.py:398
  295.7 11.2 %collective-permute-start.40 = (bf16[32,1024]{1,0:T(8,128)(2,1)S(1)}, bf16[32,1024]{1,0:T(8,128)(2,1)S(1)}, u32[]{:S(2)}, u32[]{:S(2)}) collective-permute-start(bf16[32,1024]{1,0:T(8,128)(2,1)S(1)} %get-tuple-element.67), channel_id=1, source_target_pairs={{0,4},{4,0},{1,5},{5,1},{2,6},{6,2},{3,7},{7,3},{8,12},{12,8},{9,1... | collective-permute-start | bytes 196616 | tf_op jit(solution)/shard_map/ppermute | solution.py:23
  297.0 9.9 %collective-permute-start.44 = (bf16[32,1024]{1,0:T(8,128)(2,1)S(1)}, bf16[32,1024]{1,0:T(8,128)(2,1)S(1)}, u32[]{:S(2)}, u32[]{:S(2)}) collective-permute-start(bf16[32,1024]{1,0:T(8,128)(2,1)S(1)} %get-tuple-element.69), channel_id=1, source_target_pairs={{0,4},{4,0},{1,5},{5,1},{2,6},{6,2},{3,7},{7,3},{8,12},{12,8},{9,1... | collective-permute-start | bytes 196616 | tf_op jit(solution)/shard_map/ppermute | solution.py:23
  300.3 15.8 %collective-permute-start.46 = (bf16[32,1024]{1,0:T(8,128)(2,1)S(1)}, bf16[32,1024]{1,0:T(8,128)(2,1)S(1)}, u32[]{:S(2)}, u32[]{:S(2)}) collective-permute-start(bf16[32,1024]{1,0:T(8,128)(2,1)S(1)} %get-tuple-element.68), channel_id=1, source_target_pairs={{0,4},{4,0},{1,5},{5,1},{2,6},{6,2},{3,7},{7,3},{8,12},{12,8},{9,1... | collective-permute-start | bytes 196616 | tf_op jit(solution)/shard_map/ppermute | solution.py:23
  303.3 17.3 %all-to-all-start.5 = ((bf16[8,32,1152]{2,1,0:T(8,128)(2,1)}), bf16[8,32,1152]{2,1,0:T(8,128)(2,1)S(1)}, u32[]{:S(2)}, u32[]{:S(2)}) async-start(bf16[8,32,1152]{2,1,0:T(8,128)(2,1)} %bitcast.88), calls=%async_computation.6 | async-start | bytes 1179648 | tf_op jit(solution)/shard_map/all_to_all | solution.py:355
  (45 other events, 374.1 us)
Sparse Core Ops, SparseCore 0:
  11.1 70.6 all-gather.2
  99.1 51.8 all-gather.4
  168.8 50.8 reduce-scatter.1

commit v2 on v1

v2 whole, which is shorter than its diff:
```python
import functools
import math

import jax
import jax.numpy as jnp
from jax import lax
from jax.experimental import pallas as pl
from jax.experimental.pallas import tpu as pltpu
from jax.sharding import Mesh
from jax.sharding import PartitionSpec as P

HEADS = 16
norm_eps = 1e-05
rope_base = 160000.0
f32 = jnp.float32
bf16 = jnp.bfloat16
LANES = 128
MIB = 1024 * 1024


def partner(array, axis):
    return lax.ppermute(array, axis, [(0, 1), (1, 0)])


def opposite(array, axes):
    return lax.ppermute(array, axes, [(i, 3 - i) for i in range(4)])


def after(array, *others):
    return lax.optimization_barrier((array, *others))[0]


def gather_chips(block):
    far = partner(block, "zh")
    near = partner(block, "zl")
    across = partner(block, "x")
    near_across = partner(near, "x")
    both = partner(far, "zl")
    far_across = partner(far, "x")
    both_across = partner(both, "x")
    return [block, across, near, near_across, far, far_across, both, both_across]


def add(*terms):
    total = terms[0].astype(f32)
    for term in terms[1:]:
        total = total + term.astype(f32)
    return total.astype(terms[0].dtype)


def scatter_chips(terms):
    across = {j: partner(terms[j ^ 1], "x") for j in (6, 4, 2, 0)}
    both = partner(add(terms[6], across[6]), "zl")
    near = partner(add(terms[2], across[2]), "zl")
    far = partner(add(terms[4], across[4], both), "zh")
    return terms[0], across[0], near, far


def gather_square(block):
    over_x = partner(block, "x")
    over_z = partner(block, "zl")
    over_both = opposite(block, ("zl", "x"))
    here = [block, over_x, over_z, over_both]
    return here + [partner(piece, "c") for piece in here]


def scatter_square(terms):
    there = [partner(piece, "c") for piece in terms[4:]]
    over_both = opposite(add(terms[3], there[3]), ("zl", "x"))
    over_x = partner(add(terms[1], there[1]), "x")
    over_z = partner(add(terms[2], there[2]), "zl")
    return terms[0], there[0], over_x, over_z, over_both


def call(kernel, name, outs, places, *arrays, scratch=(), mib=16):
    vmem = pl.BlockSpec(memory_space=pltpu.VMEM)
    return pl.pallas_call(
        kernel,
        in_specs=[pl.BlockSpec(memory_space=pltpu.SMEM)] + [vmem] * len(arrays),
        out_specs=[vmem] * len(outs),
        out_shape=[jax.ShapeDtypeStruct(shape, dtype) for shape, dtype in outs],
        scratch_shapes=list(scratch),
        compiler_params=pltpu.CompilerParams(vmem_limit_bytes=mib * MIB),
        name=name,
    )(places, *arrays)


CHIP, ZH, ZL, X, C, Y = range(6)


def nt(left, right):
    return lax.dot_general(left, right, (((1,), (1,)), ((), ())), preferred_element_type=f32)


def tn(left, right):
    return lax.dot_general(left, right, (((0,), (0,)), ((), ())), preferred_element_type=f32)


def nn(left, right):
    return lax.dot_general(left, right, (((1,), (0,)), ((), ())), preferred_element_type=f32)


def normalize(values):
    centre = values - jnp.mean(values, axis=-1, keepdims=True)
    inverse = lax.rsqrt(jnp.mean(centre * centre, axis=-1, keepdims=True) + norm_eps)
    return centre * inverse, inverse


def normalize_back(scaled, normed, inverse):
    inner = jnp.mean(scaled * normed, axis=-1, keepdims=True)
    return inverse * (scaled - jnp.mean(scaled, axis=-1, keepdims=True) - normed * inner)


def pick_kernel(places, own_ref, other_ref, block_ref):
    half = own_ref.shape[1]
    block_ref[:half, :] = own_ref[places[C]]
    block_ref[half:, :] = other_ref[places[C]]


def enter_kernel(places, own_ref, other_ref, block_ref, low_ref):
    pick_kernel(places, own_ref, other_ref, block_ref)
    low_ref[...] = normalize(block_ref[...].astype(f32))[0].astype(bf16)


def leave_kernel(places, own_ref, other_ref, out_ref):
    out_ref[places[C]] = own_ref[...]
    out_ref[1 - places[C]] = other_ref[...]


def assemble_kernel(lead, first, second, places, a_ref, b_ref, c_ref, d_ref, out_ref):
    chip = places[lead] if lead is not None else 0
    one, two = places[first], places[second]
    for i, row in enumerate(((a_ref, b_ref), (c_ref, d_ref))):
        for j, ref in enumerate(row):
            for at in range(ref.shape[0]):
                out_ref[chip ^ at, one ^ i, :, two ^ j] = ref[at]


def assemble(places, lead, first, second, pieces):
    extent = pieces[0].shape
    shape = (extent[0], 2, extent[1], 2) + extent[2:]
    if extent[2] % 16 == 0:
        kernel = functools.partial(assemble_kernel, lead, first, second)
        return call(kernel, "assemble", [(shape, bf16)], places, *pieces)[0]

    def ordered(own, other, place, axis):
        straight = jnp.stack([own, other], axis)
        return jnp.where(place == 0, straight, jnp.flip(straight, axis))

    one = ordered(pieces[0], pieces[1], places[second], 2)
    two = ordered(pieces[2], pieces[3], places[second], 2)
    whole = ordered(one, two, places[first], 1)
    if lead is None:
        return whole
    return jnp.take(whole, jnp.arange(extent[0]) ^ places[lead], axis=0)


def split_kernel(which, count, places, *refs):
    kept_ref, sent_ref = refs[count:]
    place = places[which]
    for ref, at in ((kept_ref, place), (sent_ref, 1 - place)):
        total = refs[0][:, at]
        if count > 1:
            total = total.astype(f32)
            for term in refs[1:count]:
                total = total + term[:, at].astype(f32)
        ref[...] = total.astype(bf16)


def split(places, which, parts, before):
    shape = parts[0].shape
    rest = shape[:before] + shape[before + 1 :]
    if shape[-2] % 16 == 0:
        flat = (math.prod(shape[:before]), 2, math.prod(shape[before + 1 : -1]), shape[-1])
        outs = [((flat[0],) + flat[2:], bf16)] * 2
        kernel = functools.partial(split_kernel, which, len(parts))
        halves = call(kernel, "split", outs, places, *[part.reshape(flat) for part in parts])
        return [half.reshape(rest) for half in halves]
    total = add(*parts)
    return [
        lax.dynamic_index_in_dim(total, at, before, False)
        for at in (places[which], 1 - places[which])
    ]


def halve(places, parts, steps):
    for name, which, before in steps:
        kept, sent = split(places, which, parts, before)
        parts = [kept, partner(sent, name)]
    return parts


def halves_swapped(values, half):
    lane = lax.broadcasted_iota(jnp.int32, values.shape, 1)
    up = pltpu.roll(values, half, 1)
    down = pltpu.roll(values, values.shape[1] - half, 1)
    return jnp.where(lane % (2 * half) < half, down, up)


def project_kernel(half, places, *refs):
    pieces, (weight_ref, cos_ref, sin_ref, q_ref, k_ref, v_ref) = refs[:8], refs[8:]
    width = q_ref.shape[1]
    rows = pieces[0].shape[0]
    for at in range(0, 8, 2):
        here = pl.ds(at * rows, 2 * rows)
        made = nn(jnp.concatenate([pieces[at][...], pieces[at + 1][...]]), weight_ref[...])
        cosine, sine = cos_ref[here, :], sin_ref[here, :]
        for place, ref in ((0, q_ref), (1, k_ref)):
            part = made[:, place * width : (place + 1) * width]
            ref[here, :] = (part * cosine + halves_swapped(part, half) * sine).astype(bf16)
        v_ref[here, :] = made[:, 2 * width :].astype(bf16)


def of_head(values, head, size):
    lane = lax.broadcasted_iota(jnp.int32, values.shape, 1)
    return jnp.where(lane // size == head, values, jnp.zeros_like(values))


def attend_kernel(size, places, q_ref, k_ref, v_ref, o_ref, log_ref):
    keys, values = k_ref[...], v_ref[...]
    block = o_ref.shape[1]
    step = log_ref.shape[2]
    scale = math.log2(math.e) / math.sqrt(size)

    def visit(i, carry):
        queries = q_ref[pl.ds(pl.multiple_of(i * step, step), step), :]
        outs = []
        for head in range(q_ref.shape[1] // size):
            scores = nt(keys, of_head(queries, head, size))
            top = jnp.max(scores, axis=0, keepdims=True)
            weights = jnp.exp2((scores - top) * scale)
            total = jnp.sum(weights, axis=0, keepdims=True)
            probs = (weights * (1.0 / total)).astype(bf16)
            outs.append(tn(values, probs)[head * size : (head + 1) * size])
            log_ref[i, head : head + 1, :] = top * scale + jnp.log2(total)
        out = jnp.transpose(jnp.concatenate(outs, axis=0)).astype(bf16)
        for at in range(step // block):
            chip = places[CHIP] ^ (i * (step // block) + at)
            o_ref[chip] = out[at * block : (at + 1) * block]
        return carry

    lax.fori_loop(0, q_ref.shape[0] // step, visit, 0)


def attend_back_kernel(
    size, together, places, q_ref, k_ref, v_ref, grad_ref, log_ref, cos_ref, sin_ref, dq_ref, dk_ref, dv_ref
):
    keys, values = k_ref[...], v_ref[...]
    block, width = grad_ref.shape[1:]
    step = log_ref.shape[2]
    scale = 1.0 / math.sqrt(size)
    exponent = scale * math.log2(math.e)
    dk_ref[...] = jnp.zeros_like(dk_ref)
    dv_ref[...] = jnp.zeros_like(dv_ref)

    def turned(part, here):
        back = halves_swapped(part, size // 2) * sin_ref[here, :]
        return (part * cos_ref[here, :] - back).astype(bf16)

    def visit(i, carry):
        here = pl.ds(pl.multiple_of(i * step, step), step)
        queries = q_ref[here, :]
        grads = [grad_ref[places[CHIP] ^ (i * (step // block) + at)] for at in range(step // block)]
        grads = jnp.concatenate(grads)
        outs = []
        for head in range(width // size):
            query, grad = of_head(queries, head, size), of_head(grads, head, size)
            probs = jnp.exp2(nt(keys, query) * exponent - log_ref[i, head : head + 1, :])
            grad_probs = nt(values, grad)
            delta = jnp.sum(probs * grad_probs, axis=0, keepdims=True)
            grad_scores = (probs * (grad_probs - delta)).astype(bf16)
            outs.append(tn(keys, grad_scores)[head * size : (head + 1) * size])
            dk_ref[...] += nn(grad_scores, query)
            dv_ref[...] += nn(probs.astype(bf16), grad)
        dq = jnp.transpose(jnp.concatenate(outs, axis=0)) * scale
        dq_ref[here, :width] = turned(dq, here)
        return carry

    lax.fori_loop(0, q_ref.shape[0] // step, visit, 0)
    if together:
        everything = pl.ds(0, q_ref.shape[0])
        dq_ref[:, width : 2 * width] = turned(dk_ref[...] * scale, everything)
        dq_ref[:, 2 * width :] = dv_ref[...].astype(bf16)
    else:
        dk_ref[...] = dk_ref[...] * scale


def turn_back_kernel(half, places, dq_ref, dk_ref, dv_ref, cos_ref, sin_ref, out_ref):
    width = dq_ref.shape[1]
    part = dk_ref[...]
    back = halves_swapped(part, half) * sin_ref[...]
    out_ref[:, :width] = dq_ref[...]
    out_ref[:, width : 2 * width] = (part * cos_ref[...] - back).astype(bf16)
    out_ref[:, 2 * width :] = dv_ref[...].astype(bf16)


def middle_kernel(places, arrived_ref, weight_ref, tokens_ref, attended_ref, middle_ref, low_ref):
    wide = arrived_ref.shape[2]
    for at in range(arrived_ref.shape[0]):
        attended_ref[:, at * wide : (at + 1) * wide] = arrived_ref[at]
    middle = tokens_ref[...].astype(f32) + nn(attended_ref[...], weight_ref[...])
    middle_ref[...] = middle
    low_ref[...] = normalize(middle)[0].astype(bf16)


def feed_kernel(places, *refs):
    two, cot, w_ref, (hidden_ref, grad_ref), outs = refs[:8], refs[8:16], refs[16], refs[17:19], refs[19:]
    piece = hidden_ref.shape[1]
    rows = two[0].shape[0]
    w_in, w_out = w_ref[:, : 2 * piece], w_ref[:, 2 * piece :]
    for at in (4, 6, 0, 2):
        here = pl.ds(at * rows, 2 * rows)
        gate_up = nn(jnp.concatenate([two[at][...], two[at + 1][...]]), w_in)
        grad_hidden = nn(jnp.concatenate([cot[at][...], cot[at + 1][...]]), w_out)
        gate, lift = gate_up[:, :piece], gate_up[:, piece:]
        cdf = 0.5 * (1.0 + lax.erf(gate * math.sqrt(0.5)))
        density = jnp.exp(-0.5 * gate * gate) * (1.0 / math.sqrt(2.0 * math.pi))
        activated = gate * cdf
        hidden_ref[here, :] = (activated * lift).astype(bf16)
        grad_gate = (grad_hidden * lift * (cdf + gate * density)).astype(bf16)
        grad_lift = (grad_hidden * activated).astype(bf16)
        grad_ref[here, :piece] = grad_gate
        grad_ref[here, piece:] = grad_lift
        made = nt(grad_gate, w_in[:, :piece]) + nt(grad_lift, w_in[:, piece:])
        made = made.astype(bf16)
        outs[at][...] = made[:rows]
        outs[at + 1][...] = made[rows:]


def feed(places, two, cot, weights):
    rows, width = two[0].shape
    piece = weights.shape[1] // 3
    outs = [((8 * rows, piece), bf16), ((8 * rows, 2 * piece), bf16)] + [((rows, width), bf16)] * 8
    hidden, grads, *terms = call(feed_kernel, "feed", outs, places, *two, *cot, weights, mib=24)
    return hidden, grads, terms


def feed_rest_kernel(places, *refs):
    two, cot, (hidden_ref, grad_ref, w_ref, out_ref), outs = refs[:8], refs[8:16], refs[16:20], refs[20:]
    piece = hidden_ref.shape[1]
    rows, width = two[0].shape
    w_out = w_ref[:, 2 * piece :]
    for at in (4, 6, 0, 2):
        made = nt(hidden_ref[pl.ds(at * rows, 2 * rows), :], w_out).astype(bf16)
        outs[at][...] = made[:rows]
        outs[at + 1][...] = made[rows:]
    step = width // 4
    for at in range(0, width, step):
        here = pl.ds(at, step)
        left = jnp.concatenate([ref[:, here] for ref in two])
        out_ref[here, : 2 * piece] = tn(left, grad_ref[...]).astype(bf16)
        left = jnp.concatenate([ref[:, here] for ref in cot])
        out_ref[here, 2 * piece :] = tn(left, hidden_ref[...]).astype(bf16)


def feed_rest(places, two, cot, hidden, grads, weights):
    rows, width = two[0].shape
    outs = [(weights.shape, bf16)] + [((rows, width), bf16)] * 8
    made, *terms = call(
        feed_rest_kernel, "feed_rest", outs, places, *two, *cot, hidden, grads, weights, mib=24
    )
    return made, terms


def result_kernel(places, middle_ref, a_ref, b_ref, c_ref, d_ref, e_ref, kept_ref, sent_ref):
    total = middle_ref[...]
    for ref in (a_ref, b_ref, c_ref, d_ref, e_ref):
        total = total + ref[...].astype(f32)
    total = total.astype(bf16)
    half = kept_ref.shape[0]
    kept_ref[...] = total[:half]
    sent_ref[...] = total[half:]


def middle_back_kernel(
    places, middle_ref, cot_ref, weight_ref, a_ref, b_ref, c_ref, d_ref, e_ref, grad_ref, low_ref, leaving_ref
):
    scaled = a_ref[...].astype(f32)
    for ref in (b_ref, c_ref, d_ref, e_ref):
        scaled = scaled + ref[...].astype(f32)
    normed, inverse = normalize(middle_ref[...])
    grad = cot_ref[...].astype(f32) + normalize_back(scaled, normed, inverse)
    grad_ref[...] = grad
    low = grad.astype(bf16)
    low_ref[...] = low
    made = nt(low, weight_ref[...]).astype(bf16)
    wide = leaving_ref.shape[2]
    for at in range(leaving_ref.shape[0]):
        leaving_ref[at] = made[:, at * wide : (at + 1) * wide]


def outer_kernel(places, left_ref, right_ref, out_ref):
    out_ref[...] = tn(left_ref[...], right_ref[...]).astype(bf16)


def project_back_kernel(places, grad_ref, weight_ref, *outs):
    rows = outs[0].shape[0]
    for at in (6, 4, 2, 0):
        made = nt(grad_ref[pl.ds(at * rows, 2 * rows), :], weight_ref[...]).astype(bf16)
        outs[at][...] = made[:rows]
        outs[at + 1][...] = made[rows:]


def project_outer_kernel(places, *refs):
    pieces, grad_ref, out_ref = refs[:8], refs[8], refs[9]
    width = pieces[0].shape[1]
    step = width // 4
    for at in range(0, width, step):
        left = jnp.concatenate([ref[:, pl.ds(at, step)] for ref in pieces])
        out_ref[pl.ds(at, step), :] = tn(left, grad_ref[...]).astype(bf16)


def tokens_back_kernel(places, tokens_ref, grad_ref, a_ref, b_ref, c_ref, d_ref, kept_ref, sent_ref):
    scaled = a_ref[...].astype(f32)
    for ref in (b_ref, c_ref, d_ref):
        scaled = scaled + ref[...].astype(f32)
    normed, inverse = normalize(tokens_ref[...].astype(f32))
    total = grad_ref[...] + normalize_back(scaled, normed, inverse)
    half = kept_ref.shape[0]
    kept_ref[...] = total[:half]
    sent_ref[...] = total[half:]


def columns_by(array, pieces, piece):
    rows, count = array.shape
    padded = jnp.pad(array, ((0, 0), (0, pieces * piece - count)))
    return jnp.swapaxes(padded.reshape(rows, pieces, piece), 0, 1)


def columns_back(array, count):
    pieces, rows, piece = array.shape
    return jnp.swapaxes(array, 0, 1).reshape(rows, pieces * piece)[:, :count]


def body(inputs, gain_attn, gain_mlp, w_qkv, w_attn_out, w_in, w_out, cotangent):
    pairs, squares = 8, 8
    rings = lax.axis_size("r")
    seqs, half_block, width = inputs.shape
    owned = w_qkv.shape[0]
    size = width // HEADS
    half = size // 2
    wide = width // pairs
    block = seqs * half_block
    span = pairs * block
    ff = w_out.shape[0]
    piece = -(-ff // (squares * LANES)) * LANES
    chips, square = ("zh", "zl", "x"), ("zl", "x", "c")
    ri, zh, zl, xi, ci, yi = (lax.axis_index(name) for name in ("r", "zh", "zl", "x", "c", "y"))
    places = jnp.stack([4 * zh + 2 * zl + xi, zh, zl, xi, ci, yi]).astype(jnp.int32)
    block_low, half_low = ((block, width), bf16), ((half_block, width), bf16)
    block_full, half_full = ((block, width), f32), ((half_block, width), f32)

    def over_rings(array):
        return lax.all_gather(array, "r", axis=0) if rings > 1 else array

    def ring_sums(array):
        if rings > 1:
            return lax.psum_scatter(array, "r", scatter_dimension=0, tiled=True)
        return array

    gain_one = gain_attn.astype(f32)[:, None]
    gain_two = gain_mlp.astype(f32)[:, None]

    tokens, low_one = call(
        enter_kernel, "enter", [block_low, block_low], places, inputs, partner(inputs, "c")
    )
    all_one = gather_chips(low_one)

    scaled_qkv = (w_qkv.astype(f32) * gain_one).astype(bf16)
    part = scaled_qkv.reshape(owned, 3, pairs, wide).transpose(2, 0, 1, 3)
    part = part.reshape(pairs, owned, 3 * wide)
    part = lax.all_to_all(part, chips, 0, 0, tiled=True)[:, None]
    part = [part, partner(part, "y")]
    part = part + [partner(member, "c") for member in part]
    pair_qkv = over_rings(assemble(places, None, C, Y, part)).reshape(width, 3 * wide)

    scaled_in = (w_in.astype(f32) * gain_two).astype(bf16)
    packed = jnp.concatenate(
        [
            columns_by(scaled_in[:, :ff], squares, piece),
            columns_by(scaled_in[:, ff:], squares, piece),
            columns_by(jnp.transpose(w_out), squares, piece),
        ],
        axis=2,
    )
    packed = lax.all_to_all(after(packed, low_one), square, 0, 0, tiled=True)[None]
    far = partner(packed, "zh")
    packed = [packed, partner(packed, "y"), far, partner(far, "y")]
    weights = over_rings(assemble(places, None, ZH, Y, packed)).reshape(width, 3 * piece)

    full = after(w_attn_out, low_one)
    full = jnp.stack([full, partner(full, "zh")])
    full = jnp.stack([full, partner(full, "zl")], axis=1)
    full = jnp.stack([full, partner(full, "x")], axis=2).reshape(8, 1, owned, width)
    full = [full, partner(full, "y")]
    full = full + [partner(member, "c") for member in full]
    full_attn = over_rings(assemble(places, CHIP, C, Y, full)).reshape(width, width)

    cotangent_here = call(
        pick_kernel, "pick", [block_low], places, cotangent, partner(cotangent, "c")
    )[0]
    all_cotangent = gather_square(after(cotangent_here, all_one[7]))

    chip_at = (places[CHIP] ^ jnp.arange(pairs, dtype=jnp.int32))[:, None, None]
    core_at = (ci ^ jnp.arange(2, dtype=jnp.int32))[None, :, None]
    at = jnp.arange(half_block, dtype=jnp.int32)[None, None, :]
    at = (ri * span + chip_at * block + core_at * half_block + at).reshape(span)
    frequency = rope_base ** (-2.0 * jnp.arange(half, dtype=jnp.int32).astype(f32) / size)
    angles = at.astype(f32)[:, None] * frequency[None, :]
    cosine = jnp.tile(jnp.cos(angles), (1, wide // half))
    sine = jnp.sin(angles)
    sine = jnp.tile(jnp.concatenate([-sine, sine], axis=1), (1, wide // size))
    queries, keys, values = call(
        functools.partial(project_kernel, half),
        "project",
        [((span, wide), bf16)] * 3,
        places,
        *all_one,
        pair_qkv,
        cosine,
        sine,
    )
    if rings > 1:
        keys = lax.all_gather(keys, "r", axis=0, tiled=True)
        values = lax.all_gather(values, "r", axis=0, tiled=True)
    count = keys.shape[0]
    step = 2 * block if count <= 2048 else block
    heads_out, logs = call(
        functools.partial(attend_kernel, size),
        "attend",
        [((pairs, block, wide), bf16), ((span // step, 8, step), f32)],
        places,
        queries,
        keys,
        values,
        mib=24,
    )
    arrived = lax.all_to_all(heads_out, chips, 0, 0, tiled=True)
    attended, middle, low_two = call(
        middle_kernel, "middle", [block_low, block_full, block_low], places, arrived, full_attn, tokens
    )
    all_two = gather_square(low_two)

    hidden, grad_gate_up, terms = feed(places, all_two, all_cotangent, weights)
    grad_two = scatter_square(terms)
    grad_weights, result = feed_rest(
        places, all_two, all_cotangent, hidden, grad_gate_up, weights
    )

    grad_middle, grad_branch, leaving = call(
        middle_back_kernel,
        "middle_back",
        [block_full, block_low, ((pairs, block, wide), bf16)],
        places,
        middle,
        cotangent_here,
        full_attn,
        *grad_two,
    )

    grad_heads = lax.all_to_all(leaving, chips, 0, 0, tiled=True)

    terms = ring_sums(grad_weights).reshape(2, squares, 2, owned, 3 * piece)
    terms = halve(places, [terms], [("y", Y, 2), ("zh", ZH, 0)])
    grad_packed = lax.all_to_all(add(*terms), square, 0, 0, tiled=True).astype(f32)
    grad_in = jnp.concatenate(
        [
            columns_back(grad_packed[:, :, :piece], ff),
            columns_back(grad_packed[:, :, piece : 2 * piece], ff),
        ],
        axis=1,
    )
    grad_out = jnp.transpose(columns_back(grad_packed[:, :, 2 * piece :], ff))
    grad_gain_mlp = jnp.sum(grad_in * w_in.astype(f32), axis=1)
    grad_in = grad_in * gain_two

    terms = call(outer_kernel, "outer", [((width, width), bf16)], places, attended, grad_branch)[0]
    terms = ring_sums(terms).reshape(2, 2, 2, 2, 2, owned, width)
    steps = [("c", C, 3), ("y", Y, 3), ("x", X, 2), ("zl", ZL, 1), ("zh", ZH, 0)]
    kept, sent = halve(places, [terms], steps)
    grad_attn = kept.astype(f32) + sent.astype(f32)

    result = [after(result[0], grad_heads)] + result[1:]
    kept, sent = call(
        result_kernel, "result", [half_low] * 2, places, middle, *scatter_square(result)
    )
    output = call(
        leave_kernel, "leave", [(inputs.shape, bf16)], places, kept, partner(sent, "c")
    )[0]

    parts = [queries, keys, values, grad_heads, logs, cosine, sine]
    kernel = functools.partial(attend_back_kernel, size, rings == 1)
    if rings == 1:
        grad_projected = call(
            kernel,
            "attend_back",
            [((span, 3 * wide), bf16)],
            places,
            *parts,
            scratch=[pltpu.VMEM((count, wide), f32)] * 2,
            mib=24,
        )[0]
    else:
        outs = [((span, wide), bf16), ((count, wide), f32), ((count, wide), f32)]
        grad_q, grad_k, grad_v = call(kernel, "attend_back", outs, places, *parts, mib=36)
        grad_projected = call(
            functools.partial(turn_back_kernel, half),
            "turn_back",
            [((span, 3 * wide), bf16)],
            places,
            grad_q,
            ring_sums(grad_k),
            ring_sums(grad_v),
            cosine,
            sine,
        )[0]

    terms = call(
        project_back_kernel, "project_back", [block_low] * 8, places, grad_projected, pair_qkv
    )
    kept, sent = call(
        tokens_back_kernel,
        "tokens_back",
        [half_full] * 2,
        places,
        tokens,
        grad_middle,
        *scatter_chips(terms),
    )
    input_grad = call(
        leave_kernel, "leave", [(inputs.shape, f32)], places, kept, partner(sent, "c")
    )[0]

    terms = call(
        project_outer_kernel,
        "project_outer",
        [((width, 3 * wide), bf16)],
        places,
        *all_one,
        grad_projected,
    )[0]
    terms = ring_sums(terms).reshape(pairs, 2, 2, owned, 3 * wide)
    terms = halve(places, [terms], [("c", C, 1), ("y", Y, 1)])
    terms = lax.all_to_all(add(*terms), chips, 0, 0, tiled=True).astype(f32)
    grad_qkv = terms.reshape(pairs, owned, 3, wide).transpose(1, 2, 0, 3).reshape(owned, 3 * width)
    grad_gain_attn = jnp.sum(grad_qkv * w_qkv.astype(f32), axis=1)
    grad_qkv = grad_qkv * gain_one
    return (
        output,
        input_grad,
        grad_gain_attn,
        grad_gain_mlp,
        grad_qkv,
        grad_attn,
        grad_in,
        grad_out,
    )


def solution(mesh):
    ctx, fsdp = mesh.shape["ctx"], mesh.shape["fsdp"]
    everyone = ("r", "zh", "zl", "x", "c", "y")
    grid = Mesh(mesh.devices.reshape(ctx // 16, 2, 2, 2, 2, fsdp), everyone)
    tokens = P("y", everyone[:-1], None)
    gain, rows, columns = P(everyone), P(everyone, None), P(None, everyone)
    return jax.shard_map(
        body,
        mesh=grid,
        in_specs=(tokens, gain, gain, rows, rows, rows, columns, tokens),
        out_specs=(tokens, tokens, gain, gain, rows, rows, rows, columns),
        check_vma=False,
    )
```

time: 332 us -> 294 us (0.89)
  Pallas kernels: 21.7 us -> 62.6 us
  waiting for transfers between devices: 120 us -> 98.3 us
  matrix products: 19.5 us -> 0 us
  other arithmetic: 35.9 us -> 19.7 us
  between operations: 14.9 us -> 1.81 us
  local copies, waits for them, and re-layouts: 33.2 us -> 26.6 us
    pallas_call x4 -> x28, Pallas kernels: 21.7 us -> 62.6 us  [call(): pl.pallas_call(kernel, in_specs=[pl.BlockSpec(memory_space=pltpu.SMEM)] +...]
    dot_general x11 -> x0, matrix products: 19.5 us -> none  [the longest x5 7.28 us: nt(): lax.dot_general(left, right, (((1,), (1,)), ((), ())), preferred_element_...]
    another operation x16 -> x3, other arithmetic: 16.6 us -> 0.1 us  [the longest x2 0.09 us: body(): jnp.stack([full, partner(full, 'x')], axis=2).reshape(8, 1, owned, width)]
    unnamed x79 -> x156, local copies, waits for them, and re-layouts: 10.9 us -> 22.6 us
    all_gather x2 -> x0, waiting for transfers between devices: 11.5 us -> none  [the longest x1 11.5 us: body(): packed = lax.all_gather(packed, ('r', 'z'), axis=0, tiled=True)]
    all_to_all x6, waiting for transfers between devices: 12.1 us -> 3.94 us  [the longest x1 2.02 us: body(): grad_heads = lax.all_to_all(leaving, chips, 0, 0, tiled=True)]
    squeeze x11 -> x0, local copies, waits for them, and re-layouts: 6.14 us -> none  [the longest x4 4.79 us: core_swap(): sent = lax.dynamic_index_in_dim(array, 1 - place, 0, False)]
    dynamic_update_slice x7 -> x0, local copies, waits for them, and re-layouts: 3.97 us -> none  [the longest x3 2.93 us: gather_chips(): lax.dynamic_update_slice(whole, piece[None, None], (zi ^ j, xi) + rest)]
  transfers between devices with their start and end apart: 56 -> 73, of which waited for: 24 -> 23; matrix products, arithmetic and copies ran while one was open for 19% -> 7% of each run, Pallas kernels for 7% -> 19%
where the time goes in v2:
time: 294 us; the launch traced here: 292 us
  waiting for transfers between devices  98.3 us (33%)
  starting transfers between devices  83 us (28%)
  Pallas kernels  62.6 us (21%)
  local copies, waits for them, and re-layouts  26.6 us (9%)
  other arithmetic  19.7 us (7%)
    ppermute x63, waiting for transfers between devices, partner(): return lax.ppermute(array, axis, [(0, 1), (1, 0)])  83.7 us
    pallas_call x28, Pallas kernels, call(): pl.pallas_call(kernel, in_specs=[pl.BlockSpec(memory_space=pltpu.SMEM)] +...  62.6 us
    ppermute x63, starting transfers between devices, partner(): return lax.ppermute(array, axis, [(0, 1), (1, 0)])  46.8 us
    unnamed x156, local copies, waits for them, and re-layouts  22.6 us
    ppermute x4, waiting for transfers between devices, opposite(): return lax.ppermute(array, axes, [(i, 3 - i) for i in range(4)])  10.6 us
    convert_element_type x11, other arithmetic, add(): return total.astype(terms[0].dtype)  10.5 us
    ppermute x4, starting transfers between devices, opposite(): return lax.ppermute(array, axes, [(i, 3 - i) for i in range(4)])  7.18 us
    all_to_all x1, starting transfers between devices, body(): part = lax.all_to_all(part, chips, 0, 0, tiled=True)[:, None]  6.98 us
  transfers between devices with their start and end apart: 73, of which 23 were waited for; matrix products, arithmetic and copies ran while one was open for 7% of the time, Pallas kernels for 19%

profile of v2, /device:TPU:0, one launch (start us, length us, event | category | flops | bytes accessed | tf_op | source)
XLA Modules:
  0.0 292.0 jit_solution(6311503046019165510)
XLA Ops:
  3.9 7.0 %all-to-all-start = ((bf16[8,32,384]{2,1,0:T(8,128)(2,1)}), bf16[8,32,384]{2,1,0:T(8,128)(2,1)S(1)}, u32[]{:S(2)}, u32[]{:S(2)}) async-start(bf16[8,32,384]{2,1,0:T(8,128)(2,1)} %reshape.213), calls=%async_computation | async-start | bytes 393216 | tf_op jit(solution)/shard_map/all_to_all | solution.py:472
  12.6 3.0 %collective-permute-start.11 = (bf16[32,1024]{1,0:T(8,128)(2,1)S(1)}, bf16[32,1024]{1,0:T(8,128)(2,1)S(1)}, u32[]{:S(2)}, u32[]{:S(2)}) collective-permute-start(bf16[32,1024]{1,0:T(8,128)(2,1)S(1)} %copy-done.74), channel_id=1, source_target_pairs={{0,16},{16,0},{1,17},{17,1},{2,18},{18,2},{3,19},{19,3},{4,20},{20... | collective-permute-start | bytes 196616 | tf_op jit(solution)/shard_map/ppermute | solution.py:22
  16.3 11.8 %collective-permute-done.11 = bf16[32,1024]{1,0:T(8,128)(2,1)S(1)} collective-permute-done((bf16[32,1024]{1,0:T(8,128)(2,1)S(1)}, bf16[32,1024]{1,0:T(8,128)(2,1)S(1)}, u32[]{:S(2)}, u32[]{:S(2)}) %collective-permute-start.11) | collective-permute-done | bytes 65568 | tf_op jit(solution)/shard_map/ppermute | solution.py:22
  29.1 4.4 %all-to-all-start.2 = ((bf16[8,32,1152]{2,1,0:T(8,128)(2,1)}), bf16[8,32,1152]{2,1,0:T(8,128)(2,1)}, u32[]{:S(2)}, u32[]{:S(2)}) async-start(bf16[8,32,1152]{2,1,0:T(8,128)(2,1)} %pad_maximum_fusion.1), calls=%async_computation.2 | async-start | bytes 1179648 | tf_op jit(solution)/shard_map/all_to_all | solution.py:486
  33.4 2.4 collective-permute-done.12
  37.4 2.0 collective-permute-start.6
  40.0 9.1 %collective-permute-done.13 = bf16[2,2,32,1024]{3,2,0,1:T(8,128)(2,1)S(1)} collective-permute-done((bf16[2,2,32,1024]{3,2,0,1:T(8,128)(2,1)S(1)}, bf16[2,2,32,1024]{3,2,0,1:T(8,128)(2,1)S(1)}, u32[]{:S(2)}, u32[]{:S(2)}) %collective-permute-start.13) | collective-permute-done | bytes 262176 | tf_op jit(solution)/shard_map/ppermute | solution.py:22
  52.1 2.1 collective-permute-done.6.refs_6_
  60.4 3.0 %collective-permute-done.7.refs_7_ = bf16[128,1024]{1,0:T(8,128)(2,1)S(1)} collective-permute-done((bf16[128,1024]{1,0:T(8,128)(2,1)S(1)}, bf16[128,1024]{1,0:T(8,128)(2,1)S(1)}, u32[]{:S(2)}, u32[]{:S(2)}) %collective-permute-start.7) | collective-permute-done | bytes 262176 | tf_op jit(solution)/shard_map/ppermute | solution.py:22
  71.7 2.9 %collective-permute-done.3.refs_3_ = bf16[128,1024]{1,0:T(8,128)(2,1)S(1)} collective-permute-done((bf16[128,1024]{1,0:T(8,128)(2,1)S(1)}, bf16[128,1024]{1,0:T(8,128)(2,1)S(1)}, u32[]{:S(2)}, u32[]{:S(2)}) %collective-permute-start.3) | collective-permute-done | bytes 262176 | tf_op jit(solution)/shard_map/ppermute | solution.py:22
  75.8 2.6 collective-permute-start.27
  84.8 1.9 project.1
  86.7 8.5 %attend.1 = (bf16[8,128,128]{2,1,0:T(8,128)(2,1)}, f32[4,8,256]{2,1,0:T(8,128)S(1)}) custom-call(s32[6]{0:T(128)S(1)} %stack.54.places, bf16[1024,128]{1,0:T(8,128)(2,1)S(1)} %get-tuple-element.75.q_ref, bf16[1024,128]{1,0:T(8,128)(2,1)S(1)} %get-tuple-element.76.k_ref, bf16[1024,128]{1,0:T(8,128)(2,1)S(1)} %get-tuple-element.77.v_ref), custom_call_target="tpu_custom_call" | custom-call | tf_op jit(solution)/shard_map/attend/pallas_call | solution.py:77
  95.9 4.2 %all-to-all-start.1 = ((bf16[8,128,128]{2,1,0:T(8,128)(2,1)}), bf16[8,128,128]{2,1,0:T(8,128)(2,1)}, u32[]{:S(2)}, u32[]{:S(2)}) async-start(bf16[8,128,128]{2,1,0:T(8,128)(2,1)} %get-tuple-element.78), calls=%async_computation.1 | async-start | bytes 524288 | tf_op jit(solution)/shard_map/all_to_all | solution.py:538
  106.3 1.9 all-to-all-done.1.arrived_ref
  113.0 2.0 collective-permute-start.19
  115.0 1.8 collective-permute-done.32.b_ref
  116.8 3.0 %collective-permute-done.17.refs_1_ = bf16[128,1024]{1,0:T(8,128)(2,1)S(1)} collective-permute-done((bf16[128,1024]{1,0:T(8,128)(2,1)S(1)}, bf16[128,1024]{1,0:T(8,128)(2,1)S(1)}, u32[]{:S(2)}, u32[]{:S(2)}) %collective-permute-start.17) | collective-permute-done | bytes 262176 | tf_op jit(solution)/shard_map/ppermute | solution.py:22
  120.8 4.3 %collective-permute-done.19.refs_3_ = bf16[128,1024]{1,0:T(8,128)(2,1)S(1)} collective-permute-done((bf16[128,1024]{1,0:T(8,128)(2,1)S(1)}, bf16[128,1024]{1,0:T(8,128)(2,1)S(1)}, u32[]{:S(2)}, u32[]{:S(2)}) %collective-permute-start.19) | collective-permute-done | bytes 262176 | tf_op jit(solution)/shard_map/ppermute | solution.py:26
  125.6 1.8 assemble.5
  127.4 6.8 %feed.1 = (bf16[1024,384]{1,0:T(8,128)(2,1)S(1)}, bf16[1024,768]{1,0:T(8,128)(2,1)S(1)}, bf16[128,1024]{1,0:T(8,128)(2,1)S(1)}, bf16[128,1024]{1,0:T(8,128)(2,1)...) custom-call(s32[6]{0:T(128)S(1)} %stack.54.places, ...), custom_call_target="tpu_custom_call" | custom-call | tf_op jit(solution)/shard_map/feed/pallas_call | solution.py:77
  135.4 5.7 %feed_rest.1 = (bf16[1024,1152]{1,0:T(8,128)(2,1)S(1)}, bf16[128,1024]{1,0:T(8,128)(2,1)S(1)}, bf16[128,1024]{1,0:T(8,128)(2,1)S(1)}, bf16[128,1024]{1,0:T(8,128...) custom-call(s32[6]{0:T(128)S(1)} %stack.54.places, ...), custom_call_target="tpu_custom_call" | custom-call | tf_op jit(solution)/shard_map/feed_rest/pallas_call | solution.py:77
  141.1 1.8 split.11
  144.6 2.6 collective-permute-start.41
  148.4 6.3 %collective-permute-done.41.e_ref = bf16[128,1024]{1,0:T(8,128)(2,1)S(1)} collective-permute-done((bf16[128,1024]{1,0:T(8,128)(2,1)S(1)}, bf16[128,1024]{1,0:T(8,128)(2,1)S(1)}, u32[]{:S(2)}, u32[]{:S(2)}) %collective-permute-start.41) | collective-permute-done | bytes 262176 | tf_op jit(solution)/shard_map/ppermute | solution.py:26
  154.8 4.6 %collective-permute-done.39.d_ref = bf16[128,1024]{1,0:T(8,128)(2,1)S(1)} collective-permute-done((bf16[128,1024]{1,0:T(8,128)(2,1)S(1)}, bf16[128,1024]{1,0:T(8,128)(2,1)S(1)}, u32[]{:S(2)}, u32[]{:S(2)}) %collective-permute-start.39) | collective-permute-done | bytes 262176 | tf_op jit(solution)/shard_map/ppermute | solution.py:22
  159.4 2.2 middle_back.1
  163.8 5.5 %all-to-all-start.3 = ((bf16[8,128,128]{2,1,0:T(8,128)(2,1)}), bf16[8,128,128]{2,1,0:T(8,128)(2,1)S(1)}, u32[]{:S(2)}, u32[]{:S(2)}) async-start(bf16[8,128,128]{2,1,0:T(8,128)(2,1)} %copy-done.48), calls=%async_computation.3 | async-start | bytes 524288 | tf_op jit(solution)/shard_map/all_to_all | solution.py:561
  174.7 1.8 add_convert_fusion.3
  176.4 2.0 all-to-all-done.3.grad_ref
  180.4 9.3 %attend_back.1.grad_ref.refs_8_ = bf16[1024,384]{1,0:T(8,128)(2,1)S(1)} custom-call(s32[6]{0:T(128)S(1)} %stack.54.places, bf16[1024,128]{1,0:T(8,128)(2,1)S(1)} %copy-done.9, bf16[1024,128]{1,0:T(8,128)(2,1)S(1)} %copy-done.11, bf16[1024,128]{1,0:T(8,128)(2,1)S(1)} %copy-done.13, bf16[8,128,128]{2,1,0:T(8,128)(2,1)S(1)} %all-to-all-done.3.grad_ref, ...), custom_call_target="tpu_custom_call" | custom-call | tf_op jit(solution)/shard_map/attend_back/pallas_call | solution.py:77
  189.8 2.4 project_back.1
  193.0 1.8 project_outer.1
  198.3 2.3 split.12
  201.9 1.7 add_convert_fusion.5
  209.9 1.7 collective-permute-done.59
  213.8 3.9 %all-to-all-start.4 = ((bf16[8,32,384]{2,1,0:T(8,128)(2,1)}), bf16[8,32,384]{2,1,0:T(8,128)(2,1)S(1)}, u32[]{:S(2)}, u32[]{:S(2)}) async-start(bf16[8,32,384]{2,1,0:T(8,128)(2,1)} %add_convert_fusion.9), calls=%async_computation.4 | async-start | bytes 393216 | tf_op jit(solution)/shard_map/all_to_all | solution.py:644
  217.7 14.5 %collective-permute-done.61 = bf16[8,32,1152]{2,1,0:T(8,128)(2,1)} collective-permute-done((bf16[8,32,1152]{2,1,0:T(8,128)(2,1)}, bf16[8,32,1152]{2,1,0:T(8,128)(2,1)}, u32[]{:S(2)}, u32[]{:S(2)}) %collective-permute-start.61) | collective-permute-done | bytes 589856 | tf_op jit(solution)/shard_map/ppermute | solution.py:22
  232.8 2.1 fusion
  234.8 11.4 %collective-permute-done.63 = bf16[2,2,2,32,1024]{4,3,2,1,0:T(8,128)(2,1)S(1)} collective-permute-done((bf16[2,2,2,32,1024]{4,3,2,1,0:T(8,128)(2,1)}, bf16[2,2,2,32,1024]{4,3,2,1,0:T(8,128)(2,1)S(1)}, u32[]{:S(2)}, u32[]{:S(2)}) %collective-permute-start.63) | collective-permute-done | bytes 524320 | tf_op jit(solution)/shard_map/ppermute | solution.py:22
  246.3 4.2 %all-to-all-start.5 = ((bf16[8,32,1152]{2,1,0:T(8,128)(2,1)}), bf16[8,32,1152]{2,1,0:T(8,128)(2,1)}, u32[]{:S(2)}, u32[]{:S(2)}) async-start(bf16[8,32,1152]{2,1,0:T(8,128)(2,1)} %fusion), calls=%async_computation.5 | async-start | bytes 1179648 | tf_op jit(solution)/shard_map/all_to_all | solution.py:565
  252.3 2.0 collective-permute-start.44
  255.6 1.9 collective-permute-start.50
  259.0 2.9 %collective-permute-start.56 = (bf16[128,1024]{1,0:T(8,128)(2,1)S(1)}, bf16[128,1024]{1,0:T(8,128)(2,1)S(1)}, u32[]{:S(2)}, u32[]{:S(2)}) collective-permute-start(bf16[128,1024]{1,0:T(8,128)(2,1)S(1)} %add_convert_fusion), channel_id=1, source_target_pairs={{0,16},{16,0},{1,17},{17,1},{2,18},{18,2},{3,19},{19,3},{4,20},{20... | collective-permute-start | bytes 786440 | tf_op jit(solution)/shard_map/ppermute | solution.py:22
  262.0 4.0 %collective-permute-done.44.c_ref = bf16[128,1024]{1,0:T(8,128)(2,1)S(1)} collective-permute-done((bf16[128,1024]{1,0:T(8,128)(2,1)S(1)}, bf16[128,1024]{1,0:T(8,128)(2,1)S(1)}, u32[]{:S(2)}, u32[]{:S(2)}) %collective-permute-start.44) | collective-permute-done | bytes 262176 | tf_op jit(solution)/shard_map/ppermute | solution.py:22
  267.3 4.4 %collective-permute-done.64.refs_1_ = bf16[2,2,32,1024]{3,2,1,0:T(8,128)(2,1)S(1)} collective-permute-done((bf16[2,2,32,1024]{3,2,1,0:T(8,128)(2,1)S(1)}, bf16[2,2,32,1024]{3,2,1,0:T(8,128)(2,1)S(1)}, u32[]{:S(2)}, u32[]{:S(2)}) %collective-permute-start.64) | collective-permute-done | bytes 262176 | tf_op jit(solution)/shard_map/ppermute | solution.py:22
  273.8 3.0 %collective-permute-done.50.b_ref = bf16[128,1024]{1,0:T(8,128)(2,1)S(1)} collective-permute-done((bf16[128,1024]{1,0:T(8,128)(2,1)S(1)}, bf16[128,1024]{1,0:T(8,128)(2,1)S(1)}, u32[]{:S(2)}, u32[]{:S(2)}) %collective-permute-start.50) | collective-permute-done | bytes 262176 | tf_op jit(solution)/shard_map/ppermute | solution.py:22
  280.2 3.0 %collective-permute-start.66 = (bf16[32,1024]{1,0:T(8,128)(2,1)S(1)}, bf16[32,1024]{1,0:T(8,128)(2,1)S(1)}, u32[]{:S(2)}, u32[]{:S(2)}) collective-permute-start(bf16[32,1024]{1,0:T(8,128)(2,1)S(1)} %bitcast.119), channel_id=1, source_target_pairs={{0,16},{16,0},{1,17},{17,1},{2,18},{18,2},{3,19},{19,3},{4,20},{20... | collective-permute-start | bytes 196616 | tf_op jit(solution)/shard_map/ppermute | solution.py:22
  (335 shorter events, 94.5 us)
Async XLA Ops:
  3.9 25.2 %all-to-all-start = ((bf16[8,32,384]{2,1,0:T(8,128)(2,1)}), bf16[8,32,384]{2,1,0:T(8,128)(2,1)S(1)}, u32[]{:S(2)}, u32[]{:S(2)}) async-start(bf16[8,32,384]{2,1,0:T(8,128)(2,1)} %reshape.213), calls=%async_computation | async-start | bytes 393216 | tf_op jit(solution)/shard_map/all_to_all | solution.py:472
  12.6 15.5 %collective-permute-start.11 = (bf16[32,1024]{1,0:T(8,128)(2,1)S(1)}, bf16[32,1024]{1,0:T(8,128)(2,1)S(1)}, u32[]{:S(2)}, u32[]{:S(2)}) collective-permute-start(bf16[32,1024]{1,0:T(8,128)(2,1)S(1)} %copy-done.74), channel_id=1, source_target_pairs={{0,16},{16,0},{1,17},{17,1},{2,18},{18,2},{3,19},{19,3},{4,20},{20... | collective-permute-start | bytes 196616 | tf_op jit(solution)/shard_map/ppermute | solution.py:22
  15.7 21.7 %collective-permute-start.4 = (bf16[128,1024]{1,0:T(8,128)(2,1)S(1)}, bf16[128,1024]{1,0:T(8,128)(2,1)S(1)}, u32[]{:S(2)}, u32[]{:S(2)}) collective-permute-start(bf16[128,1024]{1,0:T(8,128)(2,1)S(1)} %get-tuple-element.74.refs_0_), channel_id=1, source_target_pairs={{0,16},{16,0},{1,17},{17,1},{2,18},{18,2},{3,19},{19,3},{4,20},{20... | collective-permute-start | bytes 786440 | tf_op jit(solution)/shard_map/ppermute | solution.py:22
  29.1 34.4 %all-to-all-start.2 = ((bf16[8,32,1152]{2,1,0:T(8,128)(2,1)}), bf16[8,32,1152]{2,1,0:T(8,128)(2,1)}, u32[]{:S(2)}, u32[]{:S(2)}) async-start(bf16[8,32,1152]{2,1,0:T(8,128)(2,1)} %pad_maximum_fusion.1), calls=%async_computation.2 | async-start | bytes 1179648 | tf_op jit(solution)/shard_map/all_to_all | solution.py:486
  35.8 13.2 %collective-permute-start.13 = (bf16[2,2,32,1024]{3,2,0,1:T(8,128)(2,1)S(1)}, bf16[2,2,32,1024]{3,2,0,1:T(8,128)(2,1)S(1)}, u32[]{:S(2)}, u32[]{:S(2)}) collective-permute-start(bf16[2,2,32,1024]{3,2,0,1:T(8,128)(2,1)S(1)} %get-tuple-element.148), channel_id=1, source_target_pairs={{0,4},{4,0},{1,5},{5,1},{2,6},{6,2},{3,7},{7,3},{8,12},{12,8},{9,1... | collective-permute-start | bytes 786440 | tf_op jit(solution)/shard_map/ppermute | solution.py:22
  37.4 13.3 %collective-permute-start.24 = (bf16[2,64,1024]{2,1,0:T(8,128)(2,1)S(1)}, bf16[2,64,1024]{2,1,0:T(8,128)(2,1)S(1)}, u32[]{:S(2)}, u32[]{:S(2)}) collective-permute-start(bf16[2,64,1024]{2,1,0:T(8,128)(2,1)S(1)} %copy-done.49), channel_id=1, source_target_pairs={{0,2},{2,0},{1,3},{3,1},{4,6},{6,4},{5,7},{7,5},{8,10},{10,8},{9,1... | collective-permute-start | bytes 786440 | tf_op jit(solution)/shard_map/ppermute | solution.py:22
  37.4 14.1 %collective-permute-start.2 = (bf16[128,1024]{1,0:T(8,128)(2,1)S(1)}, bf16[128,1024]{1,0:T(8,128)(2,1)S(1)}, u32[]{:S(2)}, u32[]{:S(2)}) collective-permute-start(bf16[128,1024]{1,0:T(8,128)(2,1)S(1)} %get-tuple-element.74.refs_0_), channel_id=1, source_target_pairs={{0,8},{8,0},{1,9},{9,1},{2,10},{10,2},{3,11},{11,3},{4,12},{12,4},... | collective-permute-start | bytes 786440 | tf_op jit(solution)/shard_map/ppermute | solution.py:22
  37.4 16.8 %collective-permute-start.6 = (bf16[128,1024]{1,0:T(8,128)(2,1)S(1)}, bf16[128,1024]{1,0:T(8,128)(2,1)S(1)}, u32[]{:S(2)}, u32[]{:S(2)}) collective-permute-start(bf16[128,1024]{1,0:T(8,128)(2,1)S(1)} %collective-permute-done.4.refs_4_), channel_id=1, source_target_pairs={{0,8},{8,0},{1,9},{9,1},{2,10},{10,2},{3,11},{11,3},{4,12},{12,4},... | collective-permute-start | bytes 786440 | tf_op jit(solution)/shard_map/ppermute | solution.py:22
  39.4 16.3 %collective-permute-start.1 = (bf16[128,1024]{1,0:T(8,128)(2,1)S(1)}, bf16[128,1024]{1,0:T(8,128)(2,1)S(1)}, u32[]{:S(2)}, u32[]{:S(2)}) collective-permute-start(bf16[128,1024]{1,0:T(8,128)(2,1)S(1)} %get-tuple-element.74.refs_0_), channel_id=1, source_target_pairs={{0,4},{4,0},{1,5},{5,1},{2,6},{6,2},{3,7},{7,3},{8,12},{12,8},{9,1... | collective-permute-start | bytes 786440 | tf_op jit(solution)/shard_map/ppermute | solution.py:22
  51.5 19.0 %collective-permute-start.14 = (bf16[8,1,32,1024]{3,2,1,0:T(8,128)(2,1)S(1)}, bf16[8,1,32,1024]{3,2,1,0:T(8,128)(2,1)}, u32[]{:S(2)}, u32[]{:S(2)}) collective-permute-start(bf16[8,1,32,1024]{3,2,1,0:T(8,128)(2,1)S(1)} %bitcast.101), channel_id=1, source_target_pairs={{0,1},{1,0},{2,3},{3,2},{4,5},{5,4},{6,7},{7,6},{8,9},{9,8},{10,11... | collective-permute-start | bytes 1572872 | tf_op jit(solution)/shard_map/ppermute | solution.py:22
  55.8 13.3 %collective-permute-start.5 = (bf16[128,1024]{1,0:T(8,128)(2,1)S(1)}, bf16[128,1024]{1,0:T(8,128)(2,1)S(1)}, u32[]{:S(2)}, u32[]{:S(2)}) collective-permute-start(bf16[128,1024]{1,0:T(8,128)(2,1)S(1)} %collective-permute-done.4.refs_4_), channel_id=1, source_target_pairs={{0,4},{4,0},{1,5},{5,1},{2,6},{6,2},{3,7},{7,3},{8,12},{12,8},{9,1... | collective-permute-start | bytes 786440 | tf_op jit(solution)/shard_map/ppermute | solution.py:22
  57.7 17.4 %collective-permute-start.15 = (bf16[8,1,32,1024]{3,2,1,0:T(8,128)(2,1)S(1)}, bf16[8,1,32,1024]{3,2,1,0:T(8,128)(2,1)S(1)}, u32[]{:S(2)}, u32[]{:S(2)}) collective-permute-start(bf16[8,1,32,1024]{3,2,1,0:T(8,128)(2,1)S(1)} %bitcast.102), channel_id=1, source_target_pairs={{0,2},{2,0},{1,3},{3,1},{4,6},{6,4},{5,7},{7,5},{8,10},{10,8},{9,1... | collective-permute-start | bytes 1572872 | tf_op jit(solution)/shard_map/ppermute | solution.py:22
  58.9 15.7 %collective-permute-start.3 = (bf16[128,1024]{1,0:T(8,128)(2,1)S(1)}, bf16[128,1024]{1,0:T(8,128)(2,1)S(1)}, u32[]{:S(2)}, u32[]{:S(2)}) collective-permute-start(bf16[128,1024]{1,0:T(8,128)(2,1)S(1)} %collective-permute-done.2.refs_2_), channel_id=1, source_target_pairs={{0,4},{4,0},{1,5},{5,1},{2,6},{6,2},{3,7},{7,3},{8,12},{12,8},{9,1... | collective-permute-start | bytes 786440 | tf_op jit(solution)/shard_map/ppermute | solution.py:22
  63.4 38.3 %collective-permute-start.33 = (bf16[1,8,32,1152]{3,2,1,0:T(8,128)(2,1)}, bf16[1,8,32,1152]{3,2,1,0:T(8,128)(2,1)}, u32[]{:S(2)}, u32[]{:S(2)}) collective-permute-start(bf16[1,8,32,1152]{3,2,1,0:T(8,128)(2,1)} %bitcast.23.a_ref), channel_id=1, source_target_pairs={{0,16},{16,0},{1,17},{17,1},{2,18},{18,2},{3,19},{19,3},{4,20},{20... | collective-permute-start | bytes 1769480 | tf_op jit(solution)/shard_map/ppermute | solution.py:22
  69.1 31.1 %collective-permute-start.25 = (bf16[128,1024]{1,0:T(8,128)(2,1)}, bf16[128,1024]{1,0:T(8,128)(2,1)}, u32[]{:S(2)}, u32[]{:S(2)}) collective-permute-start(bf16[128,1024]{1,0:T(8,128)(2,1)} %pick.1.refs_8_.cot_ref), channel_id=1, source_target_pairs={{0,4},{4,0},{1,5},{5,1},{2,6},{6,2},{3,7},{7,3},{8,12},{12,8},{9,1... | collective-permute-start | bytes 786440 | tf_op jit(solution)/shard_map/ppermute | solution.py:22
  70.5 32.3 %collective-permute-start.16 = (bf16[8,1,32,1024]{3,2,1,0:T(8,128)(2,1)}, bf16[8,1,32,1024]{3,2,1,0:T(8,128)(2,1)}, u32[]{:S(2)}, u32[]{:S(2)}) collective-permute-start(bf16[8,1,32,1024]{3,2,1,0:T(8,128)(2,1)} %collective-permute-done.14.b_ref), channel_id=1, source_target_pairs={{0,2},{2,0},{1,3},{3,1},{4,6},{6,4},{5,7},{7,5},{8,10},{10,8},{9,1... | collective-permute-start | bytes 1572872 | tf_op jit(solution)/shard_map/ppermute | solution.py:22
  74.7 27.6 %collective-permute-start.26 = (bf16[128,1024]{1,0:T(8,128)(2,1)}, bf16[128,1024]{1,0:T(8,128)(2,1)}, u32[]{:S(2)}, u32[]{:S(2)}) collective-permute-start(bf16[128,1024]{1,0:T(8,128)(2,1)} %pick.1.refs_8_.cot_ref), channel_id=1, source_target_pairs={{0,8},{8,0},{1,9},{9,1},{2,10},{10,2},{3,11},{11,3},{4,12},{12,4},... | collective-permute-start | bytes 786440 | tf_op jit(solution)/shard_map/ppermute | solution.py:22
  75.8 26.5 %collective-permute-start.27 = (bf16[128,1024]{1,0:T(8,128)(2,1)}, bf16[128,1024]{1,0:T(8,128)(2,1)}, u32[]{:S(2)}, u32[]{:S(2)}) collective-permute-start(bf16[128,1024]{1,0:T(8,128)(2,1)} %pick.1.refs_8_.cot_ref), channel_id=1, source_target_pairs={{0,12},{4,8},{8,4},{12,0},{1,13},{5,9},{9,5},{13,1},{2,14},{6,10},... | collective-permute-start | bytes 786440 | tf_op jit(solution)/shard_map/ppermute | solution.py:26
  95.9 12.3 %all-to-all-start.1 = ((bf16[8,128,128]{2,1,0:T(8,128)(2,1)}), bf16[8,128,128]{2,1,0:T(8,128)(2,1)}, u32[]{:S(2)}, u32[]{:S(2)}) async-start(bf16[8,128,128]{2,1,0:T(8,128)(2,1)} %get-tuple-element.78), calls=%async_computation.1 | async-start | bytes 524288 | tf_op jit(solution)/shard_map/all_to_all | solution.py:538
  100.2 16.6 %collective-permute-start.32 = (bf16[1,8,32,1152]{3,2,1,0:T(8,128)(2,1)}, bf16[1,8,32,1152]{3,2,1,0:T(8,128)(2,1)}, u32[]{:S(2)}, u32[]{:S(2)}) collective-permute-start(bf16[1,8,32,1152]{3,2,1,0:T(8,128)(2,1)} %bitcast.23.a_ref), channel_id=1, source_target_pairs={{0,1},{1,0},{2,3},{3,2},{4,5},{5,4},{6,7},{7,6},{8,9},{9,8},{10,11... | collective-permute-start | bytes 1769480 | tf_op jit(solution)/shard_map/ppermute | solution.py:22
  101.8 23.5 %collective-permute-start.34 = (bf16[1,8,32,1152]{3,2,1,0:T(8,128)(2,1)}, bf16[1,8,32,1152]{3,2,1,0:T(8,128)(2,1)}, u32[]{:S(2)}, u32[]{:S(2)}) collective-permute-start(bf16[1,8,32,1152]{3,2,1,0:T(8,128)(2,1)} %collective-permute-done.33.c_ref), channel_id=1, source_target_pairs={{0,1},{1,0},{2,3},{3,2},{4,5},{5,4},{6,7},{7,6},{8,9},{9,8},{10,11... | collective-permute-start | bytes 1769480 | tf_op jit(solution)/shard_map/ppermute | solution.py:22
  113.0 12.1 %collective-permute-start.19 = (bf16[128,1024]{1,0:T(8,128)(2,1)S(1)}, bf16[128,1024]{1,0:T(8,128)(2,1)S(1)}, u32[]{:S(2)}, u32[]{:S(2)}) collective-permute-start(bf16[128,1024]{1,0:T(8,128)(2,1)S(1)} %get-tuple-element.82.refs_0_), channel_id=1, source_target_pairs={{0,12},{4,8},{8,4},{12,0},{1,13},{5,9},{9,5},{13,1},{2,14},{6,10},... | collective-permute-start | bytes 786440 | tf_op jit(solution)/shard_map/ppermute | solution.py:26
  134.5 12.7 %collective-permute-start.38 = (bf16[128,1024]{1,0:T(8,128)(2,1)S(1)}, bf16[128,1024]{1,0:T(8,128)(2,1)S(1)}, u32[]{:S(2)}, u32[]{:S(2)}) collective-permute-start(bf16[128,1024]{1,0:T(8,128)(2,1)S(1)} %get-tuple-element.93), channel_id=1, source_target_pairs={{0,2},{2,0},{1,3},{3,1},{4,6},{6,4},{5,7},{7,5},{8,10},{10,8},{9,1... | collective-permute-start | bytes 786440 | tf_op jit(solution)/shard_map/ppermute | solution.py:22
  134.9 13.0 %collective-permute-start.36 = (bf16[128,1024]{1,0:T(8,128)(2,1)S(1)}, bf16[128,1024]{1,0:T(8,128)(2,1)S(1)}, u32[]{:S(2)}, u32[]{:S(2)}) collective-permute-start(bf16[128,1024]{1,0:T(8,128)(2,1)S(1)} %get-tuple-element.91), channel_id=1, source_target_pairs={{0,2},{2,0},{1,3},{3,1},{4,6},{6,4},{5,7},{7,5},{8,10},{10,8},{9,1... | collective-permute-start | bytes 786440 | tf_op jit(solution)/shard_map/ppermute | solution.py:22
  135.0 13.4 %collective-permute-start.35 = (bf16[128,1024]{1,0:T(8,128)(2,1)S(1)}, bf16[128,1024]{1,0:T(8,128)(2,1)S(1)}, u32[]{:S(2)}, u32[]{:S(2)}) collective-permute-start(bf16[128,1024]{1,0:T(8,128)(2,1)S(1)} %get-tuple-element.89), channel_id=1, source_target_pairs={{0,2},{2,0},{1,3},{3,1},{4,6},{6,4},{5,7},{7,5},{8,10},{10,8},{9,1... | collective-permute-start | bytes 786440 | tf_op jit(solution)/shard_map/ppermute | solution.py:22
  142.9 55.2 %collective-permute-start.60 = (bf16[2,8,32,1152]{3,2,1,0:T(8,128)(2,1)}, bf16[2,8,32,1152]{3,2,1,0:T(8,128)(2,1)}, u32[]{:S(2)}, u32[]{:S(2)}) collective-permute-start(bf16[2,8,32,1152]{3,2,1,0:T(8,128)(2,1)} %bitcast.31), channel_id=1, source_target_pairs={{0,1},{1,0},{2,3},{3,2},{4,5},{5,4},{6,7},{7,6},{8,9},{9,8},{10,11... | collective-permute-start | bytes 3538952 | tf_op jit(solution)/shard_map/ppermute | solution.py:22
  147.2 12.1 %collective-permute-start.39 = (bf16[128,1024]{1,0:T(8,128)(2,1)S(1)}, bf16[128,1024]{1,0:T(8,128)(2,1)S(1)}, u32[]{:S(2)}, u32[]{:S(2)}) collective-permute-start(bf16[128,1024]{1,0:T(8,128)(2,1)S(1)} %add_convert_fusion.7), channel_id=1, source_target_pairs={{0,8},{8,0},{1,9},{9,1},{2,10},{10,2},{3,11},{11,3},{4,12},{12,4},... | collective-permute-start | bytes 786440 | tf_op jit(solution)/shard_map/ppermute | solution.py:22
  147.9 11.4 %collective-permute-start.37 = (bf16[128,1024]{1,0:T(8,128)(2,1)S(1)}, bf16[128,1024]{1,0:T(8,128)(2,1)S(1)}, u32[]{:S(2)}, u32[]{:S(2)}) collective-permute-start(bf16[128,1024]{1,0:T(8,128)(2,1)S(1)} %add_convert_fusion.8), channel_id=1, source_target_pairs={{0,4},{4,0},{1,5},{5,1},{2,6},{6,2},{3,7},{7,3},{8,12},{12,8},{9,1... | collective-permute-start | bytes 786440 | tf_op jit(solution)/shard_map/ppermute | solution.py:22
  148.4 26.3 %collective-permute-start.47 = (bf16[128,1024]{1,0:T(8,128)(2,1)}, bf16[128,1024]{1,0:T(8,128)(2,1)}, u32[]{:S(2)}, u32[]{:S(2)}) collective-permute-start(bf16[128,1024]{1,0:T(8,128)(2,1)} %get-tuple-element.104), channel_id=1, source_target_pairs={{0,2},{2,0},{1,3},{3,1},{4,6},{6,4},{5,7},{7,5},{8,10},{10,8},{9,1... | collective-permute-start | bytes 786440 | tf_op jit(solution)/shard_map/ppermute | solution.py:22
  163.8 14.7 %all-to-all-start.3 = ((bf16[8,128,128]{2,1,0:T(8,128)(2,1)}), bf16[8,128,128]{2,1,0:T(8,128)(2,1)S(1)}, u32[]{:S(2)}, u32[]{:S(2)}) async-start(bf16[8,128,128]{2,1,0:T(8,128)(2,1)} %copy-done.48), calls=%async_computation.3 | async-start | bytes 524288 | tf_op jit(solution)/shard_map/all_to_all | solution.py:561
  174.2 32.0 %collective-permute-start.62 = (bf16[2,2,2,2,32,1024]{5,4,3,2,1,0:T(8,128)(2,1)}, bf16[2,2,2,2,32,1024]{5,4,3,2,1,0:T(8,128)(2,1)}, u32[]{:S(2)}, u32[]{:S(2)}) collective-permute-start(bf16[2,2,2,2,32,1024]{5,4,3,2,1,0:T(8,128)(2,1)} %bitcast.39), channel_id=1, source_target_pairs={{0,2},{2,0},{1,3},{3,1},{4,6},{6,4},{5,7},{7,5},{8,10},{10,8},{9,1... | collective-permute-start | bytes 3145736 | tf_op jit(solution)/shard_map/ppermute | solution.py:22
  174.2 21.4 %collective-permute-start.45 = (bf16[128,1024]{1,0:T(8,128)(2,1)}, bf16[128,1024]{1,0:T(8,128)(2,1)}, u32[]{:S(2)}, u32[]{:S(2)}) collective-permute-start(bf16[128,1024]{1,0:T(8,128)(2,1)} %get-tuple-element.102), channel_id=1, source_target_pairs={{0,2},{2,0},{1,3},{3,1},{4,6},{6,4},{5,7},{7,5},{8,10},{10,8},{9,1... | collective-permute-start | bytes 786440 | tf_op jit(solution)/shard_map/ppermute | solution.py:22
  174.7 26.0 %collective-permute-start.43 = (bf16[128,1024]{1,0:T(8,128)(2,1)}, bf16[128,1024]{1,0:T(8,128)(2,1)}, u32[]{:S(2)}, u32[]{:S(2)}) collective-permute-start(bf16[128,1024]{1,0:T(8,128)(2,1)} %get-tuple-element.100), channel_id=1, source_target_pairs={{0,2},{2,0},{1,3},{3,1},{4,6},{6,4},{5,7},{7,5},{8,10},{10,8},{9,1... | collective-permute-start | bytes 786440 | tf_op jit(solution)/shard_map/ppermute | solution.py:22
  198.1 57.5 %collective-permute-start.42 = (bf16[128,1024]{1,0:T(8,128)(2,1)}, bf16[128,1024]{1,0:T(8,128)(2,1)}, u32[]{:S(2)}, u32[]{:S(2)}) collective-permute-start(bf16[128,1024]{1,0:T(8,128)(2,1)} %get-tuple-element.98), channel_id=1, source_target_pairs={{0,2},{2,0},{1,3},{3,1},{4,6},{6,4},{5,7},{7,5},{8,10},{10,8},{9,1... | collective-permute-start | bytes 786440 | tf_op jit(solution)/shard_map/ppermute | solution.py:22
  200.6 31.6 %collective-permute-start.61 = (bf16[8,32,1152]{2,1,0:T(8,128)(2,1)}, bf16[8,32,1152]{2,1,0:T(8,128)(2,1)}, u32[]{:S(2)}, u32[]{:S(2)}) collective-permute-start(bf16[8,32,1152]{2,1,0:T(8,128)(2,1)} %bitcast.34), channel_id=1, source_target_pairs={{0,16},{16,0},{1,17},{17,1},{2,18},{18,2},{3,19},{19,3},{4,20},{20... | collective-permute-start | bytes 1769480 | tf_op jit(solution)/shard_map/ppermute | solution.py:22
  203.6 48.7 %collective-permute-start.53 = (bf16[128,1024]{1,0:T(8,128)(2,1)}, bf16[128,1024]{1,0:T(8,128)(2,1)}, u32[]{:S(2)}, u32[]{:S(2)}) collective-permute-start(bf16[128,1024]{1,0:T(8,128)(2,1)} %get-tuple-element.114), channel_id=1, source_target_pairs={{0,4},{4,0},{1,5},{5,1},{2,6},{6,2},{3,7},{7,3},{8,12},{12,8},{9,1... | collective-permute-start | bytes 786440 | tf_op jit(solution)/shard_map/ppermute | solution.py:22
  206.2 28.6 %collective-permute-start.51 = (bf16[128,1024]{1,0:T(8,128)(2,1)}, bf16[128,1024]{1,0:T(8,128)(2,1)}, u32[]{:S(2)}, u32[]{:S(2)}) collective-permute-start(bf16[128,1024]{1,0:T(8,128)(2,1)} %get-tuple-element.112), channel_id=1, source_target_pairs={{0,4},{4,0},{1,5},{5,1},{2,6},{6,2},{3,7},{7,3},{8,12},{12,8},{9,1... | collective-permute-start | bytes 786440 | tf_op jit(solution)/shard_map/ppermute | solution.py:22
  211.7 42.6 %collective-permute-start.55 = (bf16[128,1024]{1,0:T(8,128)(2,1)}, bf16[128,1024]{1,0:T(8,128)(2,1)}, u32[]{:S(2)}, u32[]{:S(2)}) collective-permute-start(bf16[128,1024]{1,0:T(8,128)(2,1)} %add_convert_fusion.1), channel_id=1, source_target_pairs={{0,8},{8,0},{1,9},{9,1},{2,10},{10,2},{3,11},{11,3},{4,12},{12,4},... | collective-permute-start | bytes 786440 | tf_op jit(solution)/shard_map/ppermute | solution.py:22
  213.8 32.4 %all-to-all-start.4 = ((bf16[8,32,384]{2,1,0:T(8,128)(2,1)}), bf16[8,32,384]{2,1,0:T(8,128)(2,1)S(1)}, u32[]{:S(2)}, u32[]{:S(2)}) async-start(bf16[8,32,384]{2,1,0:T(8,128)(2,1)} %add_convert_fusion.9), calls=%async_computation.4 | async-start | bytes 393216 | tf_op jit(solution)/shard_map/all_to_all | solution.py:644
  232.3 14.0 %collective-permute-start.63 = (bf16[2,2,2,32,1024]{4,3,2,1,0:T(8,128)(2,1)}, bf16[2,2,2,32,1024]{4,3,2,1,0:T(8,128)(2,1)S(1)}, u32[]{:S(2)}, u32[]{:S(2)}) collective-permute-start(bf16[2,2,2,32,1024]{4,3,2,1,0:T(8,128)(2,1)} %bitcast.116), channel_id=1, source_target_pairs={{0,1},{1,0},{2,3},{3,2},{4,5},{5,4},{6,7},{7,6},{8,9},{9,8},{10,11... | collective-permute-start | bytes 1572872 | tf_op jit(solution)/shard_map/ppermute | solution.py:22
  234.8 22.7 %collective-permute-start.48 = (bf16[128,1024]{1,0:T(8,128)(2,1)S(1)}, bf16[128,1024]{1,0:T(8,128)(2,1)S(1)}, u32[]{:S(2)}, u32[]{:S(2)}) collective-permute-start(bf16[128,1024]{1,0:T(8,128)(2,1)S(1)} %copy-done.71), channel_id=1, source_target_pairs={{0,12},{4,8},{8,4},{12,0},{1,13},{5,9},{9,5},{13,1},{2,14},{6,10},... | collective-permute-start | bytes 786440 | tf_op jit(solution)/shard_map/ppermute | solution.py:26
  246.3 12.8 %collective-permute-start.46 = (bf16[128,1024]{1,0:T(8,128)(2,1)S(1)}, bf16[128,1024]{1,0:T(8,128)(2,1)S(1)}, u32[]{:S(2)}, u32[]{:S(2)}) collective-permute-start(bf16[128,1024]{1,0:T(8,128)(2,1)S(1)} %add_convert_fusion.4), channel_id=1, source_target_pairs={{0,8},{8,0},{1,9},{9,1},{2,10},{10,2},{3,11},{11,3},{4,12},{12,4},... | collective-permute-start | bytes 786440 | tf_op jit(solution)/shard_map/ppermute | solution.py:22
  246.3 41.7 %all-to-all-start.5 = ((bf16[8,32,1152]{2,1,0:T(8,128)(2,1)}), bf16[8,32,1152]{2,1,0:T(8,128)(2,1)}, u32[]{:S(2)}, u32[]{:S(2)}) async-start(bf16[8,32,1152]{2,1,0:T(8,128)(2,1)} %fusion), calls=%async_computation.5 | async-start | bytes 1179648 | tf_op jit(solution)/shard_map/all_to_all | solution.py:565
  252.3 13.7 %collective-permute-start.44 = (bf16[128,1024]{1,0:T(8,128)(2,1)S(1)}, bf16[128,1024]{1,0:T(8,128)(2,1)S(1)}, u32[]{:S(2)}, u32[]{:S(2)}) collective-permute-start(bf16[128,1024]{1,0:T(8,128)(2,1)S(1)} %copy-done.72), channel_id=1, source_target_pairs={{0,4},{4,0},{1,5},{5,1},{2,6},{6,2},{3,7},{7,3},{8,12},{12,8},{9,1... | collective-permute-start | bytes 786440 | tf_op jit(solution)/shard_map/ppermute | solution.py:22
  254.3 17.3 %collective-permute-start.64 = (bf16[2,2,32,1024]{3,2,1,0:T(8,128)(2,1)S(1)}, bf16[2,2,32,1024]{3,2,1,0:T(8,128)(2,1)S(1)}, u32[]{:S(2)}, u32[]{:S(2)}) collective-permute-start(bf16[2,2,32,1024]{3,2,1,0:T(8,128)(2,1)S(1)} %bitcast.118), channel_id=1, source_target_pairs={{0,4},{4,0},{1,5},{5,1},{2,6},{6,2},{3,7},{7,3},{8,12},{12,8},{9,1... | collective-permute-start | bytes 786440 | tf_op jit(solution)/shard_map/ppermute | solution.py:22
  255.6 21.2 %collective-permute-start.50 = (bf16[128,1024]{1,0:T(8,128)(2,1)S(1)}, bf16[128,1024]{1,0:T(8,128)(2,1)S(1)}, u32[]{:S(2)}, u32[]{:S(2)}) collective-permute-start(bf16[128,1024]{1,0:T(8,128)(2,1)S(1)} %copy-done.67), channel_id=1, source_target_pairs={{0,4},{4,0},{1,5},{5,1},{2,6},{6,2},{3,7},{7,3},{8,12},{12,8},{9,1... | collective-permute-start | bytes 786440 | tf_op jit(solution)/shard_map/ppermute | solution.py:22
  257.6 19.2 %collective-permute-start.52 = (bf16[128,1024]{1,0:T(8,128)(2,1)S(1)}, bf16[128,1024]{1,0:T(8,128)(2,1)S(1)}, u32[]{:S(2)}, u32[]{:S(2)}) collective-permute-start(bf16[128,1024]{1,0:T(8,128)(2,1)S(1)} %add_convert_fusion.2), channel_id=1, source_target_pairs={{0,8},{8,0},{1,9},{9,1},{2,10},{10,2},{3,11},{11,3},{4,12},{12,4},... | collective-permute-start | bytes 786440 | tf_op jit(solution)/shard_map/ppermute | solution.py:22
  259.0 17.7 %collective-permute-start.56 = (bf16[128,1024]{1,0:T(8,128)(2,1)S(1)}, bf16[128,1024]{1,0:T(8,128)(2,1)S(1)}, u32[]{:S(2)}, u32[]{:S(2)}) collective-permute-start(bf16[128,1024]{1,0:T(8,128)(2,1)S(1)} %add_convert_fusion), channel_id=1, source_target_pairs={{0,16},{16,0},{1,17},{17,1},{2,18},{18,2},{3,19},{19,3},{4,20},{20... | collective-permute-start | bytes 786440 | tf_op jit(solution)/shard_map/ppermute | solution.py:22
  (102 other events, 802.8 us)

commit v3 on v2

v3 whole, which is shorter than its diff:
```python
import functools
import math

import jax
import jax.numpy as jnp
from jax import lax
from jax.experimental import pallas as pl
from jax.experimental.pallas import tpu as pltpu
from jax.sharding import Mesh
from jax.sharding import PartitionSpec as P

HEADS = 16
norm_eps = 1e-05
rope_base = 160000.0
f32 = jnp.float32
bf16 = jnp.bfloat16
LANES = 128
MIB = 1024 * 1024


def partner(array, axis):
    return lax.ppermute(array, axis, [(0, 1), (1, 0)])


def opposite(array, axes):
    return lax.ppermute(array, axes, [(i, 3 - i) for i in range(4)])


def after(array, *others):
    return lax.optimization_barrier((array, *others))[0]


def fence(live):
    return dict(zip(live, lax.optimization_barrier(tuple(live.values()))))


def add(*terms):
    total = terms[0].astype(f32)
    for term in terms[1:]:
        total = total + term.astype(f32)
    return total.astype(terms[0].dtype)


def call(kernel, name, outs, places, *arrays, scratch=(), mib=16, flops=0, exps=0):
    vmem = pl.BlockSpec(memory_space=pltpu.VMEM)
    moved = sum(array.size * array.dtype.itemsize for array in arrays)
    moved += sum(math.prod(shape) * jnp.dtype(dtype).itemsize for shape, dtype in outs)
    return pl.pallas_call(
        kernel,
        in_specs=[pl.BlockSpec(memory_space=pltpu.SMEM)] + [vmem] * len(arrays),
        out_specs=[vmem] * len(outs),
        out_shape=[jax.ShapeDtypeStruct(shape, dtype) for shape, dtype in outs],
        scratch_shapes=list(scratch),
        compiler_params=pltpu.CompilerParams(vmem_limit_bytes=mib * MIB),
        cost_estimate=pl.CostEstimate(flops=flops, bytes_accessed=moved, transcendentals=exps),
        name=name,
    )(places, *arrays)


CHIP, ZH, ZL, X, C, Y = range(6)


def nt(left, right):
    return lax.dot_general(left, right, (((1,), (1,)), ((), ())), preferred_element_type=f32)


def tn(left, right):
    return lax.dot_general(left, right, (((0,), (0,)), ((), ())), preferred_element_type=f32)


def nn(left, right):
    return lax.dot_general(left, right, (((1,), (0,)), ((), ())), preferred_element_type=f32)


def normalize(values):
    centre = values - jnp.mean(values, axis=-1, keepdims=True)
    inverse = lax.rsqrt(jnp.mean(centre * centre, axis=-1, keepdims=True) + norm_eps)
    return centre * inverse, inverse


def normalize_back(scaled, normed, inverse):
    inner = jnp.mean(scaled * normed, axis=-1, keepdims=True)
    return inverse * (scaled - jnp.mean(scaled, axis=-1, keepdims=True) - normed * inner)


def pick_kernel(places, own_ref, other_ref, block_ref):
    half = own_ref.shape[1]
    block_ref[:half, :] = own_ref[places[C]]
    block_ref[half:, :] = other_ref[places[C]]


def enter_kernel(places, own_ref, other_ref, cot_a_ref, cot_b_ref, block_ref, cot_ref, low_ref):
    pick_kernel(places, own_ref, other_ref, block_ref)
    pick_kernel(places, cot_a_ref, cot_b_ref, cot_ref)
    low_ref[...] = normalize(block_ref[...].astype(f32))[0].astype(bf16)


def leave_kernel(places, own_ref, other_ref, out_ref):
    out_ref[places[C]] = own_ref[...]
    out_ref[1 - places[C]] = other_ref[...]


def assemble_kernel(lead, first, second, places, a_ref, b_ref, c_ref, d_ref, out_ref):
    chip = places[lead] if lead is not None else 0
    one, two = places[first], places[second]
    for i, row in enumerate(((a_ref, b_ref), (c_ref, d_ref))):
        for j, ref in enumerate(row):
            for at in range(ref.shape[0]):
                out_ref[chip ^ at, one ^ i, :, two ^ j] = ref[at]


def assemble(places, lead, first, second, pieces):
    extent = pieces[0].shape
    shape = (extent[0], 2, extent[1], 2) + extent[2:]
    if extent[2] % 16 == 0:
        kernel = functools.partial(assemble_kernel, lead, first, second)
        return call(kernel, "assemble", [(shape, bf16)], places, *pieces)[0]

    def ordered(own, other, place, axis):
        straight = jnp.stack([own, other], axis)
        return jnp.where(place == 0, straight, jnp.flip(straight, axis))

    one = ordered(pieces[0], pieces[1], places[second], 2)
    two = ordered(pieces[2], pieces[3], places[second], 2)
    whole = ordered(one, two, places[first], 1)
    if lead is None:
        return whole
    return jnp.take(whole, jnp.arange(extent[0]) ^ places[lead], axis=0)


def assemble_rows_kernel(places, a_ref, b_ref, c_ref, d_ref, out_ref):
    for i, row in enumerate(((a_ref, b_ref), (c_ref, d_ref))):
        for j, ref in enumerate(row):
            for at in range(4):
                for k in range(2):
                    out_ref[places[CHIP] ^ (2 * at + j), places[C] ^ i, places[Y] ^ k] = ref[at, k]


def assemble_rows(places, pieces):
    if pieces[0].shape[2] % 16 == 0:
        shape = (8, 2) + pieces[0].shape[1:]
        return call(assemble_rows_kernel, "assemble_rows", [(shape, bf16)], places, *pieces)[0]
    merged = [jnp.stack(pieces[at : at + 2], axis=1) for at in (0, 2)]
    merged = [member.reshape((8, 1) + member.shape[2:]) for member in merged]
    pieces = [member[:, :, at] for member in merged for at in range(2)]
    return assemble(places, CHIP, C, Y, pieces)


def total_kernel(places, a_ref, b_ref, out_ref):
    out_ref[...] = (a_ref[...].astype(f32) + b_ref[...].astype(f32)).astype(bf16)


def total(places, kept, other):
    if kept.shape[1] % 16 == 0:
        return call(total_kernel, "total", [(kept.shape, bf16)], places, kept, other)[0]
    return add(kept, other)


def put_shares(made, place, at, kept_ref, sent_ref):
    share, width = kept_ref.shape[1:]
    groups = made.shape[0] // (2 * share)
    made = made.reshape(groups, 2, share, width)
    kept_ref[pl.ds(at, groups)] = jnp.where(place == 0, made[:, 0], made[:, 1]).astype(bf16)
    sent_ref[pl.ds(at, groups)] = jnp.where(place == 0, made[:, 1], made[:, 0]).astype(bf16)


def split_kernel(which, count, places, *refs):
    kept_ref, sent_ref = refs[count:]
    place = places[which]
    for ref, at in ((kept_ref, place), (sent_ref, 1 - place)):
        total = refs[0][:, at]
        if count > 1:
            total = total.astype(f32)
            for term in refs[1:count]:
                total = total + term[:, at].astype(f32)
        ref[...] = total.astype(bf16)


def split(places, which, parts, before):
    shape = parts[0].shape
    rest = shape[:before] + shape[before + 1 :]
    if shape[-2] % 16 == 0:
        flat = (math.prod(shape[:before]), 2, math.prod(shape[before + 1 : -1]), shape[-1])
        outs = [((flat[0],) + flat[2:], bf16)] * 2
        kernel = functools.partial(split_kernel, which, len(parts))
        halves = call(kernel, "split", outs, places, *[part.reshape(flat) for part in parts])
        return [half.reshape(rest) for half in halves]
    total = add(*parts)
    return [
        lax.dynamic_index_in_dim(total, at, before, False)
        for at in (places[which], 1 - places[which])
    ]


def halves_swapped(values, half):
    lane = lax.broadcasted_iota(jnp.int32, values.shape, 1)
    up = pltpu.roll(values, half, 1)
    down = pltpu.roll(values, values.shape[1] - half, 1)
    return jnp.where(lane % (2 * half) < half, down, up)


def project_kernel(half, places, *refs):
    pieces, (weight_ref, table_ref, out_ref, stack_ref) = refs[:8], refs[8:]
    width = out_ref.shape[1] // 3
    rows = pieces[0].shape[0]
    for at in range(0, 8, 2):
        here = pl.ds(at * rows, 2 * rows)
        both = jnp.concatenate([ref[...] for ref in pieces[at : at + 2]])
        stack_ref[here, :] = both
        made = nn(both, weight_ref[...])
        cosine, sine = table_ref[here, :width], table_ref[here, width:]
        for place in range(2):
            part = made[:, place * width : (place + 1) * width]
            turned = part * cosine + halves_swapped(part, half) * sine
            out_ref[here, place * width : (place + 1) * width] = turned.astype(bf16)
        out_ref[here, 2 * width :] = made[:, 2 * width :].astype(bf16)


def of_head(values, head, size):
    lane = lax.broadcasted_iota(jnp.int32, values.shape, 1)
    return jnp.where(lane // size == head, values, jnp.zeros_like(values))


def keys_and_values(refs, width):
    if len(refs) == 1:
        return refs[0][:, width : 2 * width], refs[0][:, 2 * width :]
    return refs[1][:, :width], refs[1][:, width:]


def attend_kernel(size, places, *refs):
    refs, (o_ref, log_ref) = refs[:-2], refs[-2:]
    block, width = o_ref.shape[1:]
    keys, values = keys_and_values(refs, width)
    step = log_ref.shape[2]
    scale = math.log2(math.e) / math.sqrt(size)

    def visit(i, carry):
        queries = refs[0][pl.ds(pl.multiple_of(i * step, step), step), :width]
        outs = []
        for head in range(width // size):
            scores = nt(keys, of_head(queries, head, size))
            top = jnp.max(scores, axis=0, keepdims=True)
            weights = jnp.exp2((scores - top) * scale)
            total = jnp.sum(weights, axis=0, keepdims=True)
            probs = (weights * (1.0 / total)).astype(bf16)
            outs.append(tn(values, probs)[head * size : (head + 1) * size])
            log_ref[i, head : head + 1, :] = top * scale + jnp.log2(total)
        out = jnp.transpose(jnp.concatenate(outs, axis=0)).astype(bf16)
        for at in range(step // block):
            chip = places[CHIP] ^ (i * (step // block) + at)
            o_ref[chip] = out[at * block : (at + 1) * block]
        return carry

    lax.fori_loop(0, refs[0].shape[0] // step, visit, 0)


def attend_back_kernel(size, together, places, *refs):
    refs, (grad_ref, log_ref, table_ref, dq_ref, dk_ref, dv_ref) = refs[:-6], refs[-6:]
    block, width = grad_ref.shape[1:]
    keys, values = keys_and_values(refs, width)
    step = log_ref.shape[2]
    scale = 1.0 / math.sqrt(size)
    exponent = scale * math.log2(math.e)
    dk_ref[...] = jnp.zeros_like(dk_ref)
    dv_ref[...] = jnp.zeros_like(dv_ref)

    def turned(part, here):
        back = halves_swapped(part, size // 2) * table_ref[here, width:]
        return (part * table_ref[here, :width] - back).astype(bf16)

    def visit(i, carry):
        here = pl.ds(pl.multiple_of(i * step, step), step)
        queries = refs[0][here, :width]
        grads = [grad_ref[places[CHIP] ^ (i * (step // block) + at)] for at in range(step // block)]
        grads = jnp.concatenate(grads)
        outs = []
        for head in range(width // size):
            query, grad = of_head(queries, head, size), of_head(grads, head, size)
            probs = jnp.exp2(nt(keys, query) * exponent - log_ref[i, head : head + 1, :])
            grad_probs = nt(values, grad)
            delta = jnp.sum(probs * grad_probs, axis=0, keepdims=True)
            grad_scores = (probs * (grad_probs - delta)).astype(bf16)
            outs.append(tn(keys, grad_scores)[head * size : (head + 1) * size])
            dk_ref[...] += nn(grad_scores, query)
            dv_ref[...] += nn(probs.astype(bf16), grad)
        dq = jnp.transpose(jnp.concatenate(outs, axis=0)) * scale
        dq_ref[here, :width] = turned(dq, here)
        return carry

    lax.fori_loop(0, refs[0].shape[0] // step, visit, 0)
    if together:
        everything = pl.ds(0, dq_ref.shape[0])
        dq_ref[:, width : 2 * width] = turned(dk_ref[...] * scale, everything)
        dq_ref[:, 2 * width :] = dv_ref[...].astype(bf16)
    else:
        dk_ref[...] = dk_ref[...] * scale


def turn_back_kernel(half, places, dq_ref, dk_ref, dv_ref, table_ref, out_ref):
    width = dq_ref.shape[1]
    part = dk_ref[...]
    back = halves_swapped(part, half) * table_ref[:, width:]
    out_ref[:, :width] = dq_ref[...]
    out_ref[:, width : 2 * width] = (part * table_ref[:, :width] - back).astype(bf16)
    out_ref[:, 2 * width :] = dv_ref[...].astype(bf16)


def middle_kernel(places, arrived_ref, weight_ref, tokens_ref, attended_ref, middle_ref, low_ref):
    wide = arrived_ref.shape[2]
    for at in range(arrived_ref.shape[0]):
        attended_ref[:, at * wide : (at + 1) * wide] = arrived_ref[at]
    middle = tokens_ref[...].astype(f32) + nn(attended_ref[...], weight_ref[...])
    middle_ref[...] = middle
    low_ref[...] = normalize(middle)[0].astype(bf16)


def feed_kernel(places, *refs):
    two, cot, (w_ref, hidden_ref, grad_ref), outs = refs[:8], refs[8:16], refs[16:19], refs[19:]
    piece = hidden_ref.shape[1]
    rows = two[0].shape[0]
    w_in, w_out = w_ref[:, : 2 * piece], w_ref[:, 2 * piece :]
    for at in (4, 6, 0, 2):
        here = pl.ds(at * rows, 2 * rows)
        gate_up = nn(jnp.concatenate([two[at][...], two[at + 1][...]]), w_in)
        grad_hidden = nn(jnp.concatenate([cot[at][...], cot[at + 1][...]]), w_out)
        gate, lift = gate_up[:, :piece], gate_up[:, piece:]
        cdf = 0.5 * (1.0 + lax.erf(gate * math.sqrt(0.5)))
        density = jnp.exp(-0.5 * gate * gate) * (1.0 / math.sqrt(2.0 * math.pi))
        activated = gate * cdf
        hidden_ref[here, :] = (activated * lift).astype(bf16)
        grad_gate = (grad_hidden * lift * (cdf + gate * density)).astype(bf16)
        grad_lift = (grad_hidden * activated).astype(bf16)
        grad_ref[here, :piece] = grad_gate
        grad_ref[here, piece:] = grad_lift
        made = nt(grad_gate, w_in[:, :piece]) + nt(grad_lift, w_in[:, piece:])
        outs[at // 4][pl.ds(at % 4 * rows, 2 * rows), :] = made.astype(bf16)


def feed(places, two, cot, weights):
    rows, width = two[0].shape
    piece = weights.shape[1] // 3
    outs = [((8 * rows, piece), bf16), ((8 * rows, 2 * piece), bf16)] + [((4 * rows, width), bf16)] * 2
    hidden, grads, *terms = call(
        feed_kernel,
        "feed",
        outs,
        places,
        *two,
        *cot,
        weights,
        mib=24,
        flops=80 * rows * width * piece,
        exps=16 * rows * piece,
    )
    return hidden, grads, terms


def feed_rest_kernel(places, *refs):
    two, cot, (hidden_ref, grad_ref, w_ref), outs, made_refs = (
        refs[:8],
        refs[8:16],
        refs[16:19],
        refs[19:21],
        refs[21:],
    )
    piece = hidden_ref.shape[1]
    rows, width = two[0].shape
    w_out = w_ref[:, 2 * piece :]
    for at in (4, 6, 0, 2):
        made = nt(hidden_ref[pl.ds(at * rows, 2 * rows), :], w_out)
        outs[at // 4][pl.ds(at % 4 * rows, 2 * rows), :] = made.astype(bf16)
    step = width // 4
    for at in range(0, width, step):
        here = pl.ds(at, step)
        left = jnp.concatenate([ref[:, here] for ref in two])
        made = tn(left, grad_ref[...])
        left = jnp.concatenate([ref[:, here] for ref in cot])
        made = jnp.concatenate([made, tn(left, hidden_ref[...])], axis=1)
        if len(made_refs) == 1:
            made_refs[0][here, :] = made.astype(bf16)
        else:
            put_shares(made, places[Y], at // (2 * made_refs[0].shape[1]), *made_refs)


def feed_rest(places, two, cot, hidden, grads, weights, shares):
    rows, width = two[0].shape
    outs = [((4 * rows, width), bf16)] * 2 + [(shape, bf16) for shape in shares]
    made = call(
        feed_rest_kernel,
        "feed_rest",
        outs,
        places,
        *two,
        *cot,
        hidden,
        grads,
        weights,
        mib=24,
        flops=64 * rows * width * (weights.shape[1] // 3),
    )
    return made[:2], made[2:]


def chip_sums_kernel(places, a_ref, b_ref, *outs):
    rows = outs[0].shape[0]
    for at, ref in enumerate(outs):
        here = pl.ds(at * rows, rows)
        ref[...] = (a_ref[here, :].astype(f32) + b_ref[here, :].astype(f32)).astype(bf16)


def chip_sums(places, here, there):
    shape = (here.shape[0] // 4, here.shape[1])
    return call(chip_sums_kernel, "chip_sums", [(shape, bf16)] * 4, places, here, partner(there, "c"))


def far_sums_kernel(places, kept_ref, across_ref, six_ref, four_ref):
    rows = six_ref.shape[0]
    for at, ref in enumerate((six_ref, four_ref)):
        here = pl.ds(at * rows, rows)
        ref[...] = (kept_ref[here, :].astype(f32) + across_ref[here, :].astype(f32)).astype(bf16)


def near_sums_kernel(places, kept_ref, across_ref, four_ref, both_ref, two_ref, own_ref, out_ref):
    far_sums_kernel(places, kept_ref, across_ref, two_ref, own_ref)
    out_ref[...] = (four_ref[...].astype(f32) + both_ref[...].astype(f32)).astype(bf16)


def result_kernel(places, middle_ref, a_ref, b_ref, c_ref, d_ref, kept_ref, sent_ref):
    total = middle_ref[...]
    for ref in (a_ref, b_ref, c_ref, d_ref):
        total = total + ref[...].astype(f32)
    total = total.astype(bf16)
    half = kept_ref.shape[0]
    kept_ref[...] = total[:half]
    sent_ref[...] = total[half:]


def middle_back_kernel(
    places, middle_ref, cot_ref, weight_ref, a_ref, b_ref, c_ref, d_ref, grad_ref, low_ref, leaving_ref
):
    scaled = a_ref[...].astype(f32)
    for ref in (b_ref, c_ref, d_ref):
        scaled = scaled + ref[...].astype(f32)
    normed, inverse = normalize(middle_ref[...])
    grad = cot_ref[...].astype(f32) + normalize_back(scaled, normed, inverse)
    grad_ref[...] = grad
    low = grad.astype(bf16)
    low_ref[...] = low
    made = nt(low, weight_ref[...]).astype(bf16)
    wide = leaving_ref.shape[2]
    for at in range(leaving_ref.shape[0]):
        leaving_ref[at] = made[:, at * wide : (at + 1) * wide]


def outer_kernel(places, left_ref, right_ref, *made_refs):
    made = tn(left_ref[...], right_ref[...])
    if len(made_refs) == 1:
        made_refs[0][...] = made.astype(bf16)
    else:
        put_shares(made, places[C], 0, *made_refs)


def project_back_kernel(places, grad_ref, weight_ref, *outs):
    rows = outs[0].shape[0] // 2
    for at in (6, 4, 2, 0):
        made = nt(grad_ref[pl.ds(at * rows, 2 * rows), :], weight_ref[...]).astype(bf16)
        first = 0 if at >= 4 else 2
        here = pl.ds((0 if at in (6, 2) else 1) * rows, rows)
        outs[first][here, :] = made[:rows]
        outs[first + 1][here, :] = made[rows:]


def project_outer_kernel(places, left_ref, grad_ref, *made_refs):
    width = left_ref.shape[1]
    step = width // 4
    for at in range(0, width, step):
        made = tn(left_ref[:, pl.ds(at, step)], grad_ref[...])
        if len(made_refs) == 1:
            made_refs[0][pl.ds(at, step), :] = made.astype(bf16)
        else:
            put_shares(made, places[C], at // (2 * made_refs[0].shape[1]), *made_refs)


def tokens_back_kernel(places, tokens_ref, grad_ref, a_ref, b_ref, c_ref, kept_ref, sent_ref):
    scaled = a_ref[...].astype(f32)
    for ref in (b_ref, c_ref):
        scaled = scaled + ref[...].astype(f32)
    normed, inverse = normalize(tokens_ref[...].astype(f32))
    total = grad_ref[...] + normalize_back(scaled, normed, inverse)
    half = kept_ref.shape[0]
    kept_ref[...] = total[:half]
    sent_ref[...] = total[half:]


def columns_by(array, pieces, piece):
    rows, count = array.shape
    padded = jnp.pad(array, ((0, 0), (0, pieces * piece - count)))
    return jnp.swapaxes(padded.reshape(rows, pieces, piece), 0, 1)


def columns_back(array, count):
    pieces, rows, piece = array.shape
    return jnp.swapaxes(array, 0, 1).reshape(rows, pieces * piece)[:, :count]


def body(inputs, gain_attn, gain_mlp, w_qkv, w_attn_out, w_in, w_out, cotangent):
    pairs, squares = 8, 8
    rings = lax.axis_size("r")
    seqs, half_block, width = inputs.shape
    owned = w_qkv.shape[0]
    size = width // HEADS
    half = size // 2
    wide = width // pairs
    block = seqs * half_block
    span = pairs * block
    ff = w_out.shape[0]
    piece = -(-ff // (squares * LANES)) * LANES
    chips, square = ("zh", "zl", "x"), ("zl", "x", "c")
    ri, zh, zl, xi, ci, yi = (lax.axis_index(name) for name in ("r", "zh", "zl", "x", "c", "y"))
    places = jnp.stack([4 * zh + 2 * zl + xi, zh, zl, xi, ci, yi]).astype(jnp.int32)
    block_low, half_low = ((block, width), bf16), ((half_block, width), bf16)
    block_full, half_full = ((block, width), f32), ((half_block, width), f32)

    def over_rings(array):
        return lax.all_gather(array, "r", axis=0) if rings > 1 else array

    def ring_sums(array):
        if rings > 1:
            return lax.psum_scatter(array, "r", scatter_dimension=0, tiled=True)
        return array

    gain_one = gain_attn.astype(f32)[:, None]
    gain_two = gain_mlp.astype(f32)[:, None]


    tokens, cot, low_one = call(
        enter_kernel,
        "enter",
        [block_low] * 3,
        places,
        inputs,
        partner(inputs, "c"),
        cotangent,
        partner(cotangent, "c"),
    )
    scaled_qkv = (w_qkv.astype(f32) * gain_one).astype(bf16)
    slices = scaled_qkv.reshape(owned, 3, pairs, wide).transpose(2, 0, 1, 3)
    live = {"tokens": tokens, "cot": cot, "one0": low_one}
    live |= {"slices": slices.reshape(pairs, owned, 3 * wide), "attn": w_attn_out}
    live |= {"in": w_in, "out": w_out, "places": places}
    live = fence(live)

    one4 = partner(live["one0"], "zh")
    one2 = partner(live["one0"], "zl")
    one1 = partner(live["one0"], "x")
    cot_x = partner(live["cot"], "x")
    qkv = lax.all_to_all(live.pop("slices"), chips, 0, 0, tiled=True)[:, None]
    full = live.pop("attn")
    full = jnp.stack([full, partner(full, "y")])
    scaled_in = (live.pop("in").astype(f32) * gain_two).astype(bf16)
    packed = jnp.concatenate(
        [
            columns_by(scaled_in[:, :ff], squares, piece),
            columns_by(scaled_in[:, ff:], squares, piece),
            columns_by(jnp.transpose(live.pop("out")), squares, piece),
        ],
        axis=2,
    )
    live |= {"one1": one1, "one2": one2, "one4": one4, "full": full, "packed": packed}
    live["cot_x"] = cot_x
    live = fence(live)

    places = live["places"]
    one6 = partner(live["one4"], "zl")
    one5 = partner(live["one4"], "x")
    one3 = partner(live["one2"], "x")
    packed = lax.all_to_all(live.pop("packed"), square, 0, 0, tiled=True)[None]
    full = live.pop("full")
    full = jnp.stack([full, partner(full, "zh")])
    lane = jnp.arange(wide, dtype=jnp.int32)
    frequency = rope_base ** (-2.0 * (lane % half).astype(f32) / size)
    sign = jnp.where(lane % size < half, -1.0, 1.0)
    row = jnp.arange(span, dtype=jnp.int32)
    at = (places[CHIP] ^ (row // block)) * block + (places[C] ^ (row % block // half_block)) * half_block
    at = ri * span + at + row % half_block
    angles = at.astype(f32)[:, None] * frequency[None, :]
    table = jnp.concatenate([jnp.cos(angles), jnp.sin(angles) * sign], axis=1)
    live |= {"one3": one3, "one5": one5, "one6": one6, "qkv": qkv, "table": table, "full": full}
    live["packed"] = packed
    live = fence(live)

    one7 = partner(live["one6"], "x")
    qkv = live.pop("qkv")
    qkv = [qkv, partner(qkv, "y")]
    qkv = qkv + [partner(member, "c") for member in qkv]
    cot_z = partner(live["cot"], "zl")
    full = live.pop("full")
    full = jnp.stack([full, partner(full, "zl")], axis=1)
    pair_qkv = over_rings(assemble(places, None, C, Y, qkv)).reshape(width, 3 * wide)
    live |= {"one7": one7, "qkv": pair_qkv, "full": full}
    live = fence(live)

    full_x = partner(live["full"], "x")
    packed_far = partner(live["packed"], "zh")
    packed_y = partner(live["packed"], "y")
    projected, all_one = call(
        functools.partial(project_kernel, half),
        "project",
        [((span, 3 * wide), bf16), ((span, width), bf16)],
        places,
        *[live.pop(f"one{j}") for j in range(8)],
        live["qkv"],
        live["table"],
        flops=6 * span * width * wide,
    )
    projected = [projected]
    if rings > 1:
        projected += [lax.all_gather(projected[0][:, wide:], "r", axis=0, tiled=True)]
    count = projected[-1].shape[0]
    step = 2 * block if count <= 2048 else block
    heads_out, logs = call(
        functools.partial(attend_kernel, size),
        "attend",
        [((pairs, block, wide), bf16), ((span // step, 8, step), f32)],
        places,
        *projected,
        mib=24,
        flops=16 * span * count * wide,
        exps=2 * span * count,
    )
    live |= {"heads": heads_out, "full_x": full_x, "cot_z": cot_z}
    live = fence(live)

    arrived = lax.all_to_all(live.pop("heads"), chips, 0, 0, tiled=True)
    cot_zx = partner(live["cot_z"], "x")
    full = [member.reshape(4, 2, owned, width) for member in (live.pop("full"), live.pop("full_x"))]
    full = full + [partner(member, "c") for member in full]
    full_attn = over_rings(assemble_rows(places, full)).reshape(width, width)
    live |= {"arrived": arrived, "attn": full_attn}
    live |= {"far": packed_far, "packed_y": packed_y, "cot_zx": cot_zx}
    live = fence(live)

    far_y = partner(live["far"], "y")
    attended, middle, low_two = call(
        middle_kernel,
        "middle",
        [block_low, block_full, block_low],
        places,
        live.pop("arrived"),
        live["attn"],
        live["tokens"],
        flops=2 * block * width * width,
    )
    live |= {"attended": attended, "middle": middle, "two": low_two}
    live = fence(live)

    over_x = partner(live["two"], "x")
    over_z = partner(live["two"], "zl")
    over_both = opposite(live["two"], ("zl", "x"))
    all_cotangent = [live[name] for name in ("cot", "cot_x", "cot_z", "cot_zx")]
    all_cotangent += [partner(member, "c") for member in all_cotangent]
    packed = [live.pop("packed"), live.pop("packed_y"), live.pop("far"), far_y]
    weights = assemble(places, None, ZH, Y, packed)
    live["weights"] = over_rings(weights).reshape(width, 3 * piece)
    live |= {"over_x": over_x, "over_z": over_z, "over_both": over_both}
    live = fence(live)

    all_two = [live.pop(name) for name in ("two", "over_x", "over_z", "over_both")]
    all_two += [partner(member, "c") for member in all_two]
    hidden, grad_gate_up, terms = feed(places, all_two, all_cotangent, live["weights"])
    live |= {"hidden": hidden, "gate_up": grad_gate_up}
    live |= {"here": terms[0], "there": terms[1]}
    live = fence(live)

    sums = chip_sums(places, live.pop("here"), live.pop("there"))
    live |= {f"sum{j}": member for j, member in enumerate(sums)}
    live = fence(live)

    sums = [live.pop(f"sum{j}") for j in range(4)]
    over_both = opposite(sums[3], ("zl", "x"))
    over_x = partner(sums[1], "x")
    over_z = partner(sums[2], "zl")
    direct = rings == 1 and owned % 16 == 0
    shape = (2 * squares, owned, 3 * piece)
    result, shares = feed_rest(
        places,
        all_two,
        all_cotangent,
        live.pop("hidden"),
        live.pop("gate_up"),
        live.pop("weights"),
        [shape] * 2 if direct else [(width, 3 * piece)],
    )
    if not direct:
        terms = ring_sums(shares[0]).reshape(2 * squares, 2, owned, 3 * piece)
        shares = split(places, Y, [terms], 1)
    weights_kept, weights_y = shares[0], partner(shares[1], "y")
    live |= {"result_here": result[0], "result_there": result[1]}
    live |= {f"sum{j}": m for j, m in enumerate([sums[0], over_x, over_z, over_both])}
    live["weights_kept"] = weights_kept
    live = fence(live)

    grad_middle, grad_branch, leaving = call(
        middle_back_kernel,
        "middle_back",
        [block_full, block_low, ((pairs, block, wide), bf16)],
        places,
        live["middle"],
        live.pop("cot"),
        live.pop("attn"),
        *[live.pop(f"sum{j}") for j in range(4)],
        flops=2 * block * width * width,
    )
    live |= {"grad_middle": grad_middle, "branch": grad_branch, "leaving": leaving}
    live = fence(live)

    grad_heads = lax.all_to_all(live.pop("leaving"), chips, 0, 0, tiled=True)
    result = chip_sums(places, live.pop("result_here"), live.pop("result_there"))
    result_both = opposite(result[3], ("zl", "x"))
    result_x = partner(result[1], "x")
    result_z = partner(result[2], "zl")
    live["result0"] = result[0]
    shape = (pairs, 2 * owned, width)
    shares = call(
        outer_kernel,
        "outer",
        [(shape, bf16)] * 2 if direct else [((width, width), bf16)],
        places,
        live.pop("attended"),
        live.pop("branch"),
        flops=2 * block * width * width,
    )
    if not direct:
        shares = split(places, C, [ring_sums(shares[0]).reshape(pairs, 2, 2 * owned, width)], 1)
    shares = [shares[0], partner(shares[1], "c")]
    shares = [share.reshape(8, 2, owned, width) for share in shares]
    live["attn_kept"], live["attn_sent"] = split(places, Y, shares, 1)
    live |= {"grad_heads": grad_heads, "weights_y": weights_y}
    live = fence(live)

    attn_y = partner(live.pop("attn_sent"), "y")
    kernel = functools.partial(attend_back_kernel, size, rings == 1)
    parts = projected + [live.pop("grad_heads"), logs, live["table"]]
    if rings == 1:
        grad_projected = call(
            kernel,
            "attend_back",
            [((span, 3 * wide), bf16)],
            places,
            *parts,
            scratch=[pltpu.VMEM((count, wide), f32)] * 2,
            mib=24,
            flops=40 * span * count * wide,
            exps=2 * span * count,
        )[0]
    else:
        outs = [((span, wide), bf16), ((count, wide), f32), ((count, wide), f32)]
        grad_q, grad_k, grad_v = call(kernel, "attend_back", outs, places, *parts, mib=36)
        grad_projected = call(
            functools.partial(turn_back_kernel, half),
            "turn_back",
            [((span, 3 * wide), bf16)],
            places,
            grad_q,
            ring_sums(grad_k),
            ring_sums(grad_v),
            live["table"],
        )[0]
    terms = call(
        project_back_kernel,
        "project_back",
        [((2 * block, width), bf16)] * 4,
        places,
        grad_projected,
        live["qkv"],
        flops=6 * span * width * wide,
    )
    live |= dict(zip(("kept_far", "sent_far", "kept_near", "sent_near"), terms))
    live["projected"] = grad_projected
    live |= {"result_x": result_x, "result_z": result_z, "result_both": result_both}
    live["attn_y"] = attn_y
    live = fence(live)

    over_x = partner(live.pop("sent_far"), "x")
    shares = [live.pop("weights_kept"), live.pop("weights_y")]
    shares = [share.reshape(1, 2, squares * owned, 3 * piece) for share in shares]
    live["weights_kept"], sent = split(places, ZH, shares, 1)
    weights_far = partner(sent, "zh")
    shape = (pairs, 2 * owned, 3 * wide)
    shares = call(
        project_outer_kernel,
        "project_outer",
        [(shape, bf16)] * 2 if direct else [((width, 3 * wide), bf16)],
        places,
        all_one,
        live.pop("projected"),
        flops=6 * span * width * wide,
    )
    if not direct:
        shares = split(places, C, [ring_sums(shares[0]).reshape(pairs, 2, 2 * owned, 3 * wide)], 1)
    shares = [shares[0], partner(shares[1], "c")]
    shares = [share.reshape(pairs, 2, owned, 3 * wide) for share in shares]
    live["qkv_kept"], live["qkv_sent"] = split(places, Y, shares, 1)
    shares = [share.reshape(2, 2, 2 * owned, width) for share in (live.pop("attn_kept"), live.pop("attn_y"))]
    live["attn_kept"], sent = split(places, ZL, shares, 1)
    live["attn_zl"] = partner(sent, "zl")
    live["sum6"], live["sum4"] = call(
        far_sums_kernel, "far_sums", [block_low] * 2, places, live.pop("kept_far"), over_x
    )
    live = fence(live)

    both = partner(live.pop("sum6"), "zl")
    over_x = partner(live.pop("sent_near"), "x")
    qkv_y = partner(live.pop("qkv_sent"), "y")
    shares = [share.reshape(2, 2, owned, width) for share in (live.pop("attn_kept"), live.pop("attn_zl"))]
    live["attn_kept"], sent = split(places, X, shares, 1)
    live["attn_x"] = partner(sent, "x")
    live["sum2"], live["sum0"], live["sum4"] = call(
        near_sums_kernel,
        "near_sums",
        [block_low] * 3,
        places,
        live.pop("kept_near"),
        over_x,
        live["sum4"],
        both,
    )
    live["qkv"] = total(places, live.pop("qkv_kept"), qkv_y)
    live = fence(live)

    far = partner(live.pop("sum4"), "zh")
    near = partner(live.pop("sum2"), "zl")
    shares = [share.reshape(squares, owned, 3 * piece) for share in (live.pop("weights_kept"), weights_far)]
    grad_packed = lax.all_to_all(total(places, *shares), square, 0, 0, tiled=True)
    shares = [share.reshape(1, 2, owned, width) for share in (live.pop("attn_kept"), live.pop("attn_x"))]
    kept_attn, sent = split(places, ZH, shares, 1)
    attn_zh = partner(sent, "zh")
    half_result, sent = call(
        result_kernel,
        "result",
        [half_low] * 2,
        places,
        live["middle"],
        live["result0"],
        live["result_x"],
        live["result_z"],
        live["result_both"],
    )
    output = call(
        leave_kernel, "leave", [(inputs.shape, bf16)], places, half_result, partner(sent, "c")
    )[0]
    live |= {"far": far, "near": near, "output": output, "grad_packed": grad_packed}
    live |= {"attn_kept": kept_attn, "attn_zh": attn_zh}
    live = fence(live)
    output, grad_packed = live["output"], live["grad_packed"]
    grad_qkv = lax.all_to_all(live.pop("qkv"), chips, 0, 0, tiled=True)
    grad_attn = (live["attn_kept"].astype(f32) + live["attn_zh"].astype(f32))[0]

    kept, sent = call(
        tokens_back_kernel,
        "tokens_back",
        [half_full] * 2,
        places,
        live["tokens"],
        live["grad_middle"],
        live["sum0"],
        live["near"],
        live["far"],
    )
    input_grad = call(
        leave_kernel, "leave", [(inputs.shape, f32)], places, kept, partner(sent, "c")
    )[0]

    grad_qkv = grad_qkv.astype(f32)
    grad_packed = grad_packed.astype(f32)
    grad_qkv = grad_qkv.reshape(pairs, owned, 3, wide)
    grad_qkv = grad_qkv.transpose(1, 2, 0, 3).reshape(owned, 3 * width)
    grad_gain_attn = jnp.sum(grad_qkv * w_qkv.astype(f32), axis=1)
    grad_qkv = grad_qkv * gain_one

    grad_in = jnp.concatenate(
        [
            columns_back(grad_packed[:, :, :piece], ff),
            columns_back(grad_packed[:, :, piece : 2 * piece], ff),
        ],
        axis=1,
    )
    grad_out = jnp.transpose(columns_back(grad_packed[:, :, 2 * piece :], ff))
    grad_gain_mlp = jnp.sum(grad_in * w_in.astype(f32), axis=1)
    grad_in = grad_in * gain_two
    return (
        output,
        input_grad,
        grad_gain_attn,
        grad_gain_mlp,
        grad_qkv,
        grad_attn,
        grad_in,
        grad_out,
    )


def solution(mesh):
    ctx, fsdp = mesh.shape["ctx"], mesh.shape["fsdp"]
    everyone = ("r", "zh", "zl", "x", "c", "y")
    grid = Mesh(mesh.devices.reshape(ctx // 16, 2, 2, 2, 2, fsdp), everyone)
    tokens = P("y", everyone[:-1], None)
    gain, rows, columns = P(everyone), P(everyone, None), P(None, everyone)
    return jax.shard_map(
        body,
        mesh=grid,
        in_specs=(tokens, gain, gain, rows, rows, rows, columns, tokens),
        out_specs=(tokens, tokens, gain, gain, rows, rows, rows, columns),
        check_vma=False,
    )
```

time: 294 us -> 256 us (0.87)
  waiting for transfers between devices: 98.3 us -> 80.4 us
  local copies, waits for them, and re-layouts: 26.6 us -> 18 us
  other arithmetic: 19.7 us -> 12.2 us
    ppermute x63 -> x56, waiting for transfers between devices: 83.7 us -> 65.9 us  [partner(): return lax.ppermute(array, axis, [(0, 1), (1, 0)])]
    convert_element_type x13 -> x2, other arithmetic: 11.8 us -> 0.21 us  [the longest x1 0.12 us: body(): scaled_in = (live.pop('in').astype(f32) * gain_two).astype(bf16)]
    unnamed x156 -> x92, local copies, waits for them, and re-layouts: 22.6 us -> 13.9 us
    ppermute x63 -> x56, starting transfers between devices: 46.8 us -> 54.3 us  [partner(): return lax.ppermute(array, axis, [(0, 1), (1, 0)])]
    all_to_all x6, starting transfers between devices: 29.1 us -> 22.9 us  [the longest x1 4.21 us: body(): grad_heads = lax.all_to_all(live.pop('leaving'), chips, 0, 0, tiled=True)]
    ppermute x4 -> x3, starting transfers between devices: 7.18 us -> 3 us  [opposite(): return lax.ppermute(array, axes, [(i, 3 - i) for i in range(4)])]
    pallas_call x28 -> x30, Pallas kernels: 62.6 us -> 62.4 us  [call(): pl.pallas_call(kernel, in_specs=[pl.BlockSpec(memory_space=pltpu.SMEM)] +...]
    ppermute x4 -> x3, waiting for transfers between devices: 10.6 us -> 10.9 us  [opposite(): return lax.ppermute(array, axes, [(i, 3 - i) for i in range(4)])]
  transfers between devices with their start and end apart: 73 -> 65, of which waited for: 23 -> 29; matrix products, arithmetic and copies ran while one was open for 7% -> 5% of each run, Pallas kernels for 19% -> 21%
where the time goes in v3:
time: 256 us; the launch traced here: 255 us
  waiting for transfers between devices  80.4 us (31%)
  starting transfers between devices  80.2 us (31%)
  Pallas kernels  62.4 us (24%)
  local copies, waits for them, and re-layouts  18 us (7%)
  other arithmetic  12.2 us (5%)
    ppermute x56, waiting for transfers between devices, partner(): return lax.ppermute(array, axis, [(0, 1), (1, 0)])  65.9 us
    pallas_call x30, Pallas kernels, call(): pl.pallas_call(kernel, in_specs=[pl.BlockSpec(memory_space=pltpu.SMEM)] +...  62.4 us
    ppermute x56, starting transfers between devices, partner(): return lax.ppermute(array, axis, [(0, 1), (1, 0)])  54.3 us
    unnamed x92, local copies, waits for them, and re-layouts  13.9 us
    ppermute x3, waiting for transfers between devices, opposite(): return lax.ppermute(array, axes, [(i, 3 - i) for i in range(4)])  10.9 us
  transfers between devices with their start and end apart: 65, of which 29 were waited for; matrix products, arithmetic and copies ran while one was open for 5% of the time, Pallas kernels for 21%

profile of v3, /device:TPU:0, one launch (start us, length us, event | category | flops | bytes accessed | tf_op | source)
XLA Modules:
  0.0 254.7 jit_solution(6997379825656901913)
XLA Ops:
  6.2 4.0 %collective-permute-start.4 = (bf16[128,1024]{1,0:T(8,128)(2,1)S(1)}, bf16[128,1024]{1,0:T(8,128)(2,1)S(1)}, u32[]{:S(2)}, u32[]{:S(2)}) collective-permute-start(bf16[128,1024]{1,0:T(8,128)(2,1)S(1)} %get-tuple-element.321.refs_0_), channel_id=1, source_target_pairs={{0,16},{16,0},{1,17},{17,1},{2,18},{18,2},{3,19},{19,3},{4,20},{20... | collective-permute-start | bytes 786440 | tf_op jit(solution)/shard_map/ppermute | solution.py:22
  13.3 3.4 %all-to-all-start = ((bf16[8,32,384]{2,1,0:T(8,128)(2,1)}), bf16[8,32,384]{2,1,0:T(8,128)(2,1)S(1)}, u32[]{:S(2)}, u32[]{:S(2)}) async-start(bf16[8,32,384]{2,1,0:T(8,128)(2,1)} %reshape.182), calls=%async_computation | async-start | bytes 393216 | tf_op jit(solution)/shard_map/all_to_all | solution.py:557
  18.3 1.8 collective-permute-start.6
  21.5 5.6 %collective-permute-done.6.refs_9_ = bf16[128,1024]{1,0:T(8,128)(2,1)S(1)} collective-permute-done((bf16[128,1024]{1,0:T(8,128)(2,1)S(1)}, bf16[128,1024]{1,0:T(8,128)(2,1)S(1)}, u32[]{:S(2)}, u32[]{:S(2)}) %collective-permute-start.6) | collective-permute-done | bytes 262176 | tf_op jit(solution)/shard_map/ppermute | solution.py:22
  27.4 4.2 %all-to-all-start.1 = ((bf16[8,32,1152]{2,1,0:T(8,128)(2,1)}), bf16[8,32,1152]{2,1,0:T(8,128)(2,1)}, u32[]{:S(2)}, u32[]{:S(2)}) async-start(bf16[8,32,1152]{2,1,0:T(8,128)(2,1)} %pad_maximum_fusion.2), calls=%async_computation.1 | async-start | bytes 1179648 | tf_op jit(solution)/shard_map/all_to_all | solution.py:577
  31.6 2.0 collective-permute-start.9
  35.0 2.5 collective-permute-start.10
  39.9 1.9 multiply_cosine_fusion
  41.9 5.4 %collective-permute-done.10 = bf16[2,32,1024]{2,1,0:T(8,128)(2,1)S(1)} collective-permute-done((bf16[2,32,1024]{2,1,0:T(8,128)(2,1)S(1)}, bf16[2,32,1024]{2,1,0:T(8,128)(2,1)S(1)}, u32[]{:S(2)}, u32[]{:S(2)}) %collective-permute-start.10) | collective-permute-done | bytes 131104 | tf_op jit(solution)/shard_map/ppermute | solution.py:22
  48.1 4.2 %collective-permute-done.7.refs_3_ = bf16[128,1024]{1,0:T(8,128)(2,1)S(1)} collective-permute-done((bf16[128,1024]{1,0:T(8,128)(2,1)S(1)}, bf16[128,1024]{1,0:T(8,128)(2,1)S(1)}, u32[]{:S(2)}, u32[]{:S(2)}) %collective-permute-start.7) | collective-permute-done | bytes 262176 | tf_op jit(solution)/shard_map/ppermute | solution.py:22
  55.9 2.9 %collective-permute-done.12.b_ref = bf16[8,1,32,384]{3,2,1,0:T(8,128)(2,1)S(1)} collective-permute-done((bf16[8,1,32,384]{3,2,1,0:T(8,128)(2,1)S(1)}, bf16[8,1,32,384]{3,2,1,0:T(8,128)(2,1)S(1)}, u32[]{:S(2)}, u32[]{:S(2)}) %collective-permute-start.12) | collective-permute-done | bytes 196640 | tf_op jit(solution)/shard_map/ppermute | solution.py:22
  58.7 2.9 %collective-permute-done.15 = bf16[2,2,32,1024]{3,2,1,0:T(8,128)(2,1)S(1)} collective-permute-done((bf16[2,2,32,1024]{3,2,1,0:T(8,128)(2,1)}, bf16[2,2,32,1024]{3,2,1,0:T(8,128)(2,1)S(1)}, u32[]{:S(2)}, u32[]{:S(2)}) %collective-permute-start.15) | collective-permute-done | bytes 262176 | tf_op jit(solution)/shard_map/ppermute | solution.py:22
  63.9 1.7 collective-permute-start.17
  66.1 2.5 collective-permute-start.20
  68.5 2.0 project.1
  71.8 7.8 %attend.1 = (bf16[8,128,128]{2,1,0:T(8,128)(2,1)S(1)}, f32[4,8,256]{2,1,0:T(8,128)S(1)}) custom-call(s32[6]{0:T(128)S(1)} %stack.54.places, bf16[1024,384]{1,0:T(8,128)(2,1)S(1)} %get-tuple-element.329.refs_0_), custom_call_target="tpu_custom_call" | custom-call | flops 2147483648 | bytes 1081344 | tf_op jit(solution)/shard_map/attend/pallas_call | solution.py:48
  80.4 3.6 %all-to-all-start.2 = ((bf16[8,128,128]{2,1,0:T(8,128)(2,1)}), bf16[8,128,128]{2,1,0:T(8,128)(2,1)S(1)}, u32[]{:S(2)}, u32[]{:S(2)}) async-start(bf16[8,128,128]{2,1,0:T(8,128)(2,1)} %copy-done.24), calls=%async_computation.2 | async-start | bytes 524288 | tf_op jit(solution)/shard_map/all_to_all | solution.py:634
  84.0 1.7 collective-permute-start.22
  92.3 5.1 %collective-permute-done.20.c_ref = bf16[1,8,32,1152]{3,2,1,0:T(8,128)(2,1)} collective-permute-done((bf16[1,8,32,1152]{3,2,1,0:T(8,128)(2,1)}, bf16[1,8,32,1152]{3,2,1,0:T(8,128)(2,1)}, u32[]{:S(2)}, u32[]{:S(2)}) %collective-permute-start.20) | collective-permute-done | bytes 589856 | tf_op jit(solution)/shard_map/ppermute | solution.py:22
  102.8 2.2 collective-permute-start.25
  105.8 6.2 %collective-permute-done.26.refs_3_ = bf16[128,1024]{1,0:T(8,128)(2,1)S(1)} collective-permute-done((bf16[128,1024]{1,0:T(8,128)(2,1)S(1)}, bf16[128,1024]{1,0:T(8,128)(2,1)S(1)}, u32[]{:S(2)}, u32[]{:S(2)}) %collective-permute-start.26) | collective-permute-done | bytes 262176 | tf_op jit(solution)/shard_map/ppermute | solution.py:26
  117.4 6.3 %feed.1 = (bf16[1024,384]{1,0:T(8,128)(2,1)S(1)}, bf16[1024,768]{1,0:T(8,128)(2,1)S(1)}, bf16[512,1024]{1,0:T(8,128)(2,1)S(1)}, bf16[512,1024]{1,0:T(8,128)(2,1)S(1)}) custom-call(s32[6]{0:T(128)S(1)} %stack.54.places, bf16[128,1024]{1,0:T(8,128)(2,1)S(1)} %get-tuple-element.378.refs_0_, bf16[128,1024]{1,0:T(8,128)(2,1)S(1)} %collective-permute-done.24.refs_1_, ...), custom_call_target="tpu_custom_call" | custom-call | flops 4026531840 | bytes 11010048 | tf_op jit(solution)/shard_map/feed/pallas_call | solution.py:48
  124.0 2.5 collective-permute-done.35.b_ref
  128.3 2.5 collective-permute-start.38
  130.8 6.0 %feed_rest.1 = (bf16[512,1024]{1,0:T(8,128)(2,1)S(1)}, bf16[512,1024]{1,0:T(8,128)(2,1)}, bf16[16,32,1152]{2,1,0:T(8,128)(2,1)S(1)}, bf16[16,32,1152]{2,1,0:T(8,128)(2,1)}) custom-call(s32[6]{0:T(128)S(1)} %stack.54.places, bf16[128,1024]{1,0:T(8,128)(2,1)S(1)} %get-tuple-element.378.refs_0_, bf16[128,1024]{1,0:T(8,128)(2,1)S(1)} %collective-permute-done.24.refs_1_, ...), custom_call_target="tpu_custom_call" | custom-call | flops 3221225472 | bytes 13369344 | tf_op jit(solution)/shard_map/feed_rest/pallas_call | solution.py:48
  137.9 4.6 %collective-permute-done.38.d_ref = bf16[128,1024]{1,0:T(8,128)(2,1)S(1)} collective-permute-done((bf16[128,1024]{1,0:T(8,128)(2,1)S(1)}, bf16[128,1024]{1,0:T(8,128)(2,1)S(1)}, u32[]{:S(2)}, u32[]{:S(2)}) %collective-permute-start.38) | collective-permute-done | bytes 262176 | tf_op jit(solution)/shard_map/ppermute | solution.py:26
  142.5 1.7 middle_back.1
  145.1 2.5 outer.1
  148.1 4.2 %all-to-all-start.3 = ((bf16[8,128,128]{2,1,0:T(8,128)(2,1)}), bf16[8,128,128]{2,1,0:T(8,128)(2,1)S(1)}, u32[]{:S(2)}, u32[]{:S(2)}) async-start(bf16[8,128,128]{2,1,0:T(8,128)(2,1)} %copy-done.23), calls=%async_computation.3 | async-start | bytes 524288 | tf_op jit(solution)/shard_map/all_to_all | solution.py:717
  152.4 2.2 chip_sums.3
  155.2 2.0 collective-permute-start.42
  161.8 2.6 %collective-permute-done.41 = bf16[16,32,1152]{2,1,0:T(8,128)(2,1)} collective-permute-done((bf16[16,32,1152]{2,1,0:T(8,128)(2,1)}, bf16[16,32,1152]{2,1,0:T(8,128)(2,1)}, u32[]{:S(2)}, u32[]{:S(2)}) %collective-permute-start.41) | collective-permute-done | bytes 1179680 | tf_op jit(solution)/shard_map/ppermute | solution.py:22
  166.7 9.3 %attend_back.1.grad_ref = bf16[1024,384]{1,0:T(8,128)(2,1)S(1)} custom-call(s32[6]{0:T(128)S(1)} %stack.54.places, bf16[1024,384]{1,0:T(8,128)(2,1)S(1)} %copy-done.32, bf16[8,128,128]{2,1,0:T(8,128)(2,1)S(1)} %all-to-all-done.3.refs_1_, f32[4,8,256]{2,1,0:T(8,128)S(1)} %get-tuple-element.463.refs_2_, f32[1024,256]{1,0:T(8,128)S(1)} %pad_maximum_fusion.refs_9_.refs_3_), custom_call_target="tpu_custom_call" | custom-call | flops 5368709120 | bytes 2916352 | tf_op jit(solution)/shard_map/attend_back/pallas_call | solution.py:48
  176.0 1.8 project_back.1
  178.8 1.9 project_outer.1
  183.3 3.0 %collective-permute-start.56 = (bf16[1,256,1152]{2,1,0:T(8,128)(2,1)S(1)}, bf16[1,256,1152]{2,1,0:T(8,128)(2,1)S(1)}, u32[]{:S(2)}, u32[]{:S(2)}) collective-permute-start(bf16[1,256,1152]{2,1,0:T(8,128)(2,1)S(1)} %get-tuple-element.533), channel_id=1, source_target_pairs={{0,16},{16,0},{1,17},{17,1},{2,18},{18,2},{3,19},{19,3},{4,20},{20... | collective-permute-start | bytes 1769480 | tf_op jit(solution)/shard_map/ppermute | solution.py:22
  186.9 3.2 %collective-permute-done.48.across_ref = bf16[256,1024]{1,0:T(8,128)(2,1)S(1)} collective-permute-done((bf16[256,1024]{1,0:T(8,128)(2,1)S(1)}, bf16[256,1024]{1,0:T(8,128)(2,1)S(1)}, u32[]{:S(2)}, u32[]{:S(2)}) %collective-permute-start.48) | collective-permute-done | bytes 524320 | tf_op jit(solution)/shard_map/ppermute | solution.py:22
  190.8 3.2 %collective-permute-done.47 = bf16[2,64,1024]{2,1,0:T(8,128)(2,1)S(1)} collective-permute-done((bf16[2,64,1024]{2,1,0:T(8,128)(2,1)S(1)}, bf16[2,64,1024]{2,1,0:T(8,128)(2,1)S(1)}, u32[]{:S(2)}, u32[]{:S(2)}) %collective-permute-start.47) | collective-permute-done | bytes 262176 | tf_op jit(solution)/shard_map/ppermute | solution.py:22
  197.7 3.7 %collective-permute-done.49.b_ref = bf16[8,32,384]{2,1,0:T(8,128)(2,1)S(1)} collective-permute-done((bf16[8,32,384]{2,1,0:T(8,128)(2,1)S(1)}, bf16[8,32,384]{2,1,0:T(8,128)(2,1)S(1)}, u32[]{:S(2)}, u32[]{:S(2)}) %collective-permute-start.49) | collective-permute-done | bytes 196640 | tf_op jit(solution)/shard_map/ppermute | solution.py:22
  202.7 3.6 %collective-permute-done.51.both_ref = bf16[128,1024]{1,0:T(8,128)(2,1)S(1)} collective-permute-done((bf16[128,1024]{1,0:T(8,128)(2,1)S(1)}, bf16[128,1024]{1,0:T(8,128)(2,1)S(1)}, u32[]{:S(2)}, u32[]{:S(2)}) %collective-permute-start.51) | collective-permute-done | bytes 262176 | tf_op jit(solution)/shard_map/ppermute | solution.py:22
  206.3 2.5 collective-permute-done.50.across_ref
  210.3 2.4 collective-permute-done.56
  214.2 3.5 %all-to-all-start.4 = ((bf16[8,32,1152]{2,1,0:T(8,128)(2,1)}), bf16[8,32,1152]{2,1,0:T(8,128)(2,1)S(1)}, u32[]{:S(2)}, u32[]{:S(2)}) async-start(bf16[8,32,1152]{2,1,0:T(8,128)(2,1)} %total.3), calls=%async_computation.4 | async-start | bytes 1179648 | tf_op jit(solution)/shard_map/all_to_all | solution.py:834
  218.9 1.9 collective-permute-start.54
  222.8 1.8 collective-permute-start.57
  225.9 11.9 %collective-permute-done.57 = bf16[1,32,1024]{2,1,0:T(8,128)(2,1)S(1)} collective-permute-done((bf16[1,32,1024]{2,1,0:T(8,128)(2,1)S(1)}, bf16[1,32,1024]{2,1,0:T(8,128)(2,1)S(1)}, u32[]{:S(2)}, u32[]{:S(2)}) %collective-permute-start.57) | collective-permute-done | bytes 65568 | tf_op jit(solution)/shard_map/ppermute | solution.py:22
  237.8 2.0 collective-permute-done.54.b_ref
  239.8 4.0 %all-to-all-start.5 = ((bf16[8,32,384]{2,1,0:T(8,128)(2,1)}), bf16[8,32,384]{2,1,0:T(8,128)(2,1)}, u32[]{:S(2)}, u32[]{:S(2)}) async-start(bf16[8,32,384]{2,1,0:T(8,128)(2,1)} %total.2), calls=%async_computation.5 | async-start | bytes 393216 | tf_op jit(solution)/shard_map/all_to_all | solution.py:856
  (240 shorter events, 82.9 us)
Async XLA Ops:
  6.2 20.8 %collective-permute-start.4 = (bf16[128,1024]{1,0:T(8,128)(2,1)S(1)}, bf16[128,1024]{1,0:T(8,128)(2,1)S(1)}, u32[]{:S(2)}, u32[]{:S(2)}) collective-permute-start(bf16[128,1024]{1,0:T(8,128)(2,1)S(1)} %get-tuple-element.321.refs_0_), channel_id=1, source_target_pairs={{0,16},{16,0},{1,17},{17,1},{2,18},{18,2},{3,19},{19,3},{4,20},{20... | collective-permute-start | bytes 786440 | tf_op jit(solution)/shard_map/ppermute | solution.py:22
  10.3 16.8 %collective-permute-start.3 = (bf16[128,1024]{1,0:T(8,128)(2,1)S(1)}, bf16[128,1024]{1,0:T(8,128)(2,1)S(1)}, u32[]{:S(2)}, u32[]{:S(2)}) collective-permute-start(bf16[128,1024]{1,0:T(8,128)(2,1)S(1)} %get-tuple-element.321.refs_0_), channel_id=1, source_target_pairs={{0,8},{8,0},{1,9},{9,1},{2,10},{10,2},{3,11},{11,3},{4,12},{12,4},... | collective-permute-start | bytes 786440 | tf_op jit(solution)/shard_map/ppermute | solution.py:22
  11.8 15.2 %collective-permute-start.2 = (bf16[128,1024]{1,0:T(8,128)(2,1)S(1)}, bf16[128,1024]{1,0:T(8,128)(2,1)S(1)}, u32[]{:S(2)}, u32[]{:S(2)}) collective-permute-start(bf16[128,1024]{1,0:T(8,128)(2,1)S(1)} %get-tuple-element.321.refs_0_), channel_id=1, source_target_pairs={{0,4},{4,0},{1,5},{5,1},{2,6},{6,2},{3,7},{7,3},{8,12},{12,8},{9,1... | collective-permute-start | bytes 786440 | tf_op jit(solution)/shard_map/ppermute | solution.py:22
  13.3 14.0 %all-to-all-start = ((bf16[8,32,384]{2,1,0:T(8,128)(2,1)}), bf16[8,32,384]{2,1,0:T(8,128)(2,1)S(1)}, u32[]{:S(2)}, u32[]{:S(2)}) async-start(bf16[8,32,384]{2,1,0:T(8,128)(2,1)} %reshape.182), calls=%async_computation | async-start | bytes 393216 | tf_op jit(solution)/shard_map/all_to_all | solution.py:557
  18.3 8.7 %collective-permute-start.6 = (bf16[128,1024]{1,0:T(8,128)(2,1)S(1)}, bf16[128,1024]{1,0:T(8,128)(2,1)S(1)}, u32[]{:S(2)}, u32[]{:S(2)}) collective-permute-start(bf16[128,1024]{1,0:T(8,128)(2,1)S(1)} %get-tuple-element.427.refs_8_.cot_ref), channel_id=1, source_target_pairs={{0,4},{4,0},{1,5},{5,1},{2,6},{6,2},{3,7},{7,3},{8,12},{12,8},{9,1... | collective-permute-start | bytes 786440 | tf_op jit(solution)/shard_map/ppermute | solution.py:22
  27.4 24.9 %all-to-all-start.1 = ((bf16[8,32,1152]{2,1,0:T(8,128)(2,1)}), bf16[8,32,1152]{2,1,0:T(8,128)(2,1)}, u32[]{:S(2)}, u32[]{:S(2)}) async-start(bf16[8,32,1152]{2,1,0:T(8,128)(2,1)} %pad_maximum_fusion.2), calls=%async_computation.1 | async-start | bytes 1179648 | tf_op jit(solution)/shard_map/all_to_all | solution.py:577
  31.6 20.6 %collective-permute-start.9 = (bf16[128,1024]{1,0:T(8,128)(2,1)S(1)}, bf16[128,1024]{1,0:T(8,128)(2,1)S(1)}, u32[]{:S(2)}, u32[]{:S(2)}) collective-permute-start(bf16[128,1024]{1,0:T(8,128)(2,1)S(1)} %collective-permute-done.4.refs_4_), channel_id=1, source_target_pairs={{0,8},{8,0},{1,9},{9,1},{2,10},{10,2},{3,11},{11,3},{4,12},{12,4},... | collective-permute-start | bytes 786440 | tf_op jit(solution)/shard_map/ppermute | solution.py:22
  33.6 18.7 %collective-permute-start.8 = (bf16[128,1024]{1,0:T(8,128)(2,1)S(1)}, bf16[128,1024]{1,0:T(8,128)(2,1)S(1)}, u32[]{:S(2)}, u32[]{:S(2)}) collective-permute-start(bf16[128,1024]{1,0:T(8,128)(2,1)S(1)} %collective-permute-done.4.refs_4_), channel_id=1, source_target_pairs={{0,4},{4,0},{1,5},{5,1},{2,6},{6,2},{3,7},{7,3},{8,12},{12,8},{9,1... | collective-permute-start | bytes 786440 | tf_op jit(solution)/shard_map/ppermute | solution.py:22
  35.0 12.3 %collective-permute-start.10 = (bf16[2,32,1024]{2,1,0:T(8,128)(2,1)S(1)}, bf16[2,32,1024]{2,1,0:T(8,128)(2,1)S(1)}, u32[]{:S(2)}, u32[]{:S(2)}) collective-permute-start(bf16[2,32,1024]{2,1,0:T(8,128)(2,1)S(1)} %pad_maximum_fusion.5), channel_id=1, source_target_pairs={{0,16},{16,0},{1,17},{17,1},{2,18},{18,2},{3,19},{19,3},{4,20},{20... | collective-permute-start | bytes 393224 | tf_op jit(solution)/shard_map/ppermute | solution.py:22
  37.5 14.7 %collective-permute-start.7 = (bf16[128,1024]{1,0:T(8,128)(2,1)S(1)}, bf16[128,1024]{1,0:T(8,128)(2,1)S(1)}, u32[]{:S(2)}, u32[]{:S(2)}) collective-permute-start(bf16[128,1024]{1,0:T(8,128)(2,1)S(1)} %collective-permute-done.3.refs_2_), channel_id=1, source_target_pairs={{0,4},{4,0},{1,5},{5,1},{2,6},{6,2},{3,7},{7,3},{8,12},{12,8},{9,1... | collective-permute-start | bytes 786440 | tf_op jit(solution)/shard_map/ppermute | solution.py:22
  52.2 6.5 %collective-permute-start.12 = (bf16[8,1,32,384]{3,2,1,0:T(8,128)(2,1)S(1)}, bf16[8,1,32,384]{3,2,1,0:T(8,128)(2,1)S(1)}, u32[]{:S(2)}, u32[]{:S(2)}) collective-permute-start(bf16[8,1,32,384]{3,2,1,0:T(8,128)(2,1)S(1)} %bitcast.94), channel_id=1, source_target_pairs={{0,1},{1,0},{2,3},{3,2},{4,5},{5,4},{6,7},{7,6},{8,9},{9,8},{10,11... | collective-permute-start | bytes 589832 | tf_op jit(solution)/shard_map/ppermute | solution.py:22
  53.8 7.8 %collective-permute-start.15 = (bf16[2,2,32,1024]{3,2,1,0:T(8,128)(2,1)}, bf16[2,2,32,1024]{3,2,1,0:T(8,128)(2,1)S(1)}, u32[]{:S(2)}, u32[]{:S(2)}) collective-permute-start(bf16[2,2,32,1024]{3,2,1,0:T(8,128)(2,1)} %pad_maximum_fusion.4), channel_id=1, source_target_pairs={{0,8},{8,0},{1,9},{9,1},{2,10},{10,2},{3,11},{11,3},{4,12},{12,4},... | collective-permute-start | bytes 786440 | tf_op jit(solution)/shard_map/ppermute | solution.py:22
  55.3 7.9 %collective-permute-start.11 = (bf16[128,1024]{1,0:T(8,128)(2,1)S(1)}, bf16[128,1024]{1,0:T(8,128)(2,1)S(1)}, u32[]{:S(2)}, u32[]{:S(2)}) collective-permute-start(bf16[128,1024]{1,0:T(8,128)(2,1)S(1)} %collective-permute-done.9.refs_6_), channel_id=1, source_target_pairs={{0,4},{4,0},{1,5},{5,1},{2,6},{6,2},{3,7},{7,3},{8,12},{12,8},{9,1... | collective-permute-start | bytes 786440 | tf_op jit(solution)/shard_map/ppermute | solution.py:22
  55.9 6.7 %collective-permute-start.13 = (bf16[8,1,32,384]{3,2,1,0:T(8,128)(2,1)S(1)}, bf16[8,1,32,384]{3,2,1,0:T(8,128)(2,1)S(1)}, u32[]{:S(2)}, u32[]{:S(2)}) collective-permute-start(bf16[8,1,32,384]{3,2,1,0:T(8,128)(2,1)S(1)} %bitcast.95), channel_id=1, source_target_pairs={{0,2},{2,0},{1,3},{3,1},{4,6},{6,4},{5,7},{7,5},{8,10},{10,8},{9,1... | collective-permute-start | bytes 589832 | tf_op jit(solution)/shard_map/ppermute | solution.py:22
  63.3 16.4 %collective-permute-start.16 = (bf16[2,2,2,32,1024]{4,3,2,0,1:T(8,128)(2,1)S(1)}, bf16[2,2,2,32,1024]{4,3,2,0,1:T(8,128)(2,1)S(1)}, u32[]{:S(2)}, u32[]{:S(2)}) collective-permute-start(bf16[2,2,2,32,1024]{4,3,2,0,1:T(8,128)(2,1)S(1)} %pad_maximum_fusion.3), channel_id=1, source_target_pairs={{0,4},{4,0},{1,5},{5,1},{2,6},{6,2},{3,7},{7,3},{8,12},{12,8},{9,1... | collective-permute-start | bytes 1572872 | tf_op jit(solution)/shard_map/ppermute | solution.py:22
  63.9 15.7 %collective-permute-start.17 = (bf16[128,1024]{1,0:T(8,128)(2,1)S(1)}, bf16[128,1024]{1,0:T(8,128)(2,1)S(1)}, u32[]{:S(2)}, u32[]{:S(2)}) collective-permute-start(bf16[128,1024]{1,0:T(8,128)(2,1)S(1)} %get-tuple-element.427.refs_8_.cot_ref), channel_id=1, source_target_pairs={{0,8},{8,0},{1,9},{9,1},{2,10},{10,2},{3,11},{11,3},{4,12},{12,4},... | collective-permute-start | bytes 786440 | tf_op jit(solution)/shard_map/ppermute | solution.py:22
  65.6 26.7 %collective-permute-start.21 = (bf16[1,8,32,1152]{3,2,1,0:T(8,128)(2,1)}, bf16[1,8,32,1152]{3,2,1,0:T(8,128)(2,1)}, u32[]{:S(2)}, u32[]{:S(2)}) collective-permute-start(bf16[1,8,32,1152]{3,2,1,0:T(8,128)(2,1)} %bitcast.18.a_ref), channel_id=1, source_target_pairs={{0,1},{1,0},{2,3},{3,2},{4,5},{5,4},{6,7},{7,6},{8,9},{9,8},{10,11... | collective-permute-start | bytes 1769480 | tf_op jit(solution)/shard_map/ppermute | solution.py:22
  66.1 31.3 %collective-permute-start.20 = (bf16[1,8,32,1152]{3,2,1,0:T(8,128)(2,1)}, bf16[1,8,32,1152]{3,2,1,0:T(8,128)(2,1)}, u32[]{:S(2)}, u32[]{:S(2)}) collective-permute-start(bf16[1,8,32,1152]{3,2,1,0:T(8,128)(2,1)} %bitcast.18.a_ref), channel_id=1, source_target_pairs={{0,16},{16,0},{1,17},{17,1},{2,18},{18,2},{3,19},{19,3},{4,20},{20... | collective-permute-start | bytes 1769480 | tf_op jit(solution)/shard_map/ppermute | solution.py:22
  80.4 18.2 %all-to-all-start.2 = ((bf16[8,128,128]{2,1,0:T(8,128)(2,1)}), bf16[8,128,128]{2,1,0:T(8,128)(2,1)S(1)}, u32[]{:S(2)}, u32[]{:S(2)}) async-start(bf16[8,128,128]{2,1,0:T(8,128)(2,1)} %copy-done.24), calls=%async_computation.2 | async-start | bytes 524288 | tf_op jit(solution)/shard_map/all_to_all | solution.py:634
  84.0 13.3 %collective-permute-start.22 = (bf16[128,1024]{1,0:T(8,128)(2,1)}, bf16[128,1024]{1,0:T(8,128)(2,1)}, u32[]{:S(2)}, u32[]{:S(2)}) collective-permute-start(bf16[128,1024]{1,0:T(8,128)(2,1)} %copy-done.36), channel_id=1, source_target_pairs={{0,4},{4,0},{1,5},{5,1},{2,6},{6,2},{3,7},{7,3},{8,12},{12,8},{9,1... | collective-permute-start | bytes 786440 | tf_op jit(solution)/shard_map/ppermute | solution.py:22
  98.6 13.4 %collective-permute-start.23 = (bf16[1,8,32,1152]{3,2,1,0:T(8,128)(2,1)}, bf16[1,8,32,1152]{3,2,1,0:T(8,128)(2,1)S(1)}, u32[]{:S(2)}, u32[]{:S(2)}) collective-permute-start(bf16[1,8,32,1152]{3,2,1,0:T(8,128)(2,1)} %collective-permute-done.20.c_ref), channel_id=1, source_target_pairs={{0,1},{1,0},{2,3},{3,2},{4,5},{5,4},{6,7},{7,6},{8,9},{9,8},{10,11... | collective-permute-start | bytes 1769480 | tf_op jit(solution)/shard_map/ppermute | solution.py:22
  102.3 9.8 %collective-permute-start.26 = (bf16[128,1024]{1,0:T(8,128)(2,1)S(1)}, bf16[128,1024]{1,0:T(8,128)(2,1)S(1)}, u32[]{:S(2)}, u32[]{:S(2)}) collective-permute-start(bf16[128,1024]{1,0:T(8,128)(2,1)S(1)} %get-tuple-element.378.refs_0_), channel_id=1, source_target_pairs={{0,12},{4,8},{8,4},{12,0},{1,13},{5,9},{9,5},{13,1},{2,14},{6,10},... | collective-permute-start | bytes 786440 | tf_op jit(solution)/shard_map/ppermute | solution.py:26
  102.8 11.4 %collective-permute-start.25 = (bf16[128,1024]{1,0:T(8,128)(2,1)S(1)}, bf16[128,1024]{1,0:T(8,128)(2,1)S(1)}, u32[]{:S(2)}, u32[]{:S(2)}) collective-permute-start(bf16[128,1024]{1,0:T(8,128)(2,1)S(1)} %get-tuple-element.378.refs_0_), channel_id=1, source_target_pairs={{0,8},{8,0},{1,9},{9,1},{2,10},{10,2},{3,11},{11,3},{4,12},{12,4},... | collective-permute-start | bytes 786440 | tf_op jit(solution)/shard_map/ppermute | solution.py:22
  104.9 9.9 %collective-permute-start.24 = (bf16[128,1024]{1,0:T(8,128)(2,1)S(1)}, bf16[128,1024]{1,0:T(8,128)(2,1)S(1)}, u32[]{:S(2)}, u32[]{:S(2)}) collective-permute-start(bf16[128,1024]{1,0:T(8,128)(2,1)S(1)} %get-tuple-element.378.refs_0_), channel_id=1, source_target_pairs={{0,4},{4,0},{1,5},{5,1},{2,6},{6,2},{3,7},{7,3},{8,12},{12,8},{9,1... | collective-permute-start | bytes 786440 | tf_op jit(solution)/shard_map/ppermute | solution.py:22
  105.8 9.0 %collective-permute-start.31 = (bf16[128,1024]{1,0:T(8,128)(2,1)S(1)}, bf16[128,1024]{1,0:T(8,128)(2,1)S(1)}, u32[]{:S(2)}, u32[]{:S(2)}) collective-permute-start(bf16[128,1024]{1,0:T(8,128)(2,1)S(1)} %copy-done.22), channel_id=1, source_target_pairs={{0,2},{2,0},{1,3},{3,1},{4,6},{6,4},{5,7},{7,5},{8,10},{10,8},{9,1... | collective-permute-start | bytes 786440 | tf_op jit(solution)/shard_map/ppermute | solution.py:22
  127.3 10.6 %collective-permute-start.36 = (bf16[128,1024]{1,0:T(8,128)(2,1)S(1)}, bf16[128,1024]{1,0:T(8,128)(2,1)S(1)}, u32[]{:S(2)}, u32[]{:S(2)}) collective-permute-start(bf16[128,1024]{1,0:T(8,128)(2,1)S(1)} %get-tuple-element.415), channel_id=1, source_target_pairs={{0,4},{4,0},{1,5},{5,1},{2,6},{6,2},{3,7},{7,3},{8,12},{12,8},{9,1... | collective-permute-start | bytes 786440 | tf_op jit(solution)/shard_map/ppermute | solution.py:22
  128.3 9.5 %collective-permute-start.37 = (bf16[128,1024]{1,0:T(8,128)(2,1)S(1)}, bf16[128,1024]{1,0:T(8,128)(2,1)S(1)}, u32[]{:S(2)}, u32[]{:S(2)}) collective-permute-start(bf16[128,1024]{1,0:T(8,128)(2,1)S(1)} %get-tuple-element.416), channel_id=1, source_target_pairs={{0,8},{8,0},{1,9},{9,1},{2,10},{10,2},{3,11},{11,3},{4,12},{12,4},... | collective-permute-start | bytes 786440 | tf_op jit(solution)/shard_map/ppermute | solution.py:22
  128.3 14.2 %collective-permute-start.38 = (bf16[128,1024]{1,0:T(8,128)(2,1)S(1)}, bf16[128,1024]{1,0:T(8,128)(2,1)S(1)}, u32[]{:S(2)}, u32[]{:S(2)}) collective-permute-start(bf16[128,1024]{1,0:T(8,128)(2,1)S(1)} %get-tuple-element.417), channel_id=1, source_target_pairs={{0,12},{4,8},{8,4},{12,0},{1,13},{5,9},{9,5},{13,1},{2,14},{6,10},... | collective-permute-start | bytes 786440 | tf_op jit(solution)/shard_map/ppermute | solution.py:26
  136.9 27.5 %collective-permute-start.41 = (bf16[16,32,1152]{2,1,0:T(8,128)(2,1)}, bf16[16,32,1152]{2,1,0:T(8,128)(2,1)}, u32[]{:S(2)}, u32[]{:S(2)}) collective-permute-start(bf16[16,32,1152]{2,1,0:T(8,128)(2,1)} %get-tuple-element.452), channel_id=1, source_target_pairs={{0,1},{1,0},{2,3},{3,2},{4,5},{5,4},{6,7},{7,6},{8,9},{9,8},{10,11... | collective-permute-start | bytes 3538952 | tf_op jit(solution)/shard_map/ppermute | solution.py:22
  145.1 7.3 %collective-permute-start.39 = (bf16[512,1024]{1,0:T(8,128)(2,1)}, bf16[512,1024]{1,0:T(8,128)(2,1)}, u32[]{:S(2)}, u32[]{:S(2)}) collective-permute-start(bf16[512,1024]{1,0:T(8,128)(2,1)} %get-tuple-element.443), channel_id=1, source_target_pairs={{0,2},{2,0},{1,3},{3,1},{4,6},{6,4},{5,7},{7,5},{8,10},{10,8},{9,1... | collective-permute-start | bytes 3145736 | tf_op jit(solution)/shard_map/ppermute | solution.py:22
  147.6 11.1 %collective-permute-start.40 = (bf16[8,64,1024]{2,1,0:T(8,128)(2,1)}, bf16[8,64,1024]{2,1,0:T(8,128)(2,1)}, u32[]{:S(2)}, u32[]{:S(2)}) collective-permute-start(bf16[8,64,1024]{2,1,0:T(8,128)(2,1)} %get-tuple-element.448), channel_id=1, source_target_pairs={{0,2},{2,0},{1,3},{3,1},{4,6},{6,4},{5,7},{7,5},{8,10},{10,8},{9,1... | collective-permute-start | bytes 3145736 | tf_op jit(solution)/shard_map/ppermute | solution.py:22
  148.1 13.7 %all-to-all-start.3 = ((bf16[8,128,128]{2,1,0:T(8,128)(2,1)}), bf16[8,128,128]{2,1,0:T(8,128)(2,1)S(1)}, u32[]{:S(2)}, u32[]{:S(2)}) async-start(bf16[8,128,128]{2,1,0:T(8,128)(2,1)} %copy-done.23), calls=%async_computation.3 | async-start | bytes 524288 | tf_op jit(solution)/shard_map/all_to_all | solution.py:717
  155.2 22.6 %collective-permute-start.42 = (bf16[128,1024]{1,0:T(8,128)(2,1)}, bf16[128,1024]{1,0:T(8,128)(2,1)}, u32[]{:S(2)}, u32[]{:S(2)}) collective-permute-start(bf16[128,1024]{1,0:T(8,128)(2,1)} %get-tuple-element.468), channel_id=1, source_target_pairs={{0,4},{4,0},{1,5},{5,1},{2,6},{6,2},{3,7},{7,3},{8,12},{12,8},{9,1... | collective-permute-start | bytes 786440 | tf_op jit(solution)/shard_map/ppermute | solution.py:22
  157.3 20.6 %collective-permute-start.43 = (bf16[128,1024]{1,0:T(8,128)(2,1)}, bf16[128,1024]{1,0:T(8,128)(2,1)}, u32[]{:S(2)}, u32[]{:S(2)}) collective-permute-start(bf16[128,1024]{1,0:T(8,128)(2,1)} %get-tuple-element.469), channel_id=1, source_target_pairs={{0,8},{8,0},{1,9},{9,1},{2,10},{10,2},{3,11},{11,3},{4,12},{12,4},... | collective-permute-start | bytes 786440 | tf_op jit(solution)/shard_map/ppermute | solution.py:22
  158.7 19.2 %collective-permute-start.44 = (bf16[128,1024]{1,0:T(8,128)(2,1)}, bf16[128,1024]{1,0:T(8,128)(2,1)}, u32[]{:S(2)}, u32[]{:S(2)}) collective-permute-start(bf16[128,1024]{1,0:T(8,128)(2,1)} %get-tuple-element.470), channel_id=1, source_target_pairs={{0,12},{4,8},{8,4},{12,0},{1,13},{5,9},{9,5},{13,1},{2,14},{6,10},... | collective-permute-start | bytes 786440 | tf_op jit(solution)/shard_map/ppermute | solution.py:26
  164.4 13.5 %collective-permute-start.45 = (bf16[8,32,1024]{2,1,0:T(8,128)(2,1)}, bf16[8,32,1024]{2,1,0:T(8,128)(2,1)S(1)}, u32[]{:S(2)}, u32[]{:S(2)}) collective-permute-start(bf16[8,32,1024]{2,1,0:T(8,128)(2,1)} %copy-done.33), channel_id=1, source_target_pairs={{0,1},{1,0},{2,3},{3,2},{4,5},{5,4},{6,7},{7,6},{8,9},{9,8},{10,11... | collective-permute-start | bytes 1572872 | tf_op jit(solution)/shard_map/ppermute | solution.py:22
  177.9 12.2 %collective-permute-start.48 = (bf16[256,1024]{1,0:T(8,128)(2,1)S(1)}, bf16[256,1024]{1,0:T(8,128)(2,1)S(1)}, u32[]{:S(2)}, u32[]{:S(2)}) collective-permute-start(bf16[256,1024]{1,0:T(8,128)(2,1)S(1)} %get-tuple-element.495), channel_id=1, source_target_pairs={{0,4},{4,0},{1,5},{5,1},{2,6},{6,2},{3,7},{7,3},{8,12},{12,8},{9,1... | collective-permute-start | bytes 1572872 | tf_op jit(solution)/shard_map/ppermute | solution.py:22
  181.4 12.5 %collective-permute-start.47 = (bf16[2,64,1024]{2,1,0:T(8,128)(2,1)S(1)}, bf16[2,64,1024]{2,1,0:T(8,128)(2,1)S(1)}, u32[]{:S(2)}, u32[]{:S(2)}) collective-permute-start(bf16[2,64,1024]{2,1,0:T(8,128)(2,1)S(1)} %get-tuple-element.493), channel_id=1, source_target_pairs={{0,8},{8,0},{1,9},{9,1},{2,10},{10,2},{3,11},{11,3},{4,12},{12,4},... | collective-permute-start | bytes 786440 | tf_op jit(solution)/shard_map/ppermute | solution.py:22
  183.3 29.3 %collective-permute-start.56 = (bf16[1,256,1152]{2,1,0:T(8,128)(2,1)S(1)}, bf16[1,256,1152]{2,1,0:T(8,128)(2,1)S(1)}, u32[]{:S(2)}, u32[]{:S(2)}) collective-permute-start(bf16[1,256,1152]{2,1,0:T(8,128)(2,1)S(1)} %get-tuple-element.533), channel_id=1, source_target_pairs={{0,16},{16,0},{1,17},{17,1},{2,18},{18,2},{3,19},{19,3},{4,20},{20... | collective-permute-start | bytes 1769480 | tf_op jit(solution)/shard_map/ppermute | solution.py:22
  194.0 14.8 %collective-permute-start.50 = (bf16[256,1024]{1,0:T(8,128)(2,1)S(1)}, bf16[256,1024]{1,0:T(8,128)(2,1)S(1)}, u32[]{:S(2)}, u32[]{:S(2)}) collective-permute-start(bf16[256,1024]{1,0:T(8,128)(2,1)S(1)} %get-tuple-element.509), channel_id=1, source_target_pairs={{0,4},{4,0},{1,5},{5,1},{2,6},{6,2},{3,7},{7,3},{8,12},{12,8},{9,1... | collective-permute-start | bytes 1572872 | tf_op jit(solution)/shard_map/ppermute | solution.py:22
  195.2 11.1 %collective-permute-start.51 = (bf16[128,1024]{1,0:T(8,128)(2,1)S(1)}, bf16[128,1024]{1,0:T(8,128)(2,1)S(1)}, u32[]{:S(2)}, u32[]{:S(2)}) collective-permute-start(bf16[128,1024]{1,0:T(8,128)(2,1)S(1)} %get-tuple-element.511), channel_id=1, source_target_pairs={{0,8},{8,0},{1,9},{9,1},{2,10},{10,2},{3,11},{11,3},{4,12},{12,4},... | collective-permute-start | bytes 786440 | tf_op jit(solution)/shard_map/ppermute | solution.py:22
  195.2 6.2 %collective-permute-start.49 = (bf16[8,32,384]{2,1,0:T(8,128)(2,1)S(1)}, bf16[8,32,384]{2,1,0:T(8,128)(2,1)S(1)}, u32[]{:S(2)}, u32[]{:S(2)}) collective-permute-start(bf16[8,32,384]{2,1,0:T(8,128)(2,1)S(1)} %get-tuple-element.500), channel_id=1, source_target_pairs={{0,1},{1,0},{2,3},{3,2},{4,5},{5,4},{6,7},{7,6},{8,9},{9,8},{10,11... | collective-permute-start | bytes 589832 | tf_op jit(solution)/shard_map/ppermute | solution.py:22
  196.6 13.7 %collective-permute-start.52 = (bf16[2,32,1024]{2,1,0:T(8,128)(2,1)S(1)}, bf16[2,32,1024]{2,1,0:T(8,128)(2,1)S(1)}, u32[]{:S(2)}, u32[]{:S(2)}) collective-permute-start(bf16[2,32,1024]{2,1,0:T(8,128)(2,1)S(1)} %get-tuple-element.516), channel_id=1, source_target_pairs={{0,4},{4,0},{1,5},{5,1},{2,6},{6,2},{3,7},{7,3},{8,12},{12,8},{9,1... | collective-permute-start | bytes 393224 | tf_op jit(solution)/shard_map/ppermute | solution.py:22
  214.2 25.7 %all-to-all-start.4 = ((bf16[8,32,1152]{2,1,0:T(8,128)(2,1)}), bf16[8,32,1152]{2,1,0:T(8,128)(2,1)S(1)}, u32[]{:S(2)}, u32[]{:S(2)}) async-start(bf16[8,32,1152]{2,1,0:T(8,128)(2,1)} %total.3), calls=%async_computation.4 | async-start | bytes 1179648 | tf_op jit(solution)/shard_map/all_to_all | solution.py:834
  217.7 20.0 %collective-permute-start.53 = (bf16[128,1024]{1,0:T(8,128)(2,1)}, bf16[128,1024]{1,0:T(8,128)(2,1)S(1)}, u32[]{:S(2)}, u32[]{:S(2)}) collective-permute-start(bf16[128,1024]{1,0:T(8,128)(2,1)} %get-tuple-element.528), channel_id=1, source_target_pairs={{0,16},{16,0},{1,17},{17,1},{2,18},{18,2},{3,19},{19,3},{4,20},{20... | collective-permute-start | bytes 786440 | tf_op jit(solution)/shard_map/ppermute | solution.py:22
  218.9 20.9 %collective-permute-start.54 = (bf16[128,1024]{1,0:T(8,128)(2,1)}, bf16[128,1024]{1,0:T(8,128)(2,1)S(1)}, u32[]{:S(2)}, u32[]{:S(2)}) collective-permute-start(bf16[128,1024]{1,0:T(8,128)(2,1)} %copy-done.38), channel_id=1, source_target_pairs={{0,8},{8,0},{1,9},{9,1},{2,10},{10,2},{3,11},{11,3},{4,12},{12,4},... | collective-permute-start | bytes 786440 | tf_op jit(solution)/shard_map/ppermute | solution.py:22
  222.8 15.0 %collective-permute-start.57 = (bf16[1,32,1024]{2,1,0:T(8,128)(2,1)S(1)}, bf16[1,32,1024]{2,1,0:T(8,128)(2,1)S(1)}, u32[]{:S(2)}, u32[]{:S(2)}) collective-permute-start(bf16[1,32,1024]{2,1,0:T(8,128)(2,1)S(1)} %get-tuple-element.537), channel_id=1, source_target_pairs={{0,16},{16,0},{1,17},{17,1},{2,18},{18,2},{3,19},{19,3},{4,20},{20... | collective-permute-start | bytes 196616 | tf_op jit(solution)/shard_map/ppermute | solution.py:22
  239.8 12.1 %all-to-all-start.5 = ((bf16[8,32,384]{2,1,0:T(8,128)(2,1)}), bf16[8,32,384]{2,1,0:T(8,128)(2,1)}, u32[]{:S(2)}, u32[]{:S(2)}) async-start(bf16[8,32,384]{2,1,0:T(8,128)(2,1)} %total.2), calls=%async_computation.5 | async-start | bytes 393216 | tf_op jit(solution)/shard_map/all_to_all | solution.py:856
  (62 other events, 414.2 us)

commit v4 on v3

--- a/solution.py
+++ b/solution.py
@@ -30,8 +30,82 @@
     return lax.optimization_barrier((array, *others))[0]
 
 
-def fence(live):
-    return dict(zip(live, lax.optimization_barrier(tuple(live.values()))))
+class Taken:
+    def __init__(self, arrays):
+        self._arrays = arrays
+
+    def __getattr__(self, name):
+        return self._arrays.pop(name)
+
+
+class Live:
+    def __init__(self):
+        self._held, self._due = {}, {}
+
+    def __getattr__(self, name):
+        return self._held[name]
+
+    def put(self, due, **arrays):
+        self._held.update(arrays)
+        self._due.update(dict.fromkeys(arrays, due))
+
+    @property
+    def take(self):
+        return Taken(self._held)
+
+    def fence(self, stage):
+        names = [name for name in self._held if self._due[name] <= stage]
+        arrays = lax.optimization_barrier(tuple(self._held[name] for name in names))
+        self._held.update(zip(names, arrays))
+
+
+ROUND_1, ROUND_2, ROUND_3, ATTEND, RETURN, MIDDLE, SPREAD, FEED, CHIP, COLLECT, MIDDLE_BACK, LEAVE, ATTEND_BACK, OVER_X, OVER_ZL, OVER_ZH, LAST = range(17)
+ENTER = -1
+SCHEDULE = dict(
+    qkv_pack=(ENTER, ENTER),
+    qkv_slices=(ROUND_1, ROUND_2),
+    qkv_y=(ROUND_3, ROUND_3),
+    qkv_whole=(ROUND_3, ROUND_3),
+    feed_pack=(ROUND_1, ROUND_1),
+    feed_slices=(ROUND_2, ROUND_2),
+    feed_zh=(ATTEND, RETURN),
+    feed_y=(ATTEND, RETURN),
+    feed_far_y=(MIDDLE, SPREAD),
+    feed_whole=(SPREAD, SPREAD),
+    attn_y=(ROUND_1, ROUND_2),
+    attn_zh=(ROUND_2, ROUND_2),
+    attn_zl=(ROUND_3, ROUND_3),
+    attn_x=(ATTEND, ATTEND),
+    attn_whole=(RETURN, RETURN),
+    cot_over_x=(ROUND_1, ROUND_1),
+    cot_over_z=(ROUND_3, ATTEND),
+    cot_over_zx=(RETURN, RETURN),
+    cot_cores=(FEED, FEED),
+    tables=(ROUND_1, ROUND_2),
+    rest=(COLLECT, COLLECT),
+    result_sums=(LEAVE, ATTEND_BACK),
+    result_x=(LEAVE, ATTEND_BACK),
+    result_z=(LEAVE, ATTEND_BACK),
+    result_both=(LEAVE, ATTEND_BACK),
+    result_out=(OVER_ZH, OVER_ZH),
+    grad_in_y=(COLLECT, LEAVE),
+    grad_in_zh=(OVER_X, OVER_ZL),
+    grad_in_slices=(OVER_ZH, OVER_ZH),
+    grad_attn_made=(LEAVE, LEAVE),
+    grad_attn_cut=(LEAVE, LEAVE),
+    grad_attn_y=(ATTEND_BACK, OVER_ZH),
+    grad_attn_zl=(OVER_X, OVER_X),
+    grad_attn_x=(OVER_ZL, OVER_ZL),
+    grad_attn_zh=(OVER_ZH, OVER_ZH),
+    grad_qkv_made=(OVER_X, OVER_X),
+    grad_qkv_y=(OVER_ZL, OVER_ZL),
+    grad_qkv_slices=(LAST, LAST),
+)
+FENCES = set(range(ENTER, LAST))
+
+
+def name_of(kernel):
+    return kernel.func.__name__ if isinstance(kernel, functools.partial) else kernel.__name__
 
 
 def add(*terms):
@@ -41,7 +115,7 @@
     return total.astype(terms[0].dtype)
 
 
-def call(kernel, name, outs, places, *arrays, scratch=(), mib=16, flops=0, exps=0):
+def call(kernel, outs, places, *arrays, scratch=(), mib=16, flops=0, exps=0):
     vmem = pl.BlockSpec(memory_space=pltpu.VMEM)
     moved = sum(array.size * array.dtype.itemsize for array in arrays)
     moved += sum(math.prod(shape) * jnp.dtype(dtype).itemsize for shape, dtype in outs)
@@ -53,7 +127,7 @@
         scratch_shapes=list(scratch),
         compiler_params=pltpu.CompilerParams(vmem_limit_bytes=mib * MIB),
         cost_estimate=pl.CostEstimate(flops=flops, bytes_accessed=moved, transcendentals=exps),
-        name=name,
+        name=name_of(kernel),
     )(places, *arrays)
 
 
@@ -114,7 +188,7 @@
     shape = (extent[0], 2, extent[1], 2) + extent[2:]
     if extent[2] % 16 == 0:
         kernel = functools.partial(assemble_kernel, lead, first, second)
-        return call(kernel, "assemble", [(shape, bf16)], places, *pieces)[0]
+        return call(kernel, [(shape, bf16)], places, *pieces)[0]
 
     def ordered(own, other, place, axis):
         straight = jnp.stack([own, other], axis)
@@ -139,7 +213,7 @@
 def assemble_rows(places, pieces):
     if pieces[0].shape[2] % 16 == 0:
         shape = (8, 2) + pieces[0].shape[1:]
-        return call(assemble_rows_kernel, "assemble_rows", [(shape, bf16)], places, *pieces)[0]
+        return call(assemble_rows_kernel, [(shape, bf16)], places, *pieces)[0]
     merged = [jnp.stack(pieces[at : at + 2], axis=1) for at in (0, 2)]
     merged = [member.reshape((8, 1) + member.shape[2:]) for member in merged]
     pieces = [member[:, :, at] for member in merged for at in range(2)]
@@ -152,7 +226,7 @@
 
 def total(places, kept, other):
     if kept.shape[1] % 16 == 0:
-        return call(total_kernel, "total", [(kept.shape, bf16)], places, kept, other)[0]
+        return call(total_kernel, [(kept.shape, bf16)], places, kept, other)[0]
     return add(kept, other)
 
 
@@ -183,7 +257,7 @@
         flat = (math.prod(shape[:before]), 2, math.prod(shape[before + 1 : -1]), shape[-1])
         outs = [((flat[0],) + flat[2:], bf16)] * 2
         kernel = functools.partial(split_kernel, which, len(parts))
-        halves = call(kernel, "split", outs, places, *[part.reshape(flat) for part in parts])
+        halves = call(kernel, outs, places, *[part.reshape(flat) for part in parts])
         return [half.reshape(rest) for half in halves]
     total = add(*parts)
     return [
@@ -342,7 +416,6 @@
     outs = [((8 * rows, piece), bf16), ((8 * rows, 2 * piece), bf16)] + [((4 * rows, width), bf16)] * 2
     hidden, grads, *terms = call(
         feed_kernel,
-        "feed",
         outs,
         places,
         *two,
@@ -387,7 +460,6 @@
     outs = [((4 * rows, width), bf16)] * 2 + [(shape, bf16) for shape in shares]
     made = call(
         feed_rest_kernel,
-        "feed_rest",
         outs,
         places,
         *two,
@@ -410,7 +482,7 @@
 
 def chip_sums(places, here, there):
     shape = (here.shape[0] // 4, here.shape[1])
-    return call(chip_sums_kernel, "chip_sums", [(shape, bf16)] * 4, places, here, partner(there, "c"))
+    return call(chip_sums_kernel, [(shape, bf16)] * 4, places, here, partner(there, "c"))
 
 
 def far_sums_kernel(places, kept_ref, across_ref, six_ref, four_ref):
@@ -516,7 +588,8 @@
     ff = w_out.shape[0]
     piece = -(-ff // (squares * LANES)) * LANES
     chips, square = ("zh", "zl", "x"), ("zl", "x", "c")
-    ri, zh, zl, xi, ci, yi = (lax.axis_index(name) for name in ("r", "zh", "zl", "x", "c", "y"))
+    everyone = ("r",) + chips + ("c", "y")
+    ri, zh, zl, xi, ci, yi = (lax.axis_index(name) for name in everyone)
     places = jnp.stack([4 * zh + 2 * zl + xi, zh, zl, xi, ci, yi]).astype(jnp.int32)
     block_low, half_low = ((block, width), bf16), ((half_block, width), bf16)
     block_full, half_full = ((block, width), f32), ((half_block, width), f32)
@@ -531,11 +604,282 @@
 
     gain_one = gain_attn.astype(f32)[:, None]
     gain_two = gain_mlp.astype(f32)[:, None]
-
+    count = rings * span
+    direct = rings == 1 and owned % 16 == 0
+
+    live = Live()
+    steps = []
+
+    def step(made):
+        steps.append((SCHEDULE[made.__name__], made))
+
+    def begin(stage):
+        for at, ((start, due), made) in enumerate(steps):
+            if start == stage:
+                steps[at] = ((None, due), made)
+                live.put(due, **made())
+
+    def reach(stage):
+        begin(stage)
+        if stage in FENCES:
+            live.fence(stage)
+
+
+    @step
+    def qkv_pack():
+        scaled = (live.take.w_qkv.astype(f32) * gain_one).astype(bf16)
+        slices = scaled.reshape(owned, 3, pairs, wide).transpose(2, 0, 1, 3)
+        return dict(slices=slices.reshape(pairs, owned, 3 * wide))
+
+    @step
+    def qkv_slices():
+        return dict(qkv_own=lax.all_to_all(live.take.slices, chips, 0, 0, tiled=True)[:, None])
+
+    @step
+    def qkv_y():
+        return dict(qkv_other=partner(live.qkv_own, "y"))
+
+    @step
+    def qkv_whole():
+        parts = [live.take.qkv_own, live.take.qkv_other]
+        parts = parts + [partner(part, "c") for part in parts]
+        return dict(qkv=over_rings(assemble(places, None, C, Y, parts)).reshape(width, 3 * wide))
+
+
+    @step
+    def feed_pack():
+        scaled = (live.take.w_in.astype(f32) * gain_two).astype(bf16)
+        packed = [
+            columns_by(scaled[:, :ff], squares, piece),
+            columns_by(scaled[:, ff:], squares, piece),
+            columns_by(jnp.transpose(live.take.w_out), squares, piece),
+        ]
+        return dict(packed=jnp.concatenate(packed, axis=2))
+
+    @step
+    def feed_slices():
+        return dict(packed=lax.all_to_all(live.take.packed, square, 0, 0, tiled=True)[None])
+
+    @step
+    def feed_zh():
+        return dict(packed_far=partner(live.packed, "zh"))
+
+    @step
+    def feed_y():
+        return dict(packed_y=partner(live.packed, "y"))
+
+    @step
+    def feed_far_y():
+        return dict(packed_far_y=partner(live.packed_far, "y"))
+
+    @step
+    def feed_whole():
+        take = live.take
+        parts = [take.packed, take.packed_y, take.packed_far, take.packed_far_y]
+        whole = assemble(places, None, ZH, Y, parts)
+        return dict(weights=over_rings(whole).reshape(width, 3 * piece))
+
+
+    @step
+    def attn_y():
+        return dict(full=jnp.stack([live.w_attn_out, partner(live.take.w_attn_out, "y")]))
+
+    @step
+    def attn_zh():
+        return dict(full=jnp.stack([live.full, partner(live.full, "zh")]))
+
+    @step
+    def attn_zl():
+        return dict(full=jnp.stack([live.full, partner(live.full, "zl")], axis=1))
+
+    @step
+    def attn_x():
+        return dict(full_x=partner(live.full, "x"))
+
+    @step
+    def attn_whole():
+        parts = [part.reshape(4, 2, owned, width) for part in (live.take.full, live.take.full_x)]
+        parts = parts + [partner(part, "c") for part in parts]
+        return dict(attn=over_rings(assemble_rows(places, parts)).reshape(width, width))
+
+
+    @step
+    def cot_over_x():
+        return dict(cot_x=partner(live.cot, "x"))
+
+    @step
+    def cot_over_z():
+        return dict(cot_z=partner(live.cot, "zl"))
+
+    @step
+    def cot_over_zx():
+        return dict(cot_zx=partner(live.cot_z, "x"))
+
+    @step
+    def cot_cores():
+        parts = (live.cot, live.cot_x, live.cot_z, live.cot_zx)
+        own, over_x, over_z, over_zx = (partner(part, "c") for part in parts)
+        return dict(core=own, core_x=over_x, core_z=over_z, core_zx=over_zx)
+
+    @step
+    def tables():
+        lane = jnp.arange(wide, dtype=jnp.int32)
+        frequency = rope_base ** (-2.0 * (lane % half).astype(f32) / size)
+        sign = jnp.where(lane % size < half, -1.0, 1.0)
+        row = jnp.arange(span, dtype=jnp.int32)
+        chip = (live.places[CHIP] ^ (row // block)) * block
+        core = (live.places[C] ^ (row % block // half_block)) * half_block
+        at = ri * span + chip + core + row % half_block
+        angles = at.astype(f32)[:, None] * frequency[None, :]
+        return dict(table=jnp.concatenate([jnp.cos(angles), jnp.sin(angles) * sign], axis=1))
+
+
+    @step
+    def rest():
+        shape = (2 * squares, owned, 3 * piece)
+        result, shares = feed_rest(
+            places,
+            all_two,
+            all_cotangent(),
+            live.take.hidden,
+            live.take.gate_up,
+            live.take.weights,
+            [shape] * 2 if direct else [(width, 3 * piece)],
+        )
+        if not direct:
+            terms = ring_sums(shares[0]).reshape(2 * squares, 2, owned, 3 * piece)
+            shares = split(places, Y, [terms], 1)
+        return dict(
+            result_here=result[0],
+            result_there=result[1],
+            weights_kept=shares[0],
+            weights_sent=shares[1],
+        )
+
+    @step
+    def result_sums():
+        sums = chip_sums(places, live.take.result_here, live.take.result_there)
+        return dict(result0=sums[0], result1=sums[1], result2=sums[2], result3=sums[3])
+
+    @step
+    def result_x():
+        return dict(result1=partner(live.result1, "x"))
+
+    @step
+    def result_z():
+        return dict(result2=partner(live.result2, "zl"))
+
+    @step
+    def result_both():
+        return dict(result3=opposite(live.result3, ("zl", "x")))
+
+    @step
+    def result_out():
+        take = live.take
+        kept, sent = call(
+            result_kernel,
+            [half_low] * 2,
+            places,
+            live.middle,
+            take.result0,
+            take.result1,
+            take.result2,
+            take.result3,
+        )
+        out = call(leave_kernel, [(inputs.shape, bf16)], places, kept, partner(sent, "c"))[0]
+        return dict(output=out)
+
+    @step
+    def grad_in_y():
+        return dict(weights_y=partner(live.take.weights_sent, "y"))
+
+    @step
+    def grad_in_zh():
+        shares = [live.take.weights_kept, live.take.weights_y]
+        shares = [share.reshape(1, 2, squares * owned, 3 * piece) for share in shares]
+        kept, sent = split(places, ZH, shares, 1)
+        return dict(weights_kept=kept, weights_far=partner(sent, "zh"))
+
+    @step
+    def grad_in_slices():
+        shares = [live.take.weights_kept, live.take.weights_far]
+        shares = [share.reshape(squares, owned, 3 * piece) for share in shares]
+        return dict(grad_packed=lax.all_to_all(total(places, *shares), square, 0, 0, tiled=True))
+
+
+    @step
+    def grad_attn_made():
+        shape = (pairs, 2 * owned, width)
+        shares = call(
+            outer_kernel,
+            [(shape, bf16)] * 2 if direct else [((width, width), bf16)],
+            places,
+            live.take.attended,
+            live.take.branch,
+        )
+        if not direct:
+            terms = ring_sums(shares[0]).reshape(pairs, 2, 2 * owned, width)
+            shares = split(places, C, [terms], 1)
+        return dict(attn_kept=shares[0], attn_other=partner(shares[1], "c"))
+
+    def attn_sums(which, before, after_it, name):
+        shares = [live.take.attn_kept, live.take.attn_other]
+        shares = [share.reshape(before, 2, after_it * owned, width) for share in shares]
+        kept, sent = split(places, which, shares, 1)
+        return dict(attn_kept=kept, attn_other=partner(sent, name))
+
+    @step
+    def grad_attn_cut():
+        shares = [live.take.attn_kept, live.take.attn_other]
+        shares = [share.reshape(8, 2, owned, width) for share in shares]
+        kept, sent = split(places, Y, shares, 1)
+        return dict(attn_kept=kept, attn_sent=sent)
+
+    @step
+    def grad_attn_y():
+        return dict(attn_other=partner(live.take.attn_sent, "y"))
+
+    @step
+    def grad_attn_zl():
+        return attn_sums(ZL, 2, 2, "zl")
+
+    @step
+    def grad_attn_x():
+        return attn_sums(X, 2, 1, "x")
+
+    @step
+    def grad_attn_zh():
+        return attn_sums(ZH, 1, 1, "zh")
+
+
+    @step
+    def grad_qkv_made():
+        shape = (pairs, 2 * owned, 3 * wide)
+        shares = call(
+            project_outer_kernel,
+            [(shape, bf16)] * 2 if direct else [((width, 3 * wide), bf16)],
+            places,
+            all_one,
+            live.take.projected,
+        )
+        if not direct:
+            terms = ring_sums(shares[0]).reshape(pairs, 2, 2 * owned, 3 * wide)
+            shares = split(places, C, [terms], 1)
+        shares = [shares[0], partner(shares[1], "c")]
+        shares = [share.reshape(pairs, 2, owned, 3 * wide) for share in shares]
+        kept, sent = split(places, Y, shares, 1)
+        return dict(qkv_kept=kept, qkv_sent=sent)
+
+    @step
+    def grad_qkv_y():
+        return dict(qkv_kept=total(places, live.take.qkv_kept, partner(live.take.qkv_sent, "y")))
+
+    @step
+    def grad_qkv_slices():
+        return dict(grad_qkv=lax.all_to_all(live.take.qkv_kept, chips, 0, 0, tiled=True))
 
     tokens, cot, low_one = call(
         enter_kernel,
-        "enter",
         [block_low] * 3,
         places,
         inputs,
@@ -543,341 +887,175 @@
         cotangent,
         partner(cotangent, "c"),
     )
-    scaled_qkv = (w_qkv.astype(f32) * gain_one).astype(bf16)
-    slices = scaled_qkv.reshape(owned, 3, pairs, wide).transpose(2, 0, 1, 3)
-    live = {"tokens": tokens, "cot": cot, "one0": low_one}
-    live |= {"slices": slices.reshape(pairs, owned, 3 * wide), "attn": w_attn_out}
-    live |= {"in": w_in, "out": w_out, "places": places}
-    live = fence(live)
-
-    one4 = partner(live["one0"], "zh")
-    one2 = partner(live["one0"], "zl")
-    one1 = partner(live["one0"], "x")
-    cot_x = partner(live["cot"], "x")
-    qkv = lax.all_to_all(live.pop("slices"), chips, 0, 0, tiled=True)[:, None]
-    full = live.pop("attn")
-    full = jnp.stack([full, partner(full, "y")])
-    scaled_in = (live.pop("in").astype(f32) * gain_two).astype(bf16)
-    packed = jnp.concatenate(
-        [
-            columns_by(scaled_in[:, :ff], squares, piece),
-            columns_by(scaled_in[:, ff:], squares, piece),
-            columns_by(jnp.transpose(live.pop("out")), squares, piece),
-        ],
-        axis=2,
-    )
-    live |= {"one1": one1, "one2": one2, "one4": one4, "full": full, "packed": packed}
-    live["cot_x"] = cot_x
-    live = fence(live)
-
-    places = live["places"]
-    one6 = partner(live["one4"], "zl")
-    one5 = partner(live["one4"], "x")
-    one3 = partner(live["one2"], "x")
-    packed = lax.all_to_all(live.pop("packed"), square, 0, 0, tiled=True)[None]
-    full = live.pop("full")
-    full = jnp.stack([full, partner(full, "zh")])
-    lane = jnp.arange(wide, dtype=jnp.int32)
-    frequency = rope_base ** (-2.0 * (lane % half).astype(f32) / size)
-    sign = jnp.where(lane % size < half, -1.0, 1.0)
-    row = jnp.arange(span, dtype=jnp.int32)
-    at = (places[CHIP] ^ (row // block)) * block + (places[C] ^ (row % block // half_block)) * half_block
-    at = ri * span + at + row % half_block
-    angles = at.astype(f32)[:, None] * frequency[None, :]
-    table = jnp.concatenate([jnp.cos(angles), jnp.sin(angles) * sign], axis=1)
-    live |= {"one3": one3, "one5": one5, "one6": one6, "qkv": qkv, "table": table, "full": full}
-    live["packed"] = packed
-    live = fence(live)
-
-    one7 = partner(live["one6"], "x")
-    qkv = live.pop("qkv")
-    qkv = [qkv, partner(qkv, "y")]
-    qkv = qkv + [partner(member, "c") for member in qkv]
-    cot_z = partner(live["cot"], "zl")
-    full = live.pop("full")
-    full = jnp.stack([full, partner(full, "zl")], axis=1)
-    pair_qkv = over_rings(assemble(places, None, C, Y, qkv)).reshape(width, 3 * wide)
-    live |= {"one7": one7, "qkv": pair_qkv, "full": full}
-    live = fence(live)
-
-    full_x = partner(live["full"], "x")
-    packed_far = partner(live["packed"], "zh")
-    packed_y = partner(live["packed"], "y")
+    live.put(-1, tokens=tokens, cot=cot, one0=low_one, places=places)
+    live.put(-1, w_qkv=w_qkv, w_attn_out=w_attn_out, w_in=w_in, w_out=w_out)
+    reach(-1)
+
+    one1, one2, one4 = (partner(live.one0, name) for name in ("x", "zl", "zh"))
+    live.put(ROUND_1, one1=one1, one2=one2, one4=one4)
+    reach(ROUND_1)
+    places = live.places
+
+    one3, one5, one6 = partner(live.one2, "x"), partner(live.one4, "x"), partner(live.one4, "zl")
+    live.put(ROUND_2, one3=one3, one5=one5, one6=one6)
+    reach(ROUND_2)
+
+    live.put(ROUND_3, one7=partner(live.one6, "x"))
+    reach(ROUND_3)
+
+    take = live.take
+    parts = [take.one0, take.one1, take.one2, take.one3, take.one4, take.one5, take.one6, take.one7]
     projected, all_one = call(
         functools.partial(project_kernel, half),
-        "project",
         [((span, 3 * wide), bf16), ((span, width), bf16)],
         places,
-        *[live.pop(f"one{j}") for j in range(8)],
-        live["qkv"],
-        live["table"],
-        flops=6 * span * width * wide,
+        *parts,
+        live.qkv,
+        live.table,
     )
     projected = [projected]
     if rings > 1:
         projected += [lax.all_gather(projected[0][:, wide:], "r", axis=0, tiled=True)]
-    count = projected[-1].shape[0]
-    step = 2 * block if count <= 2048 else block
+    rows = 2 * block if count <= 2048 else block
     heads_out, logs = call(
         functools.partial(attend_kernel, size),
-        "attend",
-        [((pairs, block, wide), bf16), ((span // step, 8, step), f32)],
+        [((pairs, block, wide), bf16), ((span // rows, 8, rows), f32)],
         places,
         *projected,
         mib=24,
-        flops=16 * span * count * wide,
-        exps=2 * span * count,
-    )
-    live |= {"heads": heads_out, "full_x": full_x, "cot_z": cot_z}
-    live = fence(live)
-
-    arrived = lax.all_to_all(live.pop("heads"), chips, 0, 0, tiled=True)
-    cot_zx = partner(live["cot_z"], "x")
-    full = [member.reshape(4, 2, owned, width) for member in (live.pop("full"), live.pop("full_x"))]
-    full = full + [partner(member, "c") for member in full]
-    full_attn = over_rings(assemble_rows(places, full)).reshape(width, width)
-    live |= {"arrived": arrived, "attn": full_attn}
-    live |= {"far": packed_far, "packed_y": packed_y, "cot_zx": cot_zx}
-    live = fence(live)
-
-    far_y = partner(live["far"], "y")
+    )
+    live.put(ATTEND, heads=heads_out)
+    reach(ATTEND)
+
+    live.put(RETURN, arrived=lax.all_to_all(live.take.heads, chips, 0, 0, tiled=True))
+    reach(RETURN)
+
     attended, middle, low_two = call(
         middle_kernel,
-        "middle",
         [block_low, block_full, block_low],
         places,
-        live.pop("arrived"),
-        live["attn"],
-        live["tokens"],
-        flops=2 * block * width * width,
-    )
-    live |= {"attended": attended, "middle": middle, "two": low_two}
-    live = fence(live)
-
-    over_x = partner(live["two"], "x")
-    over_z = partner(live["two"], "zl")
-    over_both = opposite(live["two"], ("zl", "x"))
-    all_cotangent = [live[name] for name in ("cot", "cot_x", "cot_z", "cot_zx")]
-    all_cotangent += [partner(member, "c") for member in all_cotangent]
-    packed = [live.pop("packed"), live.pop("packed_y"), live.pop("far"), far_y]
-    weights = assemble(places, None, ZH, Y, packed)
-    live["weights"] = over_rings(weights).reshape(width, 3 * piece)
-    live |= {"over_x": over_x, "over_z": over_z, "over_both": over_both}
-    live = fence(live)
-
-    all_two = [live.pop(name) for name in ("two", "over_x", "over_z", "over_both")]
+        live.take.arrived,
+        live.attn,
+        live.tokens,
+    )
+    live.put(MIDDLE, attended=attended, middle=middle, two=low_two)
+    reach(MIDDLE)
+
+    over_x, over_z = partner(live.two, "x"), partner(live.two, "zl")
+    live.put(SPREAD, over_x=over_x, over_z=over_z, over_both=opposite(live.two, ("zl", "x")))
+    reach(SPREAD)
+
+    def all_cotangent():
+        here = [live.cot, live.cot_x, live.cot_z, live.cot_zx]
+        return here + [live.core, live.core_x, live.core_z, live.core_zx]
+
+    all_two = [live.take.two, live.take.over_x, live.take.over_z, live.take.over_both]
     all_two += [partner(member, "c") for member in all_two]
-    hidden, grad_gate_up, terms = feed(places, all_two, all_cotangent, live["weights"])
-    live |= {"hidden": hidden, "gate_up": grad_gate_up}
-    live |= {"here": terms[0], "there": terms[1]}
-    live = fence(live)
-
-    sums = chip_sums(places, live.pop("here"), live.pop("there"))
-    live |= {f"sum{j}": member for j, member in enumerate(sums)}
-    live = fence(live)
-
-    sums = [live.pop(f"sum{j}") for j in range(4)]
-    over_both = opposite(sums[3], ("zl", "x"))
-    over_x = partner(sums[1], "x")
-    over_z = partner(sums[2], "zl")
-    direct = rings == 1 and owned % 16 == 0
-    shape = (2 * squares, owned, 3 * piece)
-    result, shares = feed_rest(
-        places,
-        all_two,
-        all_cotangent,
-        live.pop("hidden"),
-        live.pop("gate_up"),
-        live.pop("weights"),
-        [shape] * 2 if direct else [(width, 3 * piece)],
-    )
-    if not direct:
-        terms = ring_sums(shares[0]).reshape(2 * squares, 2, owned, 3 * piece)
-        shares = split(places, Y, [terms], 1)
-    weights_kept, weights_y = shares[0], partner(shares[1], "y")
-    live |= {"result_here": result[0], "result_there": result[1]}
-    live |= {f"sum{j}": m for j, m in enumerate([sums[0], over_x, over_z, over_both])}
-    live["weights_kept"] = weights_kept
-    live = fence(live)
-
+    begin(FEED)
+    hidden, grad_gate_up, terms = feed(places, all_two, all_cotangent(), live.weights)
+    live.put(FEED, hidden=hidden, gate_up=grad_gate_up, here=terms[0], there=terms[1])
+    reach(FEED)
+
+    sums = chip_sums(places, live.take.here, live.take.there)
+    live.put(CHIP, sum0=sums[0], sum1=sums[1], sum2=sums[2], sum3=sums[3])
+    reach(CHIP)
+
+    over_both = opposite(live.take.sum3, ("zl", "x"))
+    over_x, over_z = partner(live.take.sum1, "x"), partner(live.take.sum2, "zl")
+    live.put(COLLECT, sum1=over_x, sum2=over_z, sum3=over_both)
+    reach(COLLECT)
+
+    take = live.take
     grad_middle, grad_branch, leaving = call(
         middle_back_kernel,
-        "middle_back",
         [block_full, block_low, ((pairs, block, wide), bf16)],
         places,
-        live["middle"],
-        live.pop("cot"),
-        live.pop("attn"),
-        *[live.pop(f"sum{j}") for j in range(4)],
-        flops=2 * block * width * width,
-    )
-    live |= {"grad_middle": grad_middle, "branch": grad_branch, "leaving": leaving}
-    live = fence(live)
-
-    grad_heads = lax.all_to_all(live.pop("leaving"), chips, 0, 0, tiled=True)
-    result = chip_sums(places, live.pop("result_here"), live.pop("result_there"))
-    result_both = opposite(result[3], ("zl", "x"))
-    result_x = partner(result[1], "x")
-    result_z = partner(result[2], "zl")
-    live["result0"] = result[0]
-    shape = (pairs, 2 * owned, width)
-    shares = call(
-        outer_kernel,
-        "outer",
-        [(shape, bf16)] * 2 if direct else [((width, width), bf16)],
-        places,
-        live.pop("attended"),
-        live.pop("branch"),
-        flops=2 * block * width * width,
-    )
-    if not direct:
-        shares = split(places, C, [ring_sums(shares[0]).reshape(pairs, 2, 2 * owned, width)], 1)
-    shares = [shares[0], partner(shares[1], "c")]
-    shares = [share.reshape(8, 2, owned, width) for share in shares]
-    live["attn_kept"], live["attn_sent"] = split(places, Y, shares, 1)
-    live |= {"grad_heads": grad_heads, "weights_y": weights_y}
-    live = fence(live)
-
-    attn_y = partner(live.pop("attn_sent"), "y")
+        live.middle,
+        live.cot,
+        live.attn,
+        take.sum0,
+        take.sum1,
+        take.sum2,
+        take.sum3,
+    )
+    live.put(MIDDLE_BACK, grad_middle=grad_middle, branch=grad_branch, leaving=leaving)
+    reach(MIDDLE_BACK)
+
+    live.put(LEAVE, grad_heads=lax.all_to_all(live.take.leaving, chips, 0, 0, tiled=True))
+    reach(LEAVE)
+
     kernel = functools.partial(attend_back_kernel, size, rings == 1)
-    parts = projected + [live.pop("grad_heads"), logs, live["table"]]
+    parts = projected + [live.take.grad_heads, logs, live.table]
     if rings == 1:
         grad_projected = call(
             kernel,
-            "attend_back",
             [((span, 3 * wide), bf16)],
             places,
             *parts,
             scratch=[pltpu.VMEM((count, wide), f32)] * 2,
             mib=24,
-            flops=40 * span * count * wide,
-            exps=2 * span * count,
         )[0]
     else:
         outs = [((span, wide), bf16), ((count, wide), f32), ((count, wide), f32)]
-        grad_q, grad_k, grad_v = call(kernel, "attend_back", outs, places, *parts, mib=36)
+        grad_q, grad_k, grad_v = call(kernel, outs, places, *parts, mib=36)
         grad_projected = call(
             functools.partial(turn_back_kernel, half),
-            "turn_back",
             [((span, 3 * wide), bf16)],
             places,
             grad_q,
             ring_sums(grad_k),
             ring_sums(grad_v),
-            live["table"],
+            live.table,
         )[0]
     terms = call(
-        project_back_kernel,
-        "project_back",
-        [((2 * block, width), bf16)] * 4,
-        places,
-        grad_projected,
-        live["qkv"],
-        flops=6 * span * width * wide,
-    )
-    live |= dict(zip(("kept_far", "sent_far", "kept_near", "sent_near"), terms))
-    live["projected"] = grad_projected
-    live |= {"result_x": result_x, "result_z": result_z, "result_both": result_both}
-    live["attn_y"] = attn_y
-    live = fence(live)
-
-    over_x = partner(live.pop("sent_far"), "x")
-    shares = [live.pop("weights_kept"), live.pop("weights_y")]
-    shares = [share.reshape(1, 2, squares * owned, 3 * piece) for share in shares]
-    live["weights_kept"], sent = split(places, ZH, shares, 1)
-    weights_far = partner(sent, "zh")
-    shape = (pairs, 2 * owned, 3 * wide)
-    shares = call(
-        project_outer_kernel,
-        "project_outer",
-        [(shape, bf16)] * 2 if direct else [((width, 3 * wide), bf16)],
-        places,
-        all_one,
-        live.pop("projected"),
-        flops=6 * span * width * wide,
-    )
-    if not direct:
-        shares = split(places, C, [ring_sums(shares[0]).reshape(pairs, 2, 2 * owned, 3 * wide)], 1)
-    shares = [shares[0], partner(shares[1], "c")]
-    shares = [share.reshape(pairs, 2, owned, 3 * wide) for share in shares]
-    live["qkv_kept"], live["qkv_sent"] = split(places, Y, shares, 1)
-    shares = [share.reshape(2, 2, 2 * owned, width) for share in (live.pop("attn_kept"), live.pop("attn_y"))]
-    live["attn_kept"], sent = split(places, ZL, shares, 1)
-    live["attn_zl"] = partner(sent, "zl")
-    live["sum6"], live["sum4"] = call(
-        far_sums_kernel, "far_sums", [block_low] * 2, places, live.pop("kept_far"), over_x
-    )
-    live = fence(live)
-
-    both = partner(live.pop("sum6"), "zl")
-    over_x = partner(live.pop("sent_near"), "x")
-    qkv_y = partner(live.pop("qkv_sent"), "y")
-    shares = [share.reshape(2, 2, owned, width) for share in (live.pop("attn_kept"), live.pop("attn_zl"))]
-    live["attn_kept"], sent = split(places, X, shares, 1)
-    live["attn_x"] = partner(sent, "x")
-    live["sum2"], live["sum0"], live["sum4"] = call(
+        project_back_kernel, [((2 * block, width), bf16)] * 4, places, grad_projected, live.qkv
+    )
+    live.put(ATTEND_BACK, projected=grad_projected, kept_far=terms[0], sent_far=terms[1])
+    live.put(ATTEND_BACK, kept_near=terms[2], sent_near=terms[3])
+    reach(ATTEND_BACK)
+
+    over_x = partner(live.take.sent_far, "x")
+    six, four = call(far_sums_kernel, [block_low] * 2, places, live.take.kept_far, over_x)
+    live.put(OVER_X, six=six, four=four)
+    reach(OVER_X)
+
+    both = partner(live.take.six, "zl")
+    over_x = partner(live.take.sent_near, "x")
+    two, own, four = call(
         near_sums_kernel,
-        "near_sums",
         [block_low] * 3,
         places,
-        live.pop("kept_near"),
+        live.take.kept_near,
         over_x,
-        live["sum4"],
+        live.take.four,
         both,
     )
-    live["qkv"] = total(places, live.pop("qkv_kept"), qkv_y)
-    live = fence(live)
-
-    far = partner(live.pop("sum4"), "zh")
-    near = partner(live.pop("sum2"), "zl")
-    shares = [share.reshape(squares, owned, 3 * piece) for share in (live.pop("weights_kept"), weights_far)]
-    grad_packed = lax.all_to_all(total(places, *shares), square, 0, 0, tiled=True)
-    shares = [share.reshape(1, 2, owned, width) for share in (live.pop("attn_kept"), live.pop("attn_x"))]
-    kept_attn, sent = split(places, ZH, shares, 1)
-    attn_zh = partner(sent, "zh")
-    half_result, sent = call(
-        result_kernel,
-        "result",
-        [half_low] * 2,
-        places,
-        live["middle"],
-        live["result0"],
-        live["result_x"],
-        live["result_z"],
-        live["result_both"],
-    )
-    output = call(
-        leave_kernel, "leave", [(inputs.shape, bf16)], places, half_result, partner(sent, "c")
-    )[0]
-    live |= {"far": far, "near": near, "output": output, "grad_packed": grad_packed}
-    live |= {"attn_kept": kept_attn, "attn_zh": attn_zh}
-    live = fence(live)
-    output, grad_packed = live["output"], live["grad_packed"]
-    grad_qkv = lax.all_to_all(live.pop("qkv"), chips, 0, 0, tiled=True)
-    grad_attn = (live["attn_kept"].astype(f32) + live["attn_zh"].astype(f32))[0]
+    live.put(OVER_ZL, two=two, own=own, four=four)
+    reach(OVER_ZL)
+
+    live.put(OVER_ZH, far=partner(live.take.four, "zh"), near=partner(live.take.two, "zl"))
+    reach(OVER_ZH)
 
     kept, sent = call(
         tokens_back_kernel,
-        "tokens_back",
         [half_full] * 2,
         places,
-        live["tokens"],
-        live["grad_middle"],
-        live["sum0"],
-        live["near"],
-        live["far"],
-    )
-    input_grad = call(
-        leave_kernel, "leave", [(inputs.shape, f32)], places, kept, partner(sent, "c")
-    )[0]
-
-    grad_qkv = grad_qkv.astype(f32)
-    grad_packed = grad_packed.astype(f32)
-    grad_qkv = grad_qkv.reshape(pairs, owned, 3, wide)
+        live.tokens,
+        live.grad_middle,
+        live.own,
+        live.near,
+        live.far,
+    )
+    input_grad = call(leave_kernel, [(inputs.shape, f32)], places, kept, partner(sent, "c"))[0]
+    reach(LAST)
+
+    grad_attn = (live.attn_kept.astype(f32) + live.attn_other.astype(f32))[0]
+    grad_qkv = live.grad_qkv.astype(f32).reshape(pairs, owned, 3, wide)
     grad_qkv = grad_qkv.transpose(1, 2, 0, 3).reshape(owned, 3 * width)
     grad_gain_attn = jnp.sum(grad_qkv * w_qkv.astype(f32), axis=1)
     grad_qkv = grad_qkv * gain_one
 
+    grad_packed = live.grad_packed.astype(f32)
     grad_in = jnp.concatenate(
         [
             columns_back(grad_packed[:, :, :piece], ff),
@@ -889,7 +1067,7 @@
     grad_gain_mlp = jnp.sum(grad_in * w_in.astype(f32), axis=1)
     grad_in = grad_in * gain_two
     return (
-        output,
+        live.output,
         input_grad,
         grad_gain_attn,
         grad_gain_mlp,

time: 256 us -> 256 us (level)
    ppermute x56, waiting for transfers between devices: 65.9 us -> 76.4 us  [partner(): return lax.ppermute(array, axis, [(0, 1), (1, 0)])]
    ppermute x3, waiting for transfers between devices: 10.9 us -> 4.54 us  [opposite(): return lax.ppermute(array, axes, [(i, 3 - i) for i in range(4)])]
    unnamed x92 -> x94, local copies, waits for them, and re-layouts: 13.9 us -> 14.3 us
  transfers between devices with their start and end apart: 65 -> 65, of which waited for: 29 -> 28; matrix products, arithmetic and copies ran while one was open for 5% -> 6% of each run, Pallas kernels for 21% -> 21%
where the time goes in v4:
time: 256 us; the launch traced here: 254 us
  waiting for transfers between devices  82.2 us (32%)
  starting transfers between devices  78.2 us (31%)
  Pallas kernels  61.7 us (24%)
  local copies, waits for them, and re-layouts  17.5 us (7%)
  other arithmetic  13.3 us (5%)
    ppermute x56, waiting for transfers between devices, partner(): return lax.ppermute(array, axis, [(0, 1), (1, 0)])  76.4 us
    pallas_call x30, Pallas kernels, call(): pl.pallas_call(kernel, in_specs=[pl.BlockSpec(memory_space=pltpu.SMEM)] +...  61.7 us
    ppermute x56, starting transfers between devices, partner(): return lax.ppermute(array, axis, [(0, 1), (1, 0)])  52.2 us
    unnamed x94, local copies, waits for them, and re-layouts  14.3 us
  transfers between devices with their start and end apart: 65, of which 28 were waited for; matrix products, arithmetic and copies ran while one was open for 6% of the time, Pallas kernels for 21%

profile of v4, /device:TPU:0, one launch (start us, length us, event | category | flops | bytes accessed | tf_op | source)
XLA Modules:
  0.0 254.4 jit_solution(5870771315217615022)
XLA Ops:
  6.2 4.0 %collective-permute-start.4 = (bf16[128,1024]{1,0:T(8,128)(2,1)S(1)}, bf16[128,1024]{1,0:T(8,128)(2,1)S(1)}, u32[]{:S(2)}, u32[]{:S(2)}) collective-permute-start(bf16[128,1024]{1,0:T(8,128)(2,1)S(1)} %get-tuple-element.320.refs_0_), channel_id=1, source_target_pairs={{0,16},{16,0},{1,17},{17,1},{2,18},{18,2},{3,19},{19,3},{4,20},{20... | collective-permute-start | bytes 786440 | tf_op jit(solution)/shard_map/ppermute | solution.py:22
  13.3 3.4 %all-to-all-start = ((bf16[8,32,384]{2,1,0:T(8,128)(2,1)}), bf16[8,32,384]{2,1,0:T(8,128)(2,1)S(1)}, u32[]{:S(2)}, u32[]{:S(2)}) async-start(bf16[8,32,384]{2,1,0:T(8,128)(2,1)} %reshape.182), calls=%async_computation | async-start | bytes 393216 | tf_op jit(solution)/shard_map/all_to_all | solution.py:636
  16.7 1.9 collective-permute-start.5
  20.0 7.1 %collective-permute-done.5.refs_9_ = bf16[128,1024]{1,0:T(8,128)(2,1)S(1)} collective-permute-done((bf16[128,1024]{1,0:T(8,128)(2,1)S(1)}, bf16[128,1024]{1,0:T(8,128)(2,1)S(1)}, u32[]{:S(2)}, u32[]{:S(2)}) %collective-permute-start.5) | collective-permute-done | bytes 262176 | tf_op jit(solution)/shard_map/ppermute | solution.py:22
  27.7 4.2 %all-to-all-start.1 = ((bf16[8,32,1152]{2,1,0:T(8,128)(2,1)}), bf16[8,32,1152]{2,1,0:T(8,128)(2,1)}, u32[]{:S(2)}, u32[]{:S(2)}) async-start(bf16[8,32,1152]{2,1,0:T(8,128)(2,1)} %pad_maximum_fusion.2), calls=%async_computation.1 | async-start | bytes 1179648 | tf_op jit(solution)/shard_map/all_to_all | solution.py:661
  35.5 1.9 multiply_cosine_fusion
  37.4 2.0 collective-permute-start.10
  41.4 2.1 collective-permute-start.7
  43.6 4.2 %collective-permute-done.7 = bf16[2,32,1024]{2,1,0:T(8,128)(2,1)S(1)} collective-permute-done((bf16[2,32,1024]{2,1,0:T(8,128)(2,1)S(1)}, bf16[2,32,1024]{2,1,0:T(8,128)(2,1)S(1)}, u32[]{:S(2)}, u32[]{:S(2)}) %collective-permute-start.7) | collective-permute-done | bytes 131104 | tf_op jit(solution)/shard_map/ppermute | solution.py:22
  48.5 4.3 %collective-permute-done.8.refs_3_ = bf16[128,1024]{1,0:T(8,128)(2,1)S(1)} collective-permute-done((bf16[128,1024]{1,0:T(8,128)(2,1)S(1)}, bf16[128,1024]{1,0:T(8,128)(2,1)S(1)}, u32[]{:S(2)}, u32[]{:S(2)}) %collective-permute-start.8) | collective-permute-done | bytes 262176 | tf_op jit(solution)/shard_map/ppermute | solution.py:22
  56.2 2.6 %collective-permute-done.13.b_ref = bf16[8,1,32,384]{3,2,1,0:T(8,128)(2,1)S(1)} collective-permute-done((bf16[8,1,32,384]{3,2,1,0:T(8,128)(2,1)S(1)}, bf16[8,1,32,384]{3,2,1,0:T(8,128)(2,1)S(1)}, u32[]{:S(2)}, u32[]{:S(2)}) %collective-permute-start.13) | collective-permute-done | bytes 196640 | tf_op jit(solution)/shard_map/ppermute | solution.py:22
  58.8 3.1 %collective-permute-done.11 = bf16[2,2,32,1024]{3,2,1,0:T(8,128)(2,1)S(1)} collective-permute-done((bf16[2,2,32,1024]{3,2,1,0:T(8,128)(2,1)}, bf16[2,2,32,1024]{3,2,1,0:T(8,128)(2,1)S(1)}, u32[]{:S(2)}, u32[]{:S(2)}) %collective-permute-start.11) | collective-permute-done | bytes 262176 | tf_op jit(solution)/shard_map/ppermute | solution.py:22
  63.9 1.7 collective-permute-start.16
  66.0 2.1 collective-permute-start.18
  68.1 2.0 project_kernel.1
  71.4 7.8 %attend_kernel.1 = (bf16[8,128,128]{2,1,0:T(8,128)(2,1)S(1)}, f32[4,8,256]{2,1,0:T(8,128)S(1)}) custom-call(s32[6]{0:T(128)S(1)} %stack.54.places, bf16[1024,384]{1,0:T(8,128)(2,1)S(1)} %get-tuple-element.328.refs_0_), custom_call_target="tpu_custom_call" | custom-call | bytes 1081344 | tf_op jit(solution)/shard_map/attend_kernel/pallas_call | solution.py:122
  80.0 3.6 %all-to-all-start.2 = ((bf16[8,128,128]{2,1,0:T(8,128)(2,1)}), bf16[8,128,128]{2,1,0:T(8,128)(2,1)S(1)}, u32[]{:S(2)}, u32[]{:S(2)}) async-start(bf16[8,128,128]{2,1,0:T(8,128)(2,1)} %copy-done.30), calls=%async_computation.2 | async-start | bytes 524288 | tf_op jit(solution)/shard_map/all_to_all | solution.py:930
  83.6 1.7 collective-permute-start.22
  91.8 5.7 %collective-permute-done.18.c_ref = bf16[1,8,32,1152]{3,2,1,0:T(8,128)(2,1)} collective-permute-done((bf16[1,8,32,1152]{3,2,1,0:T(8,128)(2,1)}, bf16[1,8,32,1152]{3,2,1,0:T(8,128)(2,1)}, u32[]{:S(2)}, u32[]{:S(2)}) %collective-permute-start.18) | collective-permute-done | bytes 589856 | tf_op jit(solution)/shard_map/ppermute | solution.py:22
  103.1 2.2 collective-permute-start.24
  105.7 6.7 %collective-permute-done.26.d_ref = bf16[1,8,32,1152]{3,2,1,0:T(8,128)(2,1)S(1)} collective-permute-done((bf16[1,8,32,1152]{3,2,1,0:T(8,128)(2,1)}, bf16[1,8,32,1152]{3,2,1,0:T(8,128)(2,1)S(1)}, u32[]{:S(2)}, u32[]{:S(2)}) %collective-permute-start.26) | collective-permute-done | bytes 589856 | tf_op jit(solution)/shard_map/ppermute | solution.py:22
  118.9 6.3 %feed_kernel.1 = (bf16[1024,384]{1,0:T(8,128)(2,1)S(1)}, bf16[1024,768]{1,0:T(8,128)(2,1)S(1)}, bf16[512,1024]{1,0:T(8,128)(2,1)S(1)}, bf16[512,1024]{1,0:T(8,128)(2,1)S(1)}) custom-call(s32[6]{0:T(128)S(1)} %stack.54.places, bf16[128,1024]{1,0:T(8,128)(2,1)S(1)} %get-tuple-element.380.refs_0_, bf16[128,1024]{1,0:T(8,128)(2,1)S(1)} %collective-permute-done.23.refs_1_, ...), custom_call_target="tpu_custom_call" | custom-call | flops 4026531840 | bytes 11010048 | tf_op jit(solution)/shard_map/feed_kernel/pallas_call | solution.py:122
  125.5 2.5 collective-permute-done.35.b_ref
  130.2 2.1 collective-permute-start.38
  132.3 6.0 %feed_rest_kernel.1 = (bf16[512,1024]{1,0:T(8,128)(2,1)S(1)}, bf16[512,1024]{1,0:T(8,128)(2,1)}, bf16[16,32,1152]{2,1,0:T(8,128)(2,1)S(1)}, bf16[16,32,1152]{2,1,0:T(8,128)(2,1)}) custom-call(s32[6]{0:T(128)S(1)} %stack.54.places, bf16[128,1024]{1,0:T(8,128)(2,1)S(1)} %get-tuple-element.380.refs_0_, bf16[128,1024]{1,0:T(8,128)(2,1)S(1)} %collective-permute-done.23.refs_1_, ...), custom_call_target="tpu_custom_call" | custom-call | flops 3221225472 | bytes 13369344 | tf_op jit(solution)/shard_map/feed_rest_kernel/pallas_call | solution.py:122
  139.4 4.5 %collective-permute-done.38.d_ref = bf16[128,1024]{1,0:T(8,128)(2,1)S(1)} collective-permute-done((bf16[128,1024]{1,0:T(8,128)(2,1)S(1)}, bf16[128,1024]{1,0:T(8,128)(2,1)S(1)}, u32[]{:S(2)}, u32[]{:S(2)}) %collective-permute-start.38) | collective-permute-done | bytes 262176 | tf_op jit(solution)/shard_map/ppermute | solution.py:26
  144.0 1.7 middle_back_kernel.1
  146.6 2.5 outer_kernel.1
  149.6 3.9 %all-to-all-start.3 = ((bf16[8,128,128]{2,1,0:T(8,128)(2,1)}), bf16[8,128,128]{2,1,0:T(8,128)(2,1)S(1)}, u32[]{:S(2)}, u32[]{:S(2)}) async-start(bf16[8,128,128]{2,1,0:T(8,128)(2,1)} %copy-done.29), calls=%async_computation.3 | async-start | bytes 524288 | tf_op jit(solution)/shard_map/all_to_all | solution.py:984
  153.5 2.2 chip_sums_kernel.3
  156.4 2.0 collective-permute-start.42
  163.0 2.8 %collective-permute-done.39 = bf16[16,32,1152]{2,1,0:T(8,128)(2,1)} collective-permute-done((bf16[16,32,1152]{2,1,0:T(8,128)(2,1)}, bf16[16,32,1152]{2,1,0:T(8,128)(2,1)}, u32[]{:S(2)}, u32[]{:S(2)}) %collective-permute-start.39) | collective-permute-done | bytes 1179680 | tf_op jit(solution)/shard_map/ppermute | solution.py:22
  166.8 9.3 %attend_back_kernel.1.grad_ref = bf16[1024,384]{1,0:T(8,128)(2,1)S(1)} custom-call(s32[6]{0:T(128)S(1)} %stack.54.places, bf16[1024,384]{1,0:T(8,128)(2,1)S(1)} %copy-done.3, bf16[8,128,128]{2,1,0:T(8,128)(2,1)S(1)} %all-to-all-done.3.refs_1_, f32[4,8,256]{2,1,0:T(8,128)S(1)} %get-tuple-element.467.refs_2_, f32[1024,256]{1,0:T(8,128)S(1)} %pad_maximum_fusion.refs_9_.refs_3_), custom_call_target="tpu_custom_call" | custom-call | bytes 2916352 | tf_op jit(solution)/shard_map/attend_back_kernel/pallas_call | solution.py:122
  176.2 1.8 project_back_kernel.1
  179.5 1.9 project_outer_kernel.1
  184.1 2.2 collective-permute-start.49
  186.9 3.1 %collective-permute-done.45.across_ref = bf16[256,1024]{1,0:T(8,128)(2,1)S(1)} collective-permute-done((bf16[256,1024]{1,0:T(8,128)(2,1)S(1)}, bf16[256,1024]{1,0:T(8,128)(2,1)S(1)}, u32[]{:S(2)}, u32[]{:S(2)}) %collective-permute-start.45) | collective-permute-done | bytes 524320 | tf_op jit(solution)/shard_map/ppermute | solution.py:22
  190.7 3.4 %collective-permute-done.47 = bf16[2,64,1024]{2,1,0:T(8,128)(2,1)S(1)} collective-permute-done((bf16[2,64,1024]{2,1,0:T(8,128)(2,1)S(1)}, bf16[2,64,1024]{2,1,0:T(8,128)(2,1)S(1)}, u32[]{:S(2)}, u32[]{:S(2)}) %collective-permute-start.47) | collective-permute-done | bytes 262176 | tf_op jit(solution)/shard_map/ppermute | solution.py:22
  197.8 3.2 %collective-permute-done.53.b_ref = bf16[8,32,384]{2,1,0:T(8,128)(2,1)S(1)} collective-permute-done((bf16[8,32,384]{2,1,0:T(8,128)(2,1)S(1)}, bf16[8,32,384]{2,1,0:T(8,128)(2,1)S(1)}, u32[]{:S(2)}, u32[]{:S(2)}) %collective-permute-start.53) | collective-permute-done | bytes 196640 | tf_op jit(solution)/shard_map/ppermute | solution.py:22
  202.3 4.8 %collective-permute-done.51.both_ref = bf16[128,1024]{1,0:T(8,128)(2,1)S(1)} collective-permute-done((bf16[128,1024]{1,0:T(8,128)(2,1)S(1)}, bf16[128,1024]{1,0:T(8,128)(2,1)S(1)}, u32[]{:S(2)}, u32[]{:S(2)}) %collective-permute-start.51) | collective-permute-done | bytes 262176 | tf_op jit(solution)/shard_map/ppermute | solution.py:22
  207.0 1.9 collective-permute-done.50.across_ref
  209.7 3.5 %collective-permute-done.49 = bf16[1,256,1152]{2,1,0:T(8,128)(2,1)S(1)} collective-permute-done((bf16[1,256,1152]{2,1,0:T(8,128)(2,1)S(1)}, bf16[1,256,1152]{2,1,0:T(8,128)(2,1)S(1)}, u32[]{:S(2)}, u32[]{:S(2)}) %collective-permute-start.49) | collective-permute-done | bytes 589856 | tf_op jit(solution)/shard_map/ppermute | solution.py:22
  214.7 4.2 %all-to-all-start.4 = ((bf16[8,32,1152]{2,1,0:T(8,128)(2,1)}), bf16[8,32,1152]{2,1,0:T(8,128)(2,1)}, u32[]{:S(2)}, u32[]{:S(2)}) async-start(bf16[8,32,1152]{2,1,0:T(8,128)(2,1)} %total_kernel.3), calls=%async_computation.4 | async-start | bytes 1179648 | tf_op jit(solution)/shard_map/all_to_all | solution.py:807
  219.0 2.3 collective-permute-start.55
  223.2 2.5 collective-permute-start.57
  227.0 12.0 %collective-permute-done.57 = bf16[1,32,1024]{2,1,0:T(8,128)(2,1)S(1)} collective-permute-done((bf16[1,32,1024]{2,1,0:T(8,128)(2,1)S(1)}, bf16[1,32,1024]{2,1,0:T(8,128)(2,1)S(1)}, u32[]{:S(2)}, u32[]{:S(2)}) %collective-permute-start.57) | collective-permute-done | bytes 65568 | tf_op jit(solution)/shard_map/ppermute | solution.py:22
  238.9 2.0 collective-permute-done.55.b_ref
  241.0 3.7 %all-to-all-start.5 = ((bf16[8,32,384]{2,1,0:T(8,128)(2,1)}), bf16[8,32,384]{2,1,0:T(8,128)(2,1)S(1)}, u32[]{:S(2)}, u32[]{:S(2)}) async-start(bf16[8,32,384]{2,1,0:T(8,128)(2,1)} %total_kernel.2), calls=%async_computation.5 | async-start | bytes 393216 | tf_op jit(solution)/shard_map/all_to_all | solution.py:879
  (242 shorter events, 80.4 us)
Async XLA Ops:
  6.2 20.8 %collective-permute-start.4 = (bf16[128,1024]{1,0:T(8,128)(2,1)S(1)}, bf16[128,1024]{1,0:T(8,128)(2,1)S(1)}, u32[]{:S(2)}, u32[]{:S(2)}) collective-permute-start(bf16[128,1024]{1,0:T(8,128)(2,1)S(1)} %get-tuple-element.320.refs_0_), channel_id=1, source_target_pairs={{0,16},{16,0},{1,17},{17,1},{2,18},{18,2},{3,19},{19,3},{4,20},{20... | collective-permute-start | bytes 786440 | tf_op jit(solution)/shard_map/ppermute | solution.py:22
  10.3 16.8 %collective-permute-start.3 = (bf16[128,1024]{1,0:T(8,128)(2,1)S(1)}, bf16[128,1024]{1,0:T(8,128)(2,1)S(1)}, u32[]{:S(2)}, u32[]{:S(2)}) collective-permute-start(bf16[128,1024]{1,0:T(8,128)(2,1)S(1)} %get-tuple-element.320.refs_0_), channel_id=1, source_target_pairs={{0,8},{8,0},{1,9},{9,1},{2,10},{10,2},{3,11},{11,3},{4,12},{12,4},... | collective-permute-start | bytes 786440 | tf_op jit(solution)/shard_map/ppermute | solution.py:22
  11.8 15.9 %collective-permute-start.2 = (bf16[128,1024]{1,0:T(8,128)(2,1)S(1)}, bf16[128,1024]{1,0:T(8,128)(2,1)S(1)}, u32[]{:S(2)}, u32[]{:S(2)}) collective-permute-start(bf16[128,1024]{1,0:T(8,128)(2,1)S(1)} %get-tuple-element.320.refs_0_), channel_id=1, source_target_pairs={{0,4},{4,0},{1,5},{5,1},{2,6},{6,2},{3,7},{7,3},{8,12},{12,8},{9,1... | collective-permute-start | bytes 786440 | tf_op jit(solution)/shard_map/ppermute | solution.py:22
  13.3 14.4 %all-to-all-start = ((bf16[8,32,384]{2,1,0:T(8,128)(2,1)}), bf16[8,32,384]{2,1,0:T(8,128)(2,1)S(1)}, u32[]{:S(2)}, u32[]{:S(2)}) async-start(bf16[8,32,384]{2,1,0:T(8,128)(2,1)} %reshape.182), calls=%async_computation | async-start | bytes 393216 | tf_op jit(solution)/shard_map/all_to_all | solution.py:636
  16.7 10.3 %collective-permute-start.5 = (bf16[128,1024]{1,0:T(8,128)(2,1)S(1)}, bf16[128,1024]{1,0:T(8,128)(2,1)S(1)}, u32[]{:S(2)}, u32[]{:S(2)}) collective-permute-start(bf16[128,1024]{1,0:T(8,128)(2,1)S(1)} %get-tuple-element.422.refs_8_.cot_ref), channel_id=1, source_target_pairs={{0,4},{4,0},{1,5},{5,1},{2,6},{6,2},{3,7},{7,3},{8,12},{12,8},{9,1... | collective-permute-start | bytes 786440 | tf_op jit(solution)/shard_map/ppermute | solution.py:22
  27.7 25.0 %all-to-all-start.1 = ((bf16[8,32,1152]{2,1,0:T(8,128)(2,1)}), bf16[8,32,1152]{2,1,0:T(8,128)(2,1)}, u32[]{:S(2)}, u32[]{:S(2)}) async-start(bf16[8,32,1152]{2,1,0:T(8,128)(2,1)} %pad_maximum_fusion.2), calls=%async_computation.1 | async-start | bytes 1179648 | tf_op jit(solution)/shard_map/all_to_all | solution.py:661
  32.0 9.4 %collective-permute-start.6 = (bf16[32,1024]{1,0:T(8,128)(2,1)S(1)}, bf16[32,1024]{1,0:T(8,128)(2,1)S(1)}, u32[]{:S(2)}, u32[]{:S(2)}) collective-permute-start(bf16[32,1024]{1,0:T(8,128)(2,1)S(1)} %copy-done.44), channel_id=1, source_target_pairs={{0,1},{1,0},{2,3},{3,2},{4,5},{5,4},{6,7},{7,6},{8,9},{9,8},{10,11... | collective-permute-start | bytes 196616 | tf_op jit(solution)/shard_map/ppermute | solution.py:22
  37.4 15.4 %collective-permute-start.10 = (bf16[128,1024]{1,0:T(8,128)(2,1)S(1)}, bf16[128,1024]{1,0:T(8,128)(2,1)S(1)}, u32[]{:S(2)}, u32[]{:S(2)}) collective-permute-start(bf16[128,1024]{1,0:T(8,128)(2,1)S(1)} %collective-permute-done.4.refs_4_), channel_id=1, source_target_pairs={{0,8},{8,0},{1,9},{9,1},{2,10},{10,2},{3,11},{11,3},{4,12},{12,4},... | collective-permute-start | bytes 786440 | tf_op jit(solution)/shard_map/ppermute | solution.py:22
  39.3 13.4 %collective-permute-start.9 = (bf16[128,1024]{1,0:T(8,128)(2,1)S(1)}, bf16[128,1024]{1,0:T(8,128)(2,1)S(1)}, u32[]{:S(2)}, u32[]{:S(2)}) collective-permute-start(bf16[128,1024]{1,0:T(8,128)(2,1)S(1)} %collective-permute-done.4.refs_4_), channel_id=1, source_target_pairs={{0,4},{4,0},{1,5},{5,1},{2,6},{6,2},{3,7},{7,3},{8,12},{12,8},{9,1... | collective-permute-start | bytes 786440 | tf_op jit(solution)/shard_map/ppermute | solution.py:22
  40.8 11.9 %collective-permute-start.8 = (bf16[128,1024]{1,0:T(8,128)(2,1)S(1)}, bf16[128,1024]{1,0:T(8,128)(2,1)S(1)}, u32[]{:S(2)}, u32[]{:S(2)}) collective-permute-start(bf16[128,1024]{1,0:T(8,128)(2,1)S(1)} %collective-permute-done.3.refs_2_), channel_id=1, source_target_pairs={{0,4},{4,0},{1,5},{5,1},{2,6},{6,2},{3,7},{7,3},{8,12},{12,8},{9,1... | collective-permute-start | bytes 786440 | tf_op jit(solution)/shard_map/ppermute | solution.py:22
  41.4 6.4 %collective-permute-start.7 = (bf16[2,32,1024]{2,1,0:T(8,128)(2,1)S(1)}, bf16[2,32,1024]{2,1,0:T(8,128)(2,1)S(1)}, u32[]{:S(2)}, u32[]{:S(2)}) collective-permute-start(bf16[2,32,1024]{2,1,0:T(8,128)(2,1)S(1)} %get-tuple-element.558), channel_id=1, source_target_pairs={{0,16},{16,0},{1,17},{17,1},{2,18},{18,2},{3,19},{19,3},{4,20},{20... | collective-permute-start | bytes 393224 | tf_op jit(solution)/shard_map/ppermute | solution.py:22
  54.2 7.7 %collective-permute-start.11 = (bf16[2,2,32,1024]{3,2,1,0:T(8,128)(2,1)}, bf16[2,2,32,1024]{3,2,1,0:T(8,128)(2,1)S(1)}, u32[]{:S(2)}, u32[]{:S(2)}) collective-permute-start(bf16[2,2,32,1024]{3,2,1,0:T(8,128)(2,1)} %pad_maximum_fusion.4), channel_id=1, source_target_pairs={{0,8},{8,0},{1,9},{9,1},{2,10},{10,2},{3,11},{11,3},{4,12},{12,4},... | collective-permute-start | bytes 786440 | tf_op jit(solution)/shard_map/ppermute | solution.py:22
  55.7 7.8 %collective-permute-start.12 = (bf16[128,1024]{1,0:T(8,128)(2,1)S(1)}, bf16[128,1024]{1,0:T(8,128)(2,1)S(1)}, u32[]{:S(2)}, u32[]{:S(2)}) collective-permute-start(bf16[128,1024]{1,0:T(8,128)(2,1)S(1)} %collective-permute-done.10.refs_6_), channel_id=1, source_target_pairs={{0,4},{4,0},{1,5},{5,1},{2,6},{6,2},{3,7},{7,3},{8,12},{12,8},{9,1... | collective-permute-start | bytes 786440 | tf_op jit(solution)/shard_map/ppermute | solution.py:22
  56.2 6.6 %collective-permute-start.14 = (bf16[8,1,32,384]{3,2,1,0:T(8,128)(2,1)S(1)}, bf16[8,1,32,384]{3,2,1,0:T(8,128)(2,1)S(1)}, u32[]{:S(2)}, u32[]{:S(2)}) collective-permute-start(bf16[8,1,32,384]{3,2,1,0:T(8,128)(2,1)S(1)} %bitcast.96), channel_id=1, source_target_pairs={{0,2},{2,0},{1,3},{3,1},{4,6},{6,4},{5,7},{7,5},{8,10},{10,8},{9,1... | collective-permute-start | bytes 589832 | tf_op jit(solution)/shard_map/ppermute | solution.py:22
  63.5 15.6 %collective-permute-start.17 = (bf16[2,2,2,32,1024]{4,3,2,0,1:T(8,128)(2,1)S(1)}, bf16[2,2,2,32,1024]{4,3,2,0,1:T(8,128)(2,1)S(1)}, u32[]{:S(2)}, u32[]{:S(2)}) collective-permute-start(bf16[2,2,2,32,1024]{4,3,2,0,1:T(8,128)(2,1)S(1)} %pad_maximum_fusion.3), channel_id=1, source_target_pairs={{0,4},{4,0},{1,5},{5,1},{2,6},{6,2},{3,7},{7,3},{8,12},{12,8},{9,1... | collective-permute-start | bytes 1572872 | tf_op jit(solution)/shard_map/ppermute | solution.py:22
  63.9 15.2 %collective-permute-start.16 = (bf16[128,1024]{1,0:T(8,128)(2,1)S(1)}, bf16[128,1024]{1,0:T(8,128)(2,1)S(1)}, u32[]{:S(2)}, u32[]{:S(2)}) collective-permute-start(bf16[128,1024]{1,0:T(8,128)(2,1)S(1)} %get-tuple-element.422.refs_8_.cot_ref), channel_id=1, source_target_pairs={{0,8},{8,0},{1,9},{9,1},{2,10},{10,2},{3,11},{11,3},{4,12},{12,4},... | collective-permute-start | bytes 786440 | tf_op jit(solution)/shard_map/ppermute | solution.py:22
  65.7 26.1 %collective-permute-start.19 = (bf16[1,8,32,1152]{3,2,1,0:T(8,128)(2,1)}, bf16[1,8,32,1152]{3,2,1,0:T(8,128)(2,1)}, u32[]{:S(2)}, u32[]{:S(2)}) collective-permute-start(bf16[1,8,32,1152]{3,2,1,0:T(8,128)(2,1)} %bitcast.18.a_ref), channel_id=1, source_target_pairs={{0,1},{1,0},{2,3},{3,2},{4,5},{5,4},{6,7},{7,6},{8,9},{9,8},{10,11... | collective-permute-start | bytes 1769480 | tf_op jit(solution)/shard_map/ppermute | solution.py:22
  66.0 31.4 %collective-permute-start.18 = (bf16[1,8,32,1152]{3,2,1,0:T(8,128)(2,1)}, bf16[1,8,32,1152]{3,2,1,0:T(8,128)(2,1)}, u32[]{:S(2)}, u32[]{:S(2)}) collective-permute-start(bf16[1,8,32,1152]{3,2,1,0:T(8,128)(2,1)} %bitcast.18.a_ref), channel_id=1, source_target_pairs={{0,16},{16,0},{1,17},{17,1},{2,18},{18,2},{3,19},{19,3},{4,20},{20... | collective-permute-start | bytes 1769480 | tf_op jit(solution)/shard_map/ppermute | solution.py:22
  80.0 6.2 %collective-permute-start.20 = (bf16[4,2,32,1024]{3,2,1,0:T(8,128)(2,1)S(1)}, bf16[4,2,32,1024]{3,2,1,0:T(8,128)(2,1)S(1)}, u32[]{:S(2)}, u32[]{:S(2)}) collective-permute-start(bf16[4,2,32,1024]{3,2,1,0:T(8,128)(2,1)S(1)} %bitcast.89), channel_id=1, source_target_pairs={{0,2},{2,0},{1,3},{3,1},{4,6},{6,4},{5,7},{7,5},{8,10},{10,8},{9,1... | collective-permute-start | bytes 1572872 | tf_op jit(solution)/shard_map/ppermute | solution.py:22
  80.0 18.8 %all-to-all-start.2 = ((bf16[8,128,128]{2,1,0:T(8,128)(2,1)}), bf16[8,128,128]{2,1,0:T(8,128)(2,1)S(1)}, u32[]{:S(2)}, u32[]{:S(2)}) async-start(bf16[8,128,128]{2,1,0:T(8,128)(2,1)} %copy-done.30), calls=%async_computation.2 | async-start | bytes 524288 | tf_op jit(solution)/shard_map/all_to_all | solution.py:930
  83.6 13.9 %collective-permute-start.22 = (bf16[128,1024]{1,0:T(8,128)(2,1)}, bf16[128,1024]{1,0:T(8,128)(2,1)}, u32[]{:S(2)}, u32[]{:S(2)}) collective-permute-start(bf16[128,1024]{1,0:T(8,128)(2,1)} %copy-done.38), channel_id=1, source_target_pairs={{0,4},{4,0},{1,5},{5,1},{2,6},{6,2},{3,7},{7,3},{8,12},{12,8},{9,1... | collective-permute-start | bytes 786440 | tf_op jit(solution)/shard_map/ppermute | solution.py:22
  98.8 13.7 %collective-permute-start.26 = (bf16[1,8,32,1152]{3,2,1,0:T(8,128)(2,1)}, bf16[1,8,32,1152]{3,2,1,0:T(8,128)(2,1)S(1)}, u32[]{:S(2)}, u32[]{:S(2)}) collective-permute-start(bf16[1,8,32,1152]{3,2,1,0:T(8,128)(2,1)} %collective-permute-done.18.c_ref), channel_id=1, source_target_pairs={{0,1},{1,0},{2,3},{3,2},{4,5},{5,4},{6,7},{7,6},{8,9},{9,8},{10,11... | collective-permute-start | bytes 1769480 | tf_op jit(solution)/shard_map/ppermute | solution.py:22
  102.1 11.9 %collective-permute-start.25 = (bf16[128,1024]{1,0:T(8,128)(2,1)S(1)}, bf16[128,1024]{1,0:T(8,128)(2,1)S(1)}, u32[]{:S(2)}, u32[]{:S(2)}) collective-permute-start(bf16[128,1024]{1,0:T(8,128)(2,1)S(1)} %get-tuple-element.380.refs_0_), channel_id=1, source_target_pairs={{0,12},{4,8},{8,4},{12,0},{1,13},{5,9},{9,5},{13,1},{2,14},{6,10},... | collective-permute-start | bytes 786440 | tf_op jit(solution)/shard_map/ppermute | solution.py:26
  103.1 11.6 %collective-permute-start.24 = (bf16[128,1024]{1,0:T(8,128)(2,1)S(1)}, bf16[128,1024]{1,0:T(8,128)(2,1)S(1)}, u32[]{:S(2)}, u32[]{:S(2)}) collective-permute-start(bf16[128,1024]{1,0:T(8,128)(2,1)S(1)} %get-tuple-element.380.refs_0_), channel_id=1, source_target_pairs={{0,8},{8,0},{1,9},{9,1},{2,10},{10,2},{3,11},{11,3},{4,12},{12,4},... | collective-permute-start | bytes 786440 | tf_op jit(solution)/shard_map/ppermute | solution.py:22
  105.3 9.5 %collective-permute-start.23 = (bf16[128,1024]{1,0:T(8,128)(2,1)S(1)}, bf16[128,1024]{1,0:T(8,128)(2,1)S(1)}, u32[]{:S(2)}, u32[]{:S(2)}) collective-permute-start(bf16[128,1024]{1,0:T(8,128)(2,1)S(1)} %get-tuple-element.380.refs_0_), channel_id=1, source_target_pairs={{0,4},{4,0},{1,5},{5,1},{2,6},{6,2},{3,7},{7,3},{8,12},{12,8},{9,1... | collective-permute-start | bytes 786440 | tf_op jit(solution)/shard_map/ppermute | solution.py:22
  128.8 10.6 %collective-permute-start.36 = (bf16[128,1024]{1,0:T(8,128)(2,1)S(1)}, bf16[128,1024]{1,0:T(8,128)(2,1)S(1)}, u32[]{:S(2)}, u32[]{:S(2)}) collective-permute-start(bf16[128,1024]{1,0:T(8,128)(2,1)S(1)} %get-tuple-element.412), channel_id=1, source_target_pairs={{0,4},{4,0},{1,5},{5,1},{2,6},{6,2},{3,7},{7,3},{8,12},{12,8},{9,1... | collective-permute-start | bytes 786440 | tf_op jit(solution)/shard_map/ppermute | solution.py:22
  130.2 9.2 %collective-permute-start.37 = (bf16[128,1024]{1,0:T(8,128)(2,1)S(1)}, bf16[128,1024]{1,0:T(8,128)(2,1)S(1)}, u32[]{:S(2)}, u32[]{:S(2)}) collective-permute-start(bf16[128,1024]{1,0:T(8,128)(2,1)S(1)} %get-tuple-element.413), channel_id=1, source_target_pairs={{0,8},{8,0},{1,9},{9,1},{2,10},{10,2},{3,11},{11,3},{4,12},{12,4},... | collective-permute-start | bytes 786440 | tf_op jit(solution)/shard_map/ppermute | solution.py:22
  130.2 13.7 %collective-permute-start.38 = (bf16[128,1024]{1,0:T(8,128)(2,1)S(1)}, bf16[128,1024]{1,0:T(8,128)(2,1)S(1)}, u32[]{:S(2)}, u32[]{:S(2)}) collective-permute-start(bf16[128,1024]{1,0:T(8,128)(2,1)S(1)} %get-tuple-element.414), channel_id=1, source_target_pairs={{0,12},{4,8},{8,4},{12,0},{1,13},{5,9},{9,5},{13,1},{2,14},{6,10},... | collective-permute-start | bytes 786440 | tf_op jit(solution)/shard_map/ppermute | solution.py:26
  138.4 27.5 %collective-permute-start.39 = (bf16[16,32,1152]{2,1,0:T(8,128)(2,1)}, bf16[16,32,1152]{2,1,0:T(8,128)(2,1)}, u32[]{:S(2)}, u32[]{:S(2)}) collective-permute-start(bf16[16,32,1152]{2,1,0:T(8,128)(2,1)} %get-tuple-element.443), channel_id=1, source_target_pairs={{0,1},{1,0},{2,3},{3,2},{4,5},{5,4},{6,7},{7,6},{8,9},{9,8},{10,11... | collective-permute-start | bytes 3538952 | tf_op jit(solution)/shard_map/ppermute | solution.py:22
  146.6 6.9 %collective-permute-start.41 = (bf16[512,1024]{1,0:T(8,128)(2,1)}, bf16[512,1024]{1,0:T(8,128)(2,1)}, u32[]{:S(2)}, u32[]{:S(2)}) collective-permute-start(bf16[512,1024]{1,0:T(8,128)(2,1)} %get-tuple-element.460), channel_id=1, source_target_pairs={{0,2},{2,0},{1,3},{3,1},{4,6},{6,4},{5,7},{7,5},{8,10},{10,8},{9,1... | collective-permute-start | bytes 3145736 | tf_op jit(solution)/shard_map/ppermute | solution.py:22
  149.1 10.8 %collective-permute-start.40 = (bf16[8,64,1024]{2,1,0:T(8,128)(2,1)}, bf16[8,64,1024]{2,1,0:T(8,128)(2,1)}, u32[]{:S(2)}, u32[]{:S(2)}) collective-permute-start(bf16[8,64,1024]{2,1,0:T(8,128)(2,1)} %get-tuple-element.449), channel_id=1, source_target_pairs={{0,2},{2,0},{1,3},{3,1},{4,6},{6,4},{5,7},{7,5},{8,10},{10,8},{9,1... | collective-permute-start | bytes 3145736 | tf_op jit(solution)/shard_map/ppermute | solution.py:22
  149.6 13.4 %all-to-all-start.3 = ((bf16[8,128,128]{2,1,0:T(8,128)(2,1)}), bf16[8,128,128]{2,1,0:T(8,128)(2,1)S(1)}, u32[]{:S(2)}, u32[]{:S(2)}) async-start(bf16[8,128,128]{2,1,0:T(8,128)(2,1)} %copy-done.29), calls=%async_computation.3 | async-start | bytes 524288 | tf_op jit(solution)/shard_map/all_to_all | solution.py:984
  156.4 21.6 %collective-permute-start.42 = (bf16[128,1024]{1,0:T(8,128)(2,1)}, bf16[128,1024]{1,0:T(8,128)(2,1)S(1)}, u32[]{:S(2)}, u32[]{:S(2)}) collective-permute-start(bf16[128,1024]{1,0:T(8,128)(2,1)} %get-tuple-element.462), channel_id=1, source_target_pairs={{0,4},{4,0},{1,5},{5,1},{2,6},{6,2},{3,7},{7,3},{8,12},{12,8},{9,1... | collective-permute-start | bytes 786440 | tf_op jit(solution)/shard_map/ppermute | solution.py:22
  158.4 19.6 %collective-permute-start.43 = (bf16[128,1024]{1,0:T(8,128)(2,1)}, bf16[128,1024]{1,0:T(8,128)(2,1)}, u32[]{:S(2)}, u32[]{:S(2)}) collective-permute-start(bf16[128,1024]{1,0:T(8,128)(2,1)} %get-tuple-element.463), channel_id=1, source_target_pairs={{0,8},{8,0},{1,9},{9,1},{2,10},{10,2},{3,11},{11,3},{4,12},{12,4},... | collective-permute-start | bytes 786440 | tf_op jit(solution)/shard_map/ppermute | solution.py:22
  159.9 18.2 %collective-permute-start.44 = (bf16[128,1024]{1,0:T(8,128)(2,1)}, bf16[128,1024]{1,0:T(8,128)(2,1)}, u32[]{:S(2)}, u32[]{:S(2)}) collective-permute-start(bf16[128,1024]{1,0:T(8,128)(2,1)} %get-tuple-element.464), channel_id=1, source_target_pairs={{0,12},{4,8},{8,4},{12,0},{1,13},{5,9},{9,5},{13,1},{2,14},{6,10},... | collective-permute-start | bytes 786440 | tf_op jit(solution)/shard_map/ppermute | solution.py:26
  165.8 15.6 %collective-permute-start.46 = (bf16[8,32,1024]{2,1,0:T(8,128)(2,1)}, bf16[8,32,1024]{2,1,0:T(8,128)(2,1)S(1)}, u32[]{:S(2)}, u32[]{:S(2)}) collective-permute-start(bf16[8,32,1024]{2,1,0:T(8,128)(2,1)} %copy-done.35), channel_id=1, source_target_pairs={{0,1},{1,0},{2,3},{3,2},{4,5},{5,4},{6,7},{7,6},{8,9},{9,8},{10,11... | collective-permute-start | bytes 1572872 | tf_op jit(solution)/shard_map/ppermute | solution.py:22
  178.1 12.0 %collective-permute-start.45 = (bf16[256,1024]{1,0:T(8,128)(2,1)S(1)}, bf16[256,1024]{1,0:T(8,128)(2,1)S(1)}, u32[]{:S(2)}, u32[]{:S(2)}) collective-permute-start(bf16[256,1024]{1,0:T(8,128)(2,1)S(1)} %get-tuple-element.482), channel_id=1, source_target_pairs={{0,4},{4,0},{1,5},{5,1},{2,6},{6,2},{3,7},{7,3},{8,12},{12,8},{9,1... | collective-permute-start | bytes 1572872 | tf_op jit(solution)/shard_map/ppermute | solution.py:22
  182.2 12.0 %collective-permute-start.47 = (bf16[2,64,1024]{2,1,0:T(8,128)(2,1)S(1)}, bf16[2,64,1024]{2,1,0:T(8,128)(2,1)S(1)}, u32[]{:S(2)}, u32[]{:S(2)}) collective-permute-start(bf16[2,64,1024]{2,1,0:T(8,128)(2,1)S(1)} %get-tuple-element.488), channel_id=1, source_target_pairs={{0,8},{8,0},{1,9},{9,1},{2,10},{10,2},{3,11},{11,3},{4,12},{12,4},... | collective-permute-start | bytes 786440 | tf_op jit(solution)/shard_map/ppermute | solution.py:22
  184.1 29.1 %collective-permute-start.49 = (bf16[1,256,1152]{2,1,0:T(8,128)(2,1)S(1)}, bf16[1,256,1152]{2,1,0:T(8,128)(2,1)S(1)}, u32[]{:S(2)}, u32[]{:S(2)}) collective-permute-start(bf16[1,256,1152]{2,1,0:T(8,128)(2,1)S(1)} %get-tuple-element.505), channel_id=1, source_target_pairs={{0,16},{16,0},{1,17},{17,1},{2,18},{18,2},{3,19},{19,3},{4,20},{20... | collective-permute-start | bytes 1769480 | tf_op jit(solution)/shard_map/ppermute | solution.py:22
  194.1 14.8 %collective-permute-start.50 = (bf16[256,1024]{1,0:T(8,128)(2,1)S(1)}, bf16[256,1024]{1,0:T(8,128)(2,1)S(1)}, u32[]{:S(2)}, u32[]{:S(2)}) collective-permute-start(bf16[256,1024]{1,0:T(8,128)(2,1)S(1)} %get-tuple-element.507), channel_id=1, source_target_pairs={{0,4},{4,0},{1,5},{5,1},{2,6},{6,2},{3,7},{7,3},{8,12},{12,8},{9,1... | collective-permute-start | bytes 1572872 | tf_op jit(solution)/shard_map/ppermute | solution.py:22
  194.8 12.3 %collective-permute-start.51 = (bf16[128,1024]{1,0:T(8,128)(2,1)S(1)}, bf16[128,1024]{1,0:T(8,128)(2,1)S(1)}, u32[]{:S(2)}, u32[]{:S(2)}) collective-permute-start(bf16[128,1024]{1,0:T(8,128)(2,1)S(1)} %get-tuple-element.509), channel_id=1, source_target_pairs={{0,8},{8,0},{1,9},{9,1},{2,10},{10,2},{3,11},{11,3},{4,12},{12,4},... | collective-permute-start | bytes 786440 | tf_op jit(solution)/shard_map/ppermute | solution.py:22
  194.8 6.2 %collective-permute-start.53 = (bf16[8,32,384]{2,1,0:T(8,128)(2,1)S(1)}, bf16[8,32,384]{2,1,0:T(8,128)(2,1)S(1)}, u32[]{:S(2)}, u32[]{:S(2)}) collective-permute-start(bf16[8,32,384]{2,1,0:T(8,128)(2,1)S(1)} %get-tuple-element.518), channel_id=1, source_target_pairs={{0,1},{1,0},{2,3},{3,2},{4,5},{5,4},{6,7},{7,6},{8,9},{9,8},{10,11... | collective-permute-start | bytes 589832 | tf_op jit(solution)/shard_map/ppermute | solution.py:22
  196.3 16.8 %collective-permute-start.52 = (bf16[2,32,1024]{2,1,0:T(8,128)(2,1)S(1)}, bf16[2,32,1024]{2,1,0:T(8,128)(2,1)S(1)}, u32[]{:S(2)}, u32[]{:S(2)}) collective-permute-start(bf16[2,32,1024]{2,1,0:T(8,128)(2,1)S(1)} %get-tuple-element.516), channel_id=1, source_target_pairs={{0,4},{4,0},{1,5},{5,1},{2,6},{6,2},{3,7},{7,3},{8,12},{12,8},{9,1... | collective-permute-start | bytes 393224 | tf_op jit(solution)/shard_map/ppermute | solution.py:22
  214.7 26.3 %all-to-all-start.4 = ((bf16[8,32,1152]{2,1,0:T(8,128)(2,1)}), bf16[8,32,1152]{2,1,0:T(8,128)(2,1)}, u32[]{:S(2)}, u32[]{:S(2)}) async-start(bf16[8,32,1152]{2,1,0:T(8,128)(2,1)} %total_kernel.3), calls=%async_computation.4 | async-start | bytes 1179648 | tf_op jit(solution)/shard_map/all_to_all | solution.py:807
  218.9 20.0 %collective-permute-start.54 = (bf16[128,1024]{1,0:T(8,128)(2,1)S(1)}, bf16[128,1024]{1,0:T(8,128)(2,1)S(1)}, u32[]{:S(2)}, u32[]{:S(2)}) collective-permute-start(bf16[128,1024]{1,0:T(8,128)(2,1)S(1)} %get-tuple-element.524), channel_id=1, source_target_pairs={{0,16},{16,0},{1,17},{17,1},{2,18},{18,2},{3,19},{19,3},{4,20},{20... | collective-permute-start | bytes 786440 | tf_op jit(solution)/shard_map/ppermute | solution.py:22
  219.0 22.0 %collective-permute-start.55 = (bf16[128,1024]{1,0:T(8,128)(2,1)S(1)}, bf16[128,1024]{1,0:T(8,128)(2,1)S(1)}, u32[]{:S(2)}, u32[]{:S(2)}) collective-permute-start(bf16[128,1024]{1,0:T(8,128)(2,1)S(1)} %get-tuple-element.525), channel_id=1, source_target_pairs={{0,8},{8,0},{1,9},{9,1},{2,10},{10,2},{3,11},{11,3},{4,12},{12,4},... | collective-permute-start | bytes 786440 | tf_op jit(solution)/shard_map/ppermute | solution.py:22
  223.2 15.7 %collective-permute-start.57 = (bf16[1,32,1024]{2,1,0:T(8,128)(2,1)S(1)}, bf16[1,32,1024]{2,1,0:T(8,128)(2,1)S(1)}, u32[]{:S(2)}, u32[]{:S(2)}) collective-permute-start(bf16[1,32,1024]{2,1,0:T(8,128)(2,1)S(1)} %get-tuple-element.537), channel_id=1, source_target_pairs={{0,16},{16,0},{1,17},{17,1},{2,18},{18,2},{3,19},{19,3},{4,20},{20... | collective-permute-start | bytes 196616 | tf_op jit(solution)/shard_map/ppermute | solution.py:22
  241.0 11.6 %all-to-all-start.5 = ((bf16[8,32,384]{2,1,0:T(8,128)(2,1)}), bf16[8,32,384]{2,1,0:T(8,128)(2,1)S(1)}, u32[]{:S(2)}, u32[]{:S(2)}) async-start(bf16[8,32,384]{2,1,0:T(8,128)(2,1)} %total_kernel.2), calls=%async_computation.5 | async-start | bytes 393216 | tf_op jit(solution)/shard_map/all_to_all | solution.py:879
  (63 other events, 430.5 us)

commit v5 on v4

--- a/solution.py
+++ b/solution.py
@@ -564,6 +564,23 @@
     sent_ref[...] = total[half:]
 
 
+def qkv_out_kernel(places, made_ref, weight_ref, gain_ref, out_ref, gain_grad_ref):
+    pairs, rows, wide = made_ref.shape
+    wide = wide // 3
+    row = lax.broadcasted_iota(jnp.int32, (rows, rows), 0)
+    lane = lax.broadcasted_iota(jnp.int32, (rows, rows), 1)
+    gain = jnp.sum(jnp.where(row == lane, gain_ref[...].astype(f32), 0.0), axis=1, keepdims=True)
+    total = jnp.zeros((rows, wide), f32)
+    for at in range(pairs):
+        for part in range(3):
+            first = (part * pairs + at) * wide
+            made = made_ref[at, :, part * wide : (part + 1) * wide].astype(f32)
+            total = total + made * weight_ref[:, first : first + wide].astype(f32)
+            out_ref[:, first : first + wide] = made * gain
+    total = jnp.sum(total, axis=1, keepdims=True)
+    gain_grad_ref[...] = jnp.sum(jnp.where(row == lane, total, 0.0), axis=0, keepdims=True)
+
+
 def columns_by(array, pieces, piece):
     rows, count = array.shape
     padded = jnp.pad(array, ((0, 0), (0, pieces * piece - count)))
@@ -1050,10 +1067,21 @@
     reach(LAST)
 
     grad_attn = (live.attn_kept.astype(f32) + live.attn_other.astype(f32))[0]
-    grad_qkv = live.grad_qkv.astype(f32).reshape(pairs, owned, 3, wide)
-    grad_qkv = grad_qkv.transpose(1, 2, 0, 3).reshape(owned, 3 * width)
-    grad_gain_attn = jnp.sum(grad_qkv * w_qkv.astype(f32), axis=1)
-    grad_qkv = grad_qkv * gain_one
+    if owned % 16 == 0:
+        grad_qkv, grad_gain_attn = call(
+            qkv_out_kernel,
+            [((owned, 3 * width), f32), ((1, owned), f32)],
+            places,
+            live.grad_qkv,
+            w_qkv,
+            gain_attn[None, :],
+        )
+        grad_gain_attn = grad_gain_attn[0]
+    else:
+        grad_qkv = live.grad_qkv.astype(f32).reshape(pairs, owned, 3, wide)
+        grad_qkv = grad_qkv.transpose(1, 2, 0, 3).reshape(owned, 3 * width)
+        grad_gain_attn = jnp.sum(grad_qkv * w_qkv.astype(f32), axis=1)
+        grad_qkv = grad_qkv * gain_one
 
     grad_packed = live.grad_packed.astype(f32)
     grad_in = jnp.concatenate(

time: 256 us -> 255 us (level)
    pallas_call x30 -> x31, Pallas kernels: 61.7 us -> 63.7 us  [call(): pl.pallas_call(kernel, in_specs=[pl.BlockSpec(memory_space=pltpu.SMEM)] +...]
    unnamed x94 -> x96, local copies, waits for them, and re-layouts: 14.3 us -> 14.3 us
where the time goes in v5:
time: 255 us; the launch traced here: 254 us
  waiting for transfers between devices  81.5 us (32%)
  starting transfers between devices  78.3 us (31%)
  Pallas kernels  63.7 us (25%)
  local copies, waits for them, and re-layouts  17.1 us (7%)
  other arithmetic  11.8 us (5%)
    ppermute x56, waiting for transfers between devices, partner(): return lax.ppermute(array, axis, [(0, 1), (1, 0)])  75.7 us
    pallas_call x31, Pallas kernels, call(): pl.pallas_call(kernel, in_specs=[pl.BlockSpec(memory_space=pltpu.SMEM)] +...  63.7 us
    ppermute x56, starting transfers between devices, partner(): return lax.ppermute(array, axis, [(0, 1), (1, 0)])  52.3 us
    unnamed x96, local copies, waits for them, and re-layouts  14.3 us
  transfers between devices with their start and end apart: 65, of which 28 were waited for; matrix products, arithmetic and copies ran while one was open for 6% of the time, Pallas kernels for 21%

profile of v5, /device:TPU:0, one launch (start us, length us, event | category | flops | bytes accessed | tf_op | source)
XLA Modules:
  0.0 254.0 jit_solution(2240556943912465103)
XLA Ops:
  6.2 4.0 %collective-permute-start.4 = (bf16[128,1024]{1,0:T(8,128)(2,1)S(1)}, bf16[128,1024]{1,0:T(8,128)(2,1)S(1)}, u32[]{:S(2)}, u32[]{:S(2)}) collective-permute-start(bf16[128,1024]{1,0:T(8,128)(2,1)S(1)} %get-tuple-element.322.refs_0_), channel_id=1, source_target_pairs={{0,16},{16,0},{1,17},{17,1},{2,18},{18,2},{3,19},{19,3},{4,20},{20... | collective-permute-start | bytes 786440 | tf_op jit(solution)/shard_map/ppermute | solution.py:22
  13.3 3.4 %all-to-all-start = ((bf16[8,32,384]{2,1,0:T(8,128)(2,1)}), bf16[8,32,384]{2,1,0:T(8,128)(2,1)S(1)}, u32[]{:S(2)}, u32[]{:S(2)}) async-start(bf16[8,32,384]{2,1,0:T(8,128)(2,1)} %reshape.172), calls=%async_computation | async-start | bytes 393216 | tf_op jit(solution)/shard_map/all_to_all | solution.py:653
  16.7 1.9 collective-permute-start.5
  20.0 7.1 %collective-permute-done.5.refs_9_ = bf16[128,1024]{1,0:T(8,128)(2,1)S(1)} collective-permute-done((bf16[128,1024]{1,0:T(8,128)(2,1)S(1)}, bf16[128,1024]{1,0:T(8,128)(2,1)S(1)}, u32[]{:S(2)}, u32[]{:S(2)}) %collective-permute-start.5) | collective-permute-done | bytes 262176 | tf_op jit(solution)/shard_map/ppermute | solution.py:22
  27.7 4.2 %all-to-all-start.1 = ((bf16[8,32,1152]{2,1,0:T(8,128)(2,1)}), bf16[8,32,1152]{2,1,0:T(8,128)(2,1)}, u32[]{:S(2)}, u32[]{:S(2)}) async-start(bf16[8,32,1152]{2,1,0:T(8,128)(2,1)} %pad_maximum_fusion.2), calls=%async_computation.1 | async-start | bytes 1179648 | tf_op jit(solution)/shard_map/all_to_all | solution.py:678
  35.5 1.9 multiply_cosine_fusion
  37.4 2.0 collective-permute-start.10
  41.4 2.1 collective-permute-start.7
  43.6 4.2 %collective-permute-done.7 = bf16[2,32,1024]{2,1,0:T(8,128)(2,1)S(1)} collective-permute-done((bf16[2,32,1024]{2,1,0:T(8,128)(2,1)S(1)}, bf16[2,32,1024]{2,1,0:T(8,128)(2,1)S(1)}, u32[]{:S(2)}, u32[]{:S(2)}) %collective-permute-start.7) | collective-permute-done | bytes 131104 | tf_op jit(solution)/shard_map/ppermute | solution.py:22
  48.5 4.3 %collective-permute-done.8.refs_3_ = bf16[128,1024]{1,0:T(8,128)(2,1)S(1)} collective-permute-done((bf16[128,1024]{1,0:T(8,128)(2,1)S(1)}, bf16[128,1024]{1,0:T(8,128)(2,1)S(1)}, u32[]{:S(2)}, u32[]{:S(2)}) %collective-permute-start.8) | collective-permute-done | bytes 262176 | tf_op jit(solution)/shard_map/ppermute | solution.py:22
  56.3 2.6 %collective-permute-done.13.b_ref = bf16[8,1,32,384]{3,2,1,0:T(8,128)(2,1)S(1)} collective-permute-done((bf16[8,1,32,384]{3,2,1,0:T(8,128)(2,1)S(1)}, bf16[8,1,32,384]{3,2,1,0:T(8,128)(2,1)S(1)}, u32[]{:S(2)}, u32[]{:S(2)}) %collective-permute-start.13) | collective-permute-done | bytes 196640 | tf_op jit(solution)/shard_map/ppermute | solution.py:22
  58.8 3.1 %collective-permute-done.11 = bf16[2,2,32,1024]{3,2,1,0:T(8,128)(2,1)S(1)} collective-permute-done((bf16[2,2,32,1024]{3,2,1,0:T(8,128)(2,1)}, bf16[2,2,32,1024]{3,2,1,0:T(8,128)(2,1)S(1)}, u32[]{:S(2)}, u32[]{:S(2)}) %collective-permute-start.11) | collective-permute-done | bytes 262176 | tf_op jit(solution)/shard_map/ppermute | solution.py:22
  64.0 1.7 collective-permute-start.16
  66.1 2.1 collective-permute-start.18
  68.1 2.0 project_kernel.1
  71.4 7.8 %attend_kernel.1 = (bf16[8,128,128]{2,1,0:T(8,128)(2,1)S(1)}, f32[4,8,256]{2,1,0:T(8,128)S(1)}) custom-call(s32[6]{0:T(128)S(1)} %stack.54.places, bf16[1024,384]{1,0:T(8,128)(2,1)S(1)} %get-tuple-element.330.refs_0_), custom_call_target="tpu_custom_call" | custom-call | bytes 1081344 | tf_op jit(solution)/shard_map/attend_kernel/pallas_call | solution.py:122
  80.0 3.6 %all-to-all-start.2 = ((bf16[8,128,128]{2,1,0:T(8,128)(2,1)}), bf16[8,128,128]{2,1,0:T(8,128)(2,1)S(1)}, u32[]{:S(2)}, u32[]{:S(2)}) async-start(bf16[8,128,128]{2,1,0:T(8,128)(2,1)} %copy-done.31), calls=%async_computation.2 | async-start | bytes 524288 | tf_op jit(solution)/shard_map/all_to_all | solution.py:947
  83.6 1.7 collective-permute-start.22
  91.8 5.6 %collective-permute-done.18.c_ref = bf16[1,8,32,1152]{3,2,1,0:T(8,128)(2,1)} collective-permute-done((bf16[1,8,32,1152]{3,2,1,0:T(8,128)(2,1)}, bf16[1,8,32,1152]{3,2,1,0:T(8,128)(2,1)}, u32[]{:S(2)}, u32[]{:S(2)}) %collective-permute-start.18) | collective-permute-done | bytes 589856 | tf_op jit(solution)/shard_map/ppermute | solution.py:22
  103.1 2.2 collective-permute-start.24
  105.7 6.7 %collective-permute-done.26.d_ref = bf16[1,8,32,1152]{3,2,1,0:T(8,128)(2,1)S(1)} collective-permute-done((bf16[1,8,32,1152]{3,2,1,0:T(8,128)(2,1)}, bf16[1,8,32,1152]{3,2,1,0:T(8,128)(2,1)S(1)}, u32[]{:S(2)}, u32[]{:S(2)}) %collective-permute-start.26) | collective-permute-done | bytes 589856 | tf_op jit(solution)/shard_map/ppermute | solution.py:22
  119.0 6.3 %feed_kernel.1 = (bf16[1024,384]{1,0:T(8,128)(2,1)S(1)}, bf16[1024,768]{1,0:T(8,128)(2,1)S(1)}, bf16[512,1024]{1,0:T(8,128)(2,1)S(1)}, bf16[512,1024]{1,0:T(8,128)(2,1)S(1)}) custom-call(s32[6]{0:T(128)S(1)} %stack.54.places, bf16[128,1024]{1,0:T(8,128)(2,1)S(1)} %get-tuple-element.382.refs_0_, bf16[128,1024]{1,0:T(8,128)(2,1)S(1)} %collective-permute-done.23.refs_1_, ...), custom_call_target="tpu_custom_call" | custom-call | flops 4026531840 | bytes 11010048 | tf_op jit(solution)/shard_map/feed_kernel/pallas_call | solution.py:122
  125.5 2.5 collective-permute-done.35.b_ref
  130.2 2.1 collective-permute-start.38
  132.3 6.1 %feed_rest_kernel.1 = (bf16[512,1024]{1,0:T(8,128)(2,1)S(1)}, bf16[512,1024]{1,0:T(8,128)(2,1)}, bf16[16,32,1152]{2,1,0:T(8,128)(2,1)S(1)}, bf16[16,32,1152]{2,1,0:T(8,128)(2,1)}) custom-call(s32[6]{0:T(128)S(1)} %stack.54.places, bf16[128,1024]{1,0:T(8,128)(2,1)S(1)} %get-tuple-element.382.refs_0_, bf16[128,1024]{1,0:T(8,128)(2,1)S(1)} %collective-permute-done.23.refs_1_, ...), custom_call_target="tpu_custom_call" | custom-call | flops 3221225472 | bytes 13369344 | tf_op jit(solution)/shard_map/feed_rest_kernel/pallas_call | solution.py:122
  139.4 4.5 %collective-permute-done.38.d_ref = bf16[128,1024]{1,0:T(8,128)(2,1)S(1)} collective-permute-done((bf16[128,1024]{1,0:T(8,128)(2,1)S(1)}, bf16[128,1024]{1,0:T(8,128)(2,1)S(1)}, u32[]{:S(2)}, u32[]{:S(2)}) %collective-permute-start.38) | collective-permute-done | bytes 262176 | tf_op jit(solution)/shard_map/ppermute | solution.py:26
  144.0 1.7 middle_back_kernel.1
  146.6 2.5 outer_kernel.1
  149.5 3.9 %all-to-all-start.3 = ((bf16[8,128,128]{2,1,0:T(8,128)(2,1)}), bf16[8,128,128]{2,1,0:T(8,128)(2,1)S(1)}, u32[]{:S(2)}, u32[]{:S(2)}) async-start(bf16[8,128,128]{2,1,0:T(8,128)(2,1)} %copy-done.30), calls=%async_computation.3 | async-start | bytes 524288 | tf_op jit(solution)/shard_map/all_to_all | solution.py:1001
  153.4 2.2 chip_sums_kernel.3
  156.4 2.0 collective-permute-start.42
  163.0 2.9 %collective-permute-done.39 = bf16[16,32,1152]{2,1,0:T(8,128)(2,1)} collective-permute-done((bf16[16,32,1152]{2,1,0:T(8,128)(2,1)}, bf16[16,32,1152]{2,1,0:T(8,128)(2,1)}, u32[]{:S(2)}, u32[]{:S(2)}) %collective-permute-start.39) | collective-permute-done | bytes 1179680 | tf_op jit(solution)/shard_map/ppermute | solution.py:22
  166.9 9.3 %attend_back_kernel.1.grad_ref = bf16[1024,384]{1,0:T(8,128)(2,1)S(1)} custom-call(s32[6]{0:T(128)S(1)} %stack.54.places, bf16[1024,384]{1,0:T(8,128)(2,1)S(1)} %copy-done.3, bf16[8,128,128]{2,1,0:T(8,128)(2,1)S(1)} %all-to-all-done.3.refs_1_, f32[4,8,256]{2,1,0:T(8,128)S(1)} %get-tuple-element.469.refs_2_, f32[1024,256]{1,0:T(8,128)S(1)} %pad_maximum_fusion.refs_9_.refs_3_), custom_call_target="tpu_custom_call" | custom-call | bytes 2916352 | tf_op jit(solution)/shard_map/attend_back_kernel/pallas_call | solution.py:122
  176.2 1.8 project_back_kernel.1
  179.6 1.9 project_outer_kernel.1
  184.1 2.2 collective-permute-start.49
  187.0 3.1 %collective-permute-done.45.across_ref = bf16[256,1024]{1,0:T(8,128)(2,1)S(1)} collective-permute-done((bf16[256,1024]{1,0:T(8,128)(2,1)S(1)}, bf16[256,1024]{1,0:T(8,128)(2,1)S(1)}, u32[]{:S(2)}, u32[]{:S(2)}) %collective-permute-start.45) | collective-permute-done | bytes 524320 | tf_op jit(solution)/shard_map/ppermute | solution.py:22
  190.7 3.5 %collective-permute-done.47 = bf16[2,64,1024]{2,1,0:T(8,128)(2,1)S(1)} collective-permute-done((bf16[2,64,1024]{2,1,0:T(8,128)(2,1)S(1)}, bf16[2,64,1024]{2,1,0:T(8,128)(2,1)S(1)}, u32[]{:S(2)}, u32[]{:S(2)}) %collective-permute-start.47) | collective-permute-done | bytes 262176 | tf_op jit(solution)/shard_map/ppermute | solution.py:22
  197.9 3.2 %collective-permute-done.53.b_ref = bf16[8,32,384]{2,1,0:T(8,128)(2,1)S(1)} collective-permute-done((bf16[8,32,384]{2,1,0:T(8,128)(2,1)S(1)}, bf16[8,32,384]{2,1,0:T(8,128)(2,1)S(1)}, u32[]{:S(2)}, u32[]{:S(2)}) %collective-permute-start.53) | collective-permute-done | bytes 196640 | tf_op jit(solution)/shard_map/ppermute | solution.py:22
  202.3 4.7 %collective-permute-done.51.both_ref = bf16[128,1024]{1,0:T(8,128)(2,1)S(1)} collective-permute-done((bf16[128,1024]{1,0:T(8,128)(2,1)S(1)}, bf16[128,1024]{1,0:T(8,128)(2,1)S(1)}, u32[]{:S(2)}, u32[]{:S(2)}) %collective-permute-start.51) | collective-permute-done | bytes 262176 | tf_op jit(solution)/shard_map/ppermute | solution.py:22
  207.1 2.0 collective-permute-done.50.across_ref
  210.4 2.8 %collective-permute-done.49 = bf16[1,256,1152]{2,1,0:T(8,128)(2,1)S(1)} collective-permute-done((bf16[1,256,1152]{2,1,0:T(8,128)(2,1)S(1)}, bf16[1,256,1152]{2,1,0:T(8,128)(2,1)S(1)}, u32[]{:S(2)}, u32[]{:S(2)}) %collective-permute-start.49) | collective-permute-done | bytes 589856 | tf_op jit(solution)/shard_map/ppermute | solution.py:22
  214.7 4.2 %all-to-all-start.4 = ((bf16[8,32,1152]{2,1,0:T(8,128)(2,1)}), bf16[8,32,1152]{2,1,0:T(8,128)(2,1)}, u32[]{:S(2)}, u32[]{:S(2)}) async-start(bf16[8,32,1152]{2,1,0:T(8,128)(2,1)} %total_kernel.3), calls=%async_computation.4 | async-start | bytes 1179648 | tf_op jit(solution)/shard_map/all_to_all | solution.py:824
  219.0 2.4 collective-permute-start.55
  223.3 2.4 collective-permute-start.57
  227.0 12.0 %collective-permute-done.57 = bf16[1,32,1024]{2,1,0:T(8,128)(2,1)S(1)} collective-permute-done((bf16[1,32,1024]{2,1,0:T(8,128)(2,1)S(1)}, bf16[1,32,1024]{2,1,0:T(8,128)(2,1)S(1)}, u32[]{:S(2)}, u32[]{:S(2)}) %collective-permute-start.57) | collective-permute-done | bytes 65568 | tf_op jit(solution)/shard_map/ppermute | solution.py:22
  238.9 2.0 collective-permute-done.55.b_ref
  241.0 3.7 %all-to-all-start.5 = ((bf16[8,32,384]{2,1,0:T(8,128)(2,1)}), bf16[8,32,384]{2,1,0:T(8,128)(2,1)S(1)}, u32[]{:S(2)}, u32[]{:S(2)}) async-start(bf16[8,32,384]{2,1,0:T(8,128)(2,1)} %total_kernel.2), calls=%async_computation.5 | async-start | bytes 393216 | tf_op jit(solution)/shard_map/all_to_all | solution.py:896
  (242 shorter events, 80.6 us)
Async XLA Ops:
  6.2 20.8 %collective-permute-start.4 = (bf16[128,1024]{1,0:T(8,128)(2,1)S(1)}, bf16[128,1024]{1,0:T(8,128)(2,1)S(1)}, u32[]{:S(2)}, u32[]{:S(2)}) collective-permute-start(bf16[128,1024]{1,0:T(8,128)(2,1)S(1)} %get-tuple-element.322.refs_0_), channel_id=1, source_target_pairs={{0,16},{16,0},{1,17},{17,1},{2,18},{18,2},{3,19},{19,3},{4,20},{20... | collective-permute-start | bytes 786440 | tf_op jit(solution)/shard_map/ppermute | solution.py:22
  10.3 16.8 %collective-permute-start.3 = (bf16[128,1024]{1,0:T(8,128)(2,1)S(1)}, bf16[128,1024]{1,0:T(8,128)(2,1)S(1)}, u32[]{:S(2)}, u32[]{:S(2)}) collective-permute-start(bf16[128,1024]{1,0:T(8,128)(2,1)S(1)} %get-tuple-element.322.refs_0_), channel_id=1, source_target_pairs={{0,8},{8,0},{1,9},{9,1},{2,10},{10,2},{3,11},{11,3},{4,12},{12,4},... | collective-permute-start | bytes 786440 | tf_op jit(solution)/shard_map/ppermute | solution.py:22
  11.8 15.9 %collective-permute-start.2 = (bf16[128,1024]{1,0:T(8,128)(2,1)S(1)}, bf16[128,1024]{1,0:T(8,128)(2,1)S(1)}, u32[]{:S(2)}, u32[]{:S(2)}) collective-permute-start(bf16[128,1024]{1,0:T(8,128)(2,1)S(1)} %get-tuple-element.322.refs_0_), channel_id=1, source_target_pairs={{0,4},{4,0},{1,5},{5,1},{2,6},{6,2},{3,7},{7,3},{8,12},{12,8},{9,1... | collective-permute-start | bytes 786440 | tf_op jit(solution)/shard_map/ppermute | solution.py:22
  13.3 14.4 %all-to-all-start = ((bf16[8,32,384]{2,1,0:T(8,128)(2,1)}), bf16[8,32,384]{2,1,0:T(8,128)(2,1)S(1)}, u32[]{:S(2)}, u32[]{:S(2)}) async-start(bf16[8,32,384]{2,1,0:T(8,128)(2,1)} %reshape.172), calls=%async_computation | async-start | bytes 393216 | tf_op jit(solution)/shard_map/all_to_all | solution.py:653
  16.7 10.3 %collective-permute-start.5 = (bf16[128,1024]{1,0:T(8,128)(2,1)S(1)}, bf16[128,1024]{1,0:T(8,128)(2,1)S(1)}, u32[]{:S(2)}, u32[]{:S(2)}) collective-permute-start(bf16[128,1024]{1,0:T(8,128)(2,1)S(1)} %get-tuple-element.424.refs_8_.cot_ref), channel_id=1, source_target_pairs={{0,4},{4,0},{1,5},{5,1},{2,6},{6,2},{3,7},{7,3},{8,12},{12,8},{9,1... | collective-permute-start | bytes 786440 | tf_op jit(solution)/shard_map/ppermute | solution.py:22
  27.7 25.0 %all-to-all-start.1 = ((bf16[8,32,1152]{2,1,0:T(8,128)(2,1)}), bf16[8,32,1152]{2,1,0:T(8,128)(2,1)}, u32[]{:S(2)}, u32[]{:S(2)}) async-start(bf16[8,32,1152]{2,1,0:T(8,128)(2,1)} %pad_maximum_fusion.2), calls=%async_computation.1 | async-start | bytes 1179648 | tf_op jit(solution)/shard_map/all_to_all | solution.py:678
  32.0 9.4 %collective-permute-start.6 = (bf16[32,1024]{1,0:T(8,128)(2,1)S(1)}, bf16[32,1024]{1,0:T(8,128)(2,1)S(1)}, u32[]{:S(2)}, u32[]{:S(2)}) collective-permute-start(bf16[32,1024]{1,0:T(8,128)(2,1)S(1)} %copy-done.45), channel_id=1, source_target_pairs={{0,1},{1,0},{2,3},{3,2},{4,5},{5,4},{6,7},{7,6},{8,9},{9,8},{10,11... | collective-permute-start | bytes 196616 | tf_op jit(solution)/shard_map/ppermute | solution.py:22
  37.4 15.4 %collective-permute-start.10 = (bf16[128,1024]{1,0:T(8,128)(2,1)S(1)}, bf16[128,1024]{1,0:T(8,128)(2,1)S(1)}, u32[]{:S(2)}, u32[]{:S(2)}) collective-permute-start(bf16[128,1024]{1,0:T(8,128)(2,1)S(1)} %collective-permute-done.4.refs_4_), channel_id=1, source_target_pairs={{0,8},{8,0},{1,9},{9,1},{2,10},{10,2},{3,11},{11,3},{4,12},{12,4},... | collective-permute-start | bytes 786440 | tf_op jit(solution)/shard_map/ppermute | solution.py:22
  39.3 13.4 %collective-permute-start.9 = (bf16[128,1024]{1,0:T(8,128)(2,1)S(1)}, bf16[128,1024]{1,0:T(8,128)(2,1)S(1)}, u32[]{:S(2)}, u32[]{:S(2)}) collective-permute-start(bf16[128,1024]{1,0:T(8,128)(2,1)S(1)} %collective-permute-done.4.refs_4_), channel_id=1, source_target_pairs={{0,4},{4,0},{1,5},{5,1},{2,6},{6,2},{3,7},{7,3},{8,12},{12,8},{9,1... | collective-permute-start | bytes 786440 | tf_op jit(solution)/shard_map/ppermute | solution.py:22
  40.8 11.9 %collective-permute-start.8 = (bf16[128,1024]{1,0:T(8,128)(2,1)S(1)}, bf16[128,1024]{1,0:T(8,128)(2,1)S(1)}, u32[]{:S(2)}, u32[]{:S(2)}) collective-permute-start(bf16[128,1024]{1,0:T(8,128)(2,1)S(1)} %collective-permute-done.3.refs_2_), channel_id=1, source_target_pairs={{0,4},{4,0},{1,5},{5,1},{2,6},{6,2},{3,7},{7,3},{8,12},{12,8},{9,1... | collective-permute-start | bytes 786440 | tf_op jit(solution)/shard_map/ppermute | solution.py:22
  41.4 6.4 %collective-permute-start.7 = (bf16[2,32,1024]{2,1,0:T(8,128)(2,1)S(1)}, bf16[2,32,1024]{2,1,0:T(8,128)(2,1)S(1)}, u32[]{:S(2)}, u32[]{:S(2)}) collective-permute-start(bf16[2,32,1024]{2,1,0:T(8,128)(2,1)S(1)} %get-tuple-element.560), channel_id=1, source_target_pairs={{0,16},{16,0},{1,17},{17,1},{2,18},{18,2},{3,19},{19,3},{4,20},{20... | collective-permute-start | bytes 393224 | tf_op jit(solution)/shard_map/ppermute | solution.py:22
  54.2 7.7 %collective-permute-start.11 = (bf16[2,2,32,1024]{3,2,1,0:T(8,128)(2,1)}, bf16[2,2,32,1024]{3,2,1,0:T(8,128)(2,1)S(1)}, u32[]{:S(2)}, u32[]{:S(2)}) collective-permute-start(bf16[2,2,32,1024]{3,2,1,0:T(8,128)(2,1)} %pad_maximum_fusion.4), channel_id=1, source_target_pairs={{0,8},{8,0},{1,9},{9,1},{2,10},{10,2},{3,11},{11,3},{4,12},{12,4},... | collective-permute-start | bytes 786440 | tf_op jit(solution)/shard_map/ppermute | solution.py:22
  55.7 7.8 %collective-permute-start.12 = (bf16[128,1024]{1,0:T(8,128)(2,1)S(1)}, bf16[128,1024]{1,0:T(8,128)(2,1)S(1)}, u32[]{:S(2)}, u32[]{:S(2)}) collective-permute-start(bf16[128,1024]{1,0:T(8,128)(2,1)S(1)} %collective-permute-done.10.refs_6_), channel_id=1, source_target_pairs={{0,4},{4,0},{1,5},{5,1},{2,6},{6,2},{3,7},{7,3},{8,12},{12,8},{9,1... | collective-permute-start | bytes 786440 | tf_op jit(solution)/shard_map/ppermute | solution.py:22
  56.3 6.6 %collective-permute-start.14 = (bf16[8,1,32,384]{3,2,1,0:T(8,128)(2,1)S(1)}, bf16[8,1,32,384]{3,2,1,0:T(8,128)(2,1)S(1)}, u32[]{:S(2)}, u32[]{:S(2)}) collective-permute-start(bf16[8,1,32,384]{3,2,1,0:T(8,128)(2,1)S(1)} %bitcast.92), channel_id=1, source_target_pairs={{0,2},{2,0},{1,3},{3,1},{4,6},{6,4},{5,7},{7,5},{8,10},{10,8},{9,1... | collective-permute-start | bytes 589832 | tf_op jit(solution)/shard_map/ppermute | solution.py:22
  63.6 15.7 %collective-permute-start.17 = (bf16[2,2,2,32,1024]{4,3,2,0,1:T(8,128)(2,1)S(1)}, bf16[2,2,2,32,1024]{4,3,2,0,1:T(8,128)(2,1)S(1)}, u32[]{:S(2)}, u32[]{:S(2)}) collective-permute-start(bf16[2,2,2,32,1024]{4,3,2,0,1:T(8,128)(2,1)S(1)} %pad_maximum_fusion.3), channel_id=1, source_target_pairs={{0,4},{4,0},{1,5},{5,1},{2,6},{6,2},{3,7},{7,3},{8,12},{12,8},{9,1... | collective-permute-start | bytes 1572872 | tf_op jit(solution)/shard_map/ppermute | solution.py:22
  64.0 15.3 %collective-permute-start.16 = (bf16[128,1024]{1,0:T(8,128)(2,1)S(1)}, bf16[128,1024]{1,0:T(8,128)(2,1)S(1)}, u32[]{:S(2)}, u32[]{:S(2)}) collective-permute-start(bf16[128,1024]{1,0:T(8,128)(2,1)S(1)} %get-tuple-element.424.refs_8_.cot_ref), channel_id=1, source_target_pairs={{0,8},{8,0},{1,9},{9,1},{2,10},{10,2},{3,11},{11,3},{4,12},{12,4},... | collective-permute-start | bytes 786440 | tf_op jit(solution)/shard_map/ppermute | solution.py:22
  65.7 26.1 %collective-permute-start.19 = (bf16[1,8,32,1152]{3,2,1,0:T(8,128)(2,1)}, bf16[1,8,32,1152]{3,2,1,0:T(8,128)(2,1)}, u32[]{:S(2)}, u32[]{:S(2)}) collective-permute-start(bf16[1,8,32,1152]{3,2,1,0:T(8,128)(2,1)} %bitcast.18.a_ref), channel_id=1, source_target_pairs={{0,1},{1,0},{2,3},{3,2},{4,5},{5,4},{6,7},{7,6},{8,9},{9,8},{10,11... | collective-permute-start | bytes 1769480 | tf_op jit(solution)/shard_map/ppermute | solution.py:22
  66.1 31.4 %collective-permute-start.18 = (bf16[1,8,32,1152]{3,2,1,0:T(8,128)(2,1)}, bf16[1,8,32,1152]{3,2,1,0:T(8,128)(2,1)}, u32[]{:S(2)}, u32[]{:S(2)}) collective-permute-start(bf16[1,8,32,1152]{3,2,1,0:T(8,128)(2,1)} %bitcast.18.a_ref), channel_id=1, source_target_pairs={{0,16},{16,0},{1,17},{17,1},{2,18},{18,2},{3,19},{19,3},{4,20},{20... | collective-permute-start | bytes 1769480 | tf_op jit(solution)/shard_map/ppermute | solution.py:22
  80.0 6.2 %collective-permute-start.20 = (bf16[4,2,32,1024]{3,2,1,0:T(8,128)(2,1)S(1)}, bf16[4,2,32,1024]{3,2,1,0:T(8,128)(2,1)S(1)}, u32[]{:S(2)}, u32[]{:S(2)}) collective-permute-start(bf16[4,2,32,1024]{3,2,1,0:T(8,128)(2,1)S(1)} %bitcast.85), channel_id=1, source_target_pairs={{0,2},{2,0},{1,3},{3,1},{4,6},{6,4},{5,7},{7,5},{8,10},{10,8},{9,1... | collective-permute-start | bytes 1572872 | tf_op jit(solution)/shard_map/ppermute | solution.py:22
  80.0 18.8 %all-to-all-start.2 = ((bf16[8,128,128]{2,1,0:T(8,128)(2,1)}), bf16[8,128,128]{2,1,0:T(8,128)(2,1)S(1)}, u32[]{:S(2)}, u32[]{:S(2)}) async-start(bf16[8,128,128]{2,1,0:T(8,128)(2,1)} %copy-done.31), calls=%async_computation.2 | async-start | bytes 524288 | tf_op jit(solution)/shard_map/all_to_all | solution.py:947
  83.6 13.9 %collective-permute-start.22 = (bf16[128,1024]{1,0:T(8,128)(2,1)}, bf16[128,1024]{1,0:T(8,128)(2,1)}, u32[]{:S(2)}, u32[]{:S(2)}) collective-permute-start(bf16[128,1024]{1,0:T(8,128)(2,1)} %copy-done.40), channel_id=1, source_target_pairs={{0,4},{4,0},{1,5},{5,1},{2,6},{6,2},{3,7},{7,3},{8,12},{12,8},{9,1... | collective-permute-start | bytes 786440 | tf_op jit(solution)/shard_map/ppermute | solution.py:22
  98.8 13.7 %collective-permute-start.26 = (bf16[1,8,32,1152]{3,2,1,0:T(8,128)(2,1)}, bf16[1,8,32,1152]{3,2,1,0:T(8,128)(2,1)S(1)}, u32[]{:S(2)}, u32[]{:S(2)}) collective-permute-start(bf16[1,8,32,1152]{3,2,1,0:T(8,128)(2,1)} %collective-permute-done.18.c_ref), channel_id=1, source_target_pairs={{0,1},{1,0},{2,3},{3,2},{4,5},{5,4},{6,7},{7,6},{8,9},{9,8},{10,11... | collective-permute-start | bytes 1769480 | tf_op jit(solution)/shard_map/ppermute | solution.py:22
  102.1 11.9 %collective-permute-start.25 = (bf16[128,1024]{1,0:T(8,128)(2,1)S(1)}, bf16[128,1024]{1,0:T(8,128)(2,1)S(1)}, u32[]{:S(2)}, u32[]{:S(2)}) collective-permute-start(bf16[128,1024]{1,0:T(8,128)(2,1)S(1)} %get-tuple-element.382.refs_0_), channel_id=1, source_target_pairs={{0,12},{4,8},{8,4},{12,0},{1,13},{5,9},{9,5},{13,1},{2,14},{6,10},... | collective-permute-start | bytes 786440 | tf_op jit(solution)/shard_map/ppermute | solution.py:26
  103.1 11.6 %collective-permute-start.24 = (bf16[128,1024]{1,0:T(8,128)(2,1)S(1)}, bf16[128,1024]{1,0:T(8,128)(2,1)S(1)}, u32[]{:S(2)}, u32[]{:S(2)}) collective-permute-start(bf16[128,1024]{1,0:T(8,128)(2,1)S(1)} %get-tuple-element.382.refs_0_), channel_id=1, source_target_pairs={{0,8},{8,0},{1,9},{9,1},{2,10},{10,2},{3,11},{11,3},{4,12},{12,4},... | collective-permute-start | bytes 786440 | tf_op jit(solution)/shard_map/ppermute | solution.py:22
  105.3 9.5 %collective-permute-start.23 = (bf16[128,1024]{1,0:T(8,128)(2,1)S(1)}, bf16[128,1024]{1,0:T(8,128)(2,1)S(1)}, u32[]{:S(2)}, u32[]{:S(2)}) collective-permute-start(bf16[128,1024]{1,0:T(8,128)(2,1)S(1)} %get-tuple-element.382.refs_0_), channel_id=1, source_target_pairs={{0,4},{4,0},{1,5},{5,1},{2,6},{6,2},{3,7},{7,3},{8,12},{12,8},{9,1... | collective-permute-start | bytes 786440 | tf_op jit(solution)/shard_map/ppermute | solution.py:22
  128.8 10.6 %collective-permute-start.36 = (bf16[128,1024]{1,0:T(8,128)(2,1)S(1)}, bf16[128,1024]{1,0:T(8,128)(2,1)S(1)}, u32[]{:S(2)}, u32[]{:S(2)}) collective-permute-start(bf16[128,1024]{1,0:T(8,128)(2,1)S(1)} %get-tuple-element.414), channel_id=1, source_target_pairs={{0,4},{4,0},{1,5},{5,1},{2,6},{6,2},{3,7},{7,3},{8,12},{12,8},{9,1... | collective-permute-start | bytes 786440 | tf_op jit(solution)/shard_map/ppermute | solution.py:22
  130.2 9.2 %collective-permute-start.37 = (bf16[128,1024]{1,0:T(8,128)(2,1)S(1)}, bf16[128,1024]{1,0:T(8,128)(2,1)S(1)}, u32[]{:S(2)}, u32[]{:S(2)}) collective-permute-start(bf16[128,1024]{1,0:T(8,128)(2,1)S(1)} %get-tuple-element.415), channel_id=1, source_target_pairs={{0,8},{8,0},{1,9},{9,1},{2,10},{10,2},{3,11},{11,3},{4,12},{12,4},... | collective-permute-start | bytes 786440 | tf_op jit(solution)/shard_map/ppermute | solution.py:22
  130.2 13.7 %collective-permute-start.38 = (bf16[128,1024]{1,0:T(8,128)(2,1)S(1)}, bf16[128,1024]{1,0:T(8,128)(2,1)S(1)}, u32[]{:S(2)}, u32[]{:S(2)}) collective-permute-start(bf16[128,1024]{1,0:T(8,128)(2,1)S(1)} %get-tuple-element.416), channel_id=1, source_target_pairs={{0,12},{4,8},{8,4},{12,0},{1,13},{5,9},{9,5},{13,1},{2,14},{6,10},... | collective-permute-start | bytes 786440 | tf_op jit(solution)/shard_map/ppermute | solution.py:26
  138.4 27.5 %collective-permute-start.39 = (bf16[16,32,1152]{2,1,0:T(8,128)(2,1)}, bf16[16,32,1152]{2,1,0:T(8,128)(2,1)}, u32[]{:S(2)}, u32[]{:S(2)}) collective-permute-start(bf16[16,32,1152]{2,1,0:T(8,128)(2,1)} %get-tuple-element.445), channel_id=1, source_target_pairs={{0,1},{1,0},{2,3},{3,2},{4,5},{5,4},{6,7},{7,6},{8,9},{9,8},{10,11... | collective-permute-start | bytes 3538952 | tf_op jit(solution)/shard_map/ppermute | solution.py:22
  146.6 6.9 %collective-permute-start.41 = (bf16[512,1024]{1,0:T(8,128)(2,1)}, bf16[512,1024]{1,0:T(8,128)(2,1)}, u32[]{:S(2)}, u32[]{:S(2)}) collective-permute-start(bf16[512,1024]{1,0:T(8,128)(2,1)} %get-tuple-element.462), channel_id=1, source_target_pairs={{0,2},{2,0},{1,3},{3,1},{4,6},{6,4},{5,7},{7,5},{8,10},{10,8},{9,1... | collective-permute-start | bytes 3145736 | tf_op jit(solution)/shard_map/ppermute | solution.py:22
  149.0 10.8 %collective-permute-start.40 = (bf16[8,64,1024]{2,1,0:T(8,128)(2,1)}, bf16[8,64,1024]{2,1,0:T(8,128)(2,1)}, u32[]{:S(2)}, u32[]{:S(2)}) collective-permute-start(bf16[8,64,1024]{2,1,0:T(8,128)(2,1)} %get-tuple-element.451), channel_id=1, source_target_pairs={{0,2},{2,0},{1,3},{3,1},{4,6},{6,4},{5,7},{7,5},{8,10},{10,8},{9,1... | collective-permute-start | bytes 3145736 | tf_op jit(solution)/shard_map/ppermute | solution.py:22
  149.5 13.5 %all-to-all-start.3 = ((bf16[8,128,128]{2,1,0:T(8,128)(2,1)}), bf16[8,128,128]{2,1,0:T(8,128)(2,1)S(1)}, u32[]{:S(2)}, u32[]{:S(2)}) async-start(bf16[8,128,128]{2,1,0:T(8,128)(2,1)} %copy-done.30), calls=%async_computation.3 | async-start | bytes 524288 | tf_op jit(solution)/shard_map/all_to_all | solution.py:1001
  156.4 21.7 %collective-permute-start.42 = (bf16[128,1024]{1,0:T(8,128)(2,1)}, bf16[128,1024]{1,0:T(8,128)(2,1)S(1)}, u32[]{:S(2)}, u32[]{:S(2)}) collective-permute-start(bf16[128,1024]{1,0:T(8,128)(2,1)} %get-tuple-element.464), channel_id=1, source_target_pairs={{0,4},{4,0},{1,5},{5,1},{2,6},{6,2},{3,7},{7,3},{8,12},{12,8},{9,1... | collective-permute-start | bytes 786440 | tf_op jit(solution)/shard_map/ppermute | solution.py:22
  158.4 19.7 %collective-permute-start.43 = (bf16[128,1024]{1,0:T(8,128)(2,1)}, bf16[128,1024]{1,0:T(8,128)(2,1)}, u32[]{:S(2)}, u32[]{:S(2)}) collective-permute-start(bf16[128,1024]{1,0:T(8,128)(2,1)} %get-tuple-element.465), channel_id=1, source_target_pairs={{0,8},{8,0},{1,9},{9,1},{2,10},{10,2},{3,11},{11,3},{4,12},{12,4},... | collective-permute-start | bytes 786440 | tf_op jit(solution)/shard_map/ppermute | solution.py:22
  159.9 18.2 %collective-permute-start.44 = (bf16[128,1024]{1,0:T(8,128)(2,1)}, bf16[128,1024]{1,0:T(8,128)(2,1)}, u32[]{:S(2)}, u32[]{:S(2)}) collective-permute-start(bf16[128,1024]{1,0:T(8,128)(2,1)} %get-tuple-element.466), channel_id=1, source_target_pairs={{0,12},{4,8},{8,4},{12,0},{1,13},{5,9},{9,5},{13,1},{2,14},{6,10},... | collective-permute-start | bytes 786440 | tf_op jit(solution)/shard_map/ppermute | solution.py:26
  165.9 15.6 %collective-permute-start.46 = (bf16[8,32,1024]{2,1,0:T(8,128)(2,1)}, bf16[8,32,1024]{2,1,0:T(8,128)(2,1)S(1)}, u32[]{:S(2)}, u32[]{:S(2)}) collective-permute-start(bf16[8,32,1024]{2,1,0:T(8,128)(2,1)} %copy-done.37), channel_id=1, source_target_pairs={{0,1},{1,0},{2,3},{3,2},{4,5},{5,4},{6,7},{7,6},{8,9},{9,8},{10,11... | collective-permute-start | bytes 1572872 | tf_op jit(solution)/shard_map/ppermute | solution.py:22
  178.1 12.0 %collective-permute-start.45 = (bf16[256,1024]{1,0:T(8,128)(2,1)S(1)}, bf16[256,1024]{1,0:T(8,128)(2,1)S(1)}, u32[]{:S(2)}, u32[]{:S(2)}) collective-permute-start(bf16[256,1024]{1,0:T(8,128)(2,1)S(1)} %get-tuple-element.484), channel_id=1, source_target_pairs={{0,4},{4,0},{1,5},{5,1},{2,6},{6,2},{3,7},{7,3},{8,12},{12,8},{9,1... | collective-permute-start | bytes 1572872 | tf_op jit(solution)/shard_map/ppermute | solution.py:22
  182.2 12.0 %collective-permute-start.47 = (bf16[2,64,1024]{2,1,0:T(8,128)(2,1)S(1)}, bf16[2,64,1024]{2,1,0:T(8,128)(2,1)S(1)}, u32[]{:S(2)}, u32[]{:S(2)}) collective-permute-start(bf16[2,64,1024]{2,1,0:T(8,128)(2,1)S(1)} %get-tuple-element.490), channel_id=1, source_target_pairs={{0,8},{8,0},{1,9},{9,1},{2,10},{10,2},{3,11},{11,3},{4,12},{12,4},... | collective-permute-start | bytes 786440 | tf_op jit(solution)/shard_map/ppermute | solution.py:22
  184.1 29.1 %collective-permute-start.49 = (bf16[1,256,1152]{2,1,0:T(8,128)(2,1)S(1)}, bf16[1,256,1152]{2,1,0:T(8,128)(2,1)S(1)}, u32[]{:S(2)}, u32[]{:S(2)}) collective-permute-start(bf16[1,256,1152]{2,1,0:T(8,128)(2,1)S(1)} %get-tuple-element.507), channel_id=1, source_target_pairs={{0,16},{16,0},{1,17},{17,1},{2,18},{18,2},{3,19},{19,3},{4,20},{20... | collective-permute-start | bytes 1769480 | tf_op jit(solution)/shard_map/ppermute | solution.py:22
  194.2 14.8 %collective-permute-start.50 = (bf16[256,1024]{1,0:T(8,128)(2,1)S(1)}, bf16[256,1024]{1,0:T(8,128)(2,1)S(1)}, u32[]{:S(2)}, u32[]{:S(2)}) collective-permute-start(bf16[256,1024]{1,0:T(8,128)(2,1)S(1)} %get-tuple-element.509), channel_id=1, source_target_pairs={{0,4},{4,0},{1,5},{5,1},{2,6},{6,2},{3,7},{7,3},{8,12},{12,8},{9,1... | collective-permute-start | bytes 1572872 | tf_op jit(solution)/shard_map/ppermute | solution.py:22
  194.8 12.2 %collective-permute-start.51 = (bf16[128,1024]{1,0:T(8,128)(2,1)S(1)}, bf16[128,1024]{1,0:T(8,128)(2,1)S(1)}, u32[]{:S(2)}, u32[]{:S(2)}) collective-permute-start(bf16[128,1024]{1,0:T(8,128)(2,1)S(1)} %get-tuple-element.511), channel_id=1, source_target_pairs={{0,8},{8,0},{1,9},{9,1},{2,10},{10,2},{3,11},{11,3},{4,12},{12,4},... | collective-permute-start | bytes 786440 | tf_op jit(solution)/shard_map/ppermute | solution.py:22
  194.8 6.2 %collective-permute-start.53 = (bf16[8,32,384]{2,1,0:T(8,128)(2,1)S(1)}, bf16[8,32,384]{2,1,0:T(8,128)(2,1)S(1)}, u32[]{:S(2)}, u32[]{:S(2)}) collective-permute-start(bf16[8,32,384]{2,1,0:T(8,128)(2,1)S(1)} %get-tuple-element.520), channel_id=1, source_target_pairs={{0,1},{1,0},{2,3},{3,2},{4,5},{5,4},{6,7},{7,6},{8,9},{9,8},{10,11... | collective-permute-start | bytes 589832 | tf_op jit(solution)/shard_map/ppermute | solution.py:22
  196.4 16.8 %collective-permute-start.52 = (bf16[2,32,1024]{2,1,0:T(8,128)(2,1)S(1)}, bf16[2,32,1024]{2,1,0:T(8,128)(2,1)S(1)}, u32[]{:S(2)}, u32[]{:S(2)}) collective-permute-start(bf16[2,32,1024]{2,1,0:T(8,128)(2,1)S(1)} %get-tuple-element.518), channel_id=1, source_target_pairs={{0,4},{4,0},{1,5},{5,1},{2,6},{6,2},{3,7},{7,3},{8,12},{12,8},{9,1... | collective-permute-start | bytes 393224 | tf_op jit(solution)/shard_map/ppermute | solution.py:22
  214.7 26.3 %all-to-all-start.4 = ((bf16[8,32,1152]{2,1,0:T(8,128)(2,1)}), bf16[8,32,1152]{2,1,0:T(8,128)(2,1)}, u32[]{:S(2)}, u32[]{:S(2)}) async-start(bf16[8,32,1152]{2,1,0:T(8,128)(2,1)} %total_kernel.3), calls=%async_computation.4 | async-start | bytes 1179648 | tf_op jit(solution)/shard_map/all_to_all | solution.py:824
  218.9 20.0 %collective-permute-start.54 = (bf16[128,1024]{1,0:T(8,128)(2,1)}, bf16[128,1024]{1,0:T(8,128)(2,1)S(1)}, u32[]{:S(2)}, u32[]{:S(2)}) collective-permute-start(bf16[128,1024]{1,0:T(8,128)(2,1)} %get-tuple-element.526), channel_id=1, source_target_pairs={{0,16},{16,0},{1,17},{17,1},{2,18},{18,2},{3,19},{19,3},{4,20},{20... | collective-permute-start | bytes 786440 | tf_op jit(solution)/shard_map/ppermute | solution.py:22
  219.0 22.0 %collective-permute-start.55 = (bf16[128,1024]{1,0:T(8,128)(2,1)S(1)}, bf16[128,1024]{1,0:T(8,128)(2,1)S(1)}, u32[]{:S(2)}, u32[]{:S(2)}) collective-permute-start(bf16[128,1024]{1,0:T(8,128)(2,1)S(1)} %get-tuple-element.527), channel_id=1, source_target_pairs={{0,8},{8,0},{1,9},{9,1},{2,10},{10,2},{3,11},{11,3},{4,12},{12,4},... | collective-permute-start | bytes 786440 | tf_op jit(solution)/shard_map/ppermute | solution.py:22
  223.3 15.7 %collective-permute-start.57 = (bf16[1,32,1024]{2,1,0:T(8,128)(2,1)S(1)}, bf16[1,32,1024]{2,1,0:T(8,128)(2,1)S(1)}, u32[]{:S(2)}, u32[]{:S(2)}) collective-permute-start(bf16[1,32,1024]{2,1,0:T(8,128)(2,1)S(1)} %get-tuple-element.539), channel_id=1, source_target_pairs={{0,16},{16,0},{1,17},{17,1},{2,18},{18,2},{3,19},{19,3},{4,20},{20... | collective-permute-start | bytes 196616 | tf_op jit(solution)/shard_map/ppermute | solution.py:22
  241.0 11.6 %all-to-all-start.5 = ((bf16[8,32,384]{2,1,0:T(8,128)(2,1)}), bf16[8,32,384]{2,1,0:T(8,128)(2,1)S(1)}, u32[]{:S(2)}, u32[]{:S(2)}) async-start(bf16[8,32,384]{2,1,0:T(8,128)(2,1)} %total_kernel.2), calls=%async_computation.5 | async-start | bytes 393216 | tf_op jit(solution)/shard_map/all_to_all | solution.py:896
  (64 other events, 434.8 us)
